TPU v7x, 512 devices: a whole 4x4x16 slice. The times are simulated.
512 devices in a mesh: segment: 16 (over z_lo, core), db: 16 (over x, y), mp: 2 (over z_hi).
Axes of the slice: x: 4, y: 4, z: 16 (z_hi: 2, z_lo: 8; z = z_hi * 8 + z_lo), core: 2. Of those that a mesh axis runs over, the one named last changes fastest.
Arguments:
- stream: bfloat16 [16, 6144, 4096], P('segment', 'db', 'mp'), may hold values from -6 to 6
- gain: float32 [16, 4096], P('segment', 'mp'), may hold values from 0.25 to 150
- key_weight: bfloat16 [16, 448, 4096], P('segment', 'db', 'mp'), may hold values from -0.25 to 0.25
- value_weight: bfloat16 [16, 448, 4096], P('segment', 'db', 'mp'), may hold values from -0.25 to 0.25
- owners: int32 [16, 96, 2], P('segment', 'db'), may hold values from 0 to 15, all different within a row; in each aligned block of 6 rows (0 to 5, 6 to 11, ..., all dimensions but the last counted through in order) at most 2 rows name the same one
- blocks: int32 [16, 96, 2], P('segment', 'db'), may hold values from 0 to 5
- valid: int32 [16, 96, 2], P('segment', 'db'), may hold values from 0 to 1, as said below
- database: bfloat16 [96, 128, 448], P('db'), may hold values from -6 to 6
Outputs:
- updated: bfloat16 [16, 6144, 4096], P('segment', 'db', 'mp')
Inputs may be any that keep to these rules, and one draw needn't show every extreme that they name: In the 6 groups that one index of db holds of one micro-batch, no owner is named by more than 2 neighbours; the 2 neighbours of a group have different owners. `valid`: 0 or 1; both neighbours of the first group of each 2048-token sequence are 0.
All inputs are finite; a program needn't handle non-finite values.
Results may differ from a plain program's by a relative error of at most 0.0045.
The roundings to bfloat16 on the way count: a program that leaves them out, or rounds other values in their place, can miss the bound.
Values may be sent and summed in bfloat16 or wider, within the bound.
No kernel may reach another device: no remote copies, remote signals or barrier semaphores. Data moves between devices by JAX's collectives and lax.ppermute only.
A program may use at most 128 MiB of HBM per device.

v0:
```python
import jax
import jax.numpy as jnp
from jax import lax
from jax.sharding import PartitionSpec as P

HD = 128
GROUP = 64


eps_norm = 1e-06


def from_behind(value, axis, steps):
    count = lax.axis_size(axis)
    pairs = [(source, (source + steps) % count) for source in range(count)]
    return lax.ppermute(value, axis, pairs)


def on_device(stream, gain, key_weight, value_weight, owners, blocks, valid, database):
    stream_rows = stream[0]
    tokens_here = stream_rows.shape[0]
    local_width = stream_rows.shape[1]
    as_float = stream_rows.astype(jnp.float32)
    square_total = lax.psum(jnp.sum(as_float * as_float, axis=1), "mp")
    full_width = local_width * lax.axis_size("mp")
    inv_rms = lax.rsqrt(square_total / full_width + eps_norm)
    queries = (as_float * inv_rms[:, None] * gain[0][None, :] * HD ** (-0.5)).astype(jnp.bfloat16)
    block_rows = database.shape[1]
    enc_width = database.shape[2]
    owner_list = owners[0].reshape(-1)
    block_list = blocks[0].reshape(-1)
    request_count = owner_list.shape[0]
    owners_count = lax.axis_size("db")
    capacity = max(2, -(-request_count // owners_count))
    order = jnp.arange(request_count)
    same_owner = owner_list[:, None] == owner_list[None, :]
    earlier = order[:, None] > order[None, :]
    slot_index = jnp.sum(jnp.logical_and(same_owner, earlier).astype(jnp.int32), axis=1)
    target = owner_list * capacity + slot_index
    slot_match = target[None, :] == jnp.arange(owners_count * capacity)[:, None]
    wanted = jnp.sum(jnp.where(slot_match, block_list[None, :], 0), axis=1)
    wanted = wanted.reshape(owners_count, capacity)
    asked = lax.all_to_all(wanted, "db", split_axis=0, concat_axis=0, tiled=True)
    served_rows = jnp.take(database, asked.reshape(-1), axis=0)
    served_rows = served_rows.reshape(asked.shape[0], asked.shape[1], block_rows, enc_width)
    replies = lax.all_to_all(served_rows, "db", split_axis=0, concat_axis=0, tiled=True)
    reply_rows = replies.reshape(owners_count * capacity, block_rows, enc_width)
    picked = jnp.take(reply_rows, target, axis=0)
    flat_enc = picked.reshape(request_count * block_rows, enc_width)
    key_full, value_full = (
        lax.all_gather(key_weight[0], "db", axis=0, tiled=True),
        lax.all_gather(value_weight[0], "db", axis=0, tiled=True),
    )
    key_sum = jnp.dot(flat_enc, key_full, preferred_element_type=jnp.float32)
    value_sum = jnp.dot(flat_enc, value_full, preferred_element_type=jnp.float32)
    key_block = key_sum.astype(jnp.bfloat16)
    value_block = value_sum.astype(jnp.bfloat16)
    groups = tokens_here // GROUP
    head_count = local_width // HD
    span = request_count // groups * block_rows
    query_heads = queries.reshape(groups, GROUP, head_count, HD)
    key_heads = key_block.reshape(groups, span, head_count, HD)
    value_heads = value_block.reshape(groups, span, head_count, HD)
    scores = jnp.einsum(
        "cthd,cshd->chts", query_heads, key_heads, preferred_element_type=jnp.float32
    )
    is_live = jnp.repeat(valid[0] > 0, block_rows, axis=1)
    live_mask = is_live[:, None, None, :]
    row_max = jnp.max(jnp.where(live_mask, scores, -1e30), axis=3, keepdims=True)
    any_live = jnp.any(is_live, axis=1)[:, None, None, None]
    row_max = jnp.where(any_live, row_max, 0.0)
    expo = jnp.exp(jnp.where(live_mask, scores - row_max, -1e30))
    row_total = jnp.maximum(jnp.sum(expo, axis=3, keepdims=True), 1.0)
    weights_bf = (expo / row_total).astype(jnp.bfloat16)
    attended = jnp.einsum(
        "chts,cshd->cthd", weights_bf, value_heads, preferred_element_type=jnp.float32
    )
    updated = (as_float + attended.reshape(tokens_here, local_width)).astype(jnp.bfloat16)
    return from_behind(updated[None], "segment", 1)


def solution(mesh):
    return jax.shard_map(
        on_device,
        mesh=mesh,
        in_specs=(
            P("segment", "db", "mp"),
            P("segment", "mp"),
            P("segment", "db", "mp"),
            P("segment", "db", "mp"),
            P("segment", "db", None),
            P("segment", "db", None),
            P("segment", "db", None),
            P("db", None, None),
        ),
        out_specs=P("segment", "db", "mp"),
        check_vma=False,
    )
```

profile of v0, /device:TPU:4, one launch (start us, length us, event | category | flops | bytes accessed | tf_op | source)
XLA Modules:
  0.0 239.1 jit_solution(4948836025001533390)
XLA Ops:
  10.5 13.7 %all_to_all.14 = s32[16,1,2]{2,1,0:T(1,128)S(1)} all-to-all(s32[16,1,2]{2,1,0:T(1,128)S(1)} %bitcast.51), channel_id=1, replica_groups=mesh['segment'=16,'db'=16,'mp'=2] {'db'}, dimensions={0} | all-to-all | bytes 256 | tf_op jit(solution)/shard_map/all_to_all | solution.py:43
  25.6 2.9 %gather_fusion = bf16[32,128,448]{1,2,0:T(8,128)(2,1)} fusion(bf16[6,128,448]{1,2,0:T(8,128)(2,1)S(1)} %copy-done, s32[1024]{0:T(1024)S(1)} %pad_clamp_fusion.1), kind=kCustom, calls=%fused_computation | custom fusion | bytes 7340160 | tf_op jit(solution)/shard_map/jit(_take)/gather | solution.py:44
  28.5 4.4 %broadcast_select_fusion = bf16[16,2,128,448]{2,3,1,0:T(8,128)(2,1)} fusion(bf16[16,2,128,448]{2,3,1,0:T(8,128)(2,1)} %bitcast.48, pred[16,2]{1,0:T(8,128)(4,1)S(1)} %copy.67), kind=kLoop, calls=%fused_computation.15 | loop fusion | flops 1835008 | bytes 7340064 | tf_op jit(solution)/shard_map/jit(_take)/select_n | solution.py:44
  32.8 6.7 %all-to-all-start.1 = ((bf16[16,2,128,448]{2,3,1,0:T(8,128)(2,1)}), bf16[16,2,128,448]{2,3,1,0:T(8,128)(2,1)}, u32[]{:S(2)}, u32[]{:S(2)}) async-start(bf16[16,2,128,448]{2,3,1,0:T(8,128)(2,1)} %broadcast_select_fusion), calls=%async_computation.1 | async-start | bytes 7340032 | tf_op jit(solution)/shard_map/all_to_all | solution.py:46
  41.1 15.9 %psum.7 = f32[384]{0:T(512)S(1)} all-reduce(f32[384]{0:T(512)S(1)} %fusion.5), channel_id=1, replica_groups=mesh['segment'=16,'db'=16,'mp'=2] {'mp'}, use_global_device_ids=true, to_apply=%region_3.4 | all-reduce | flops 384 | bytes 3072 | tf_op jit(solution)/shard_map/psum | solution.py:24
  57.5 2.3 copy.78
  60.1 25.6 %all-to-all-done.1 = bf16[16,2,128,448]{2,3,1,0:T(8,128)(2,1)} async-done(((bf16[16,2,128,448]{2,3,1,0:T(8,128)(2,1)}), bf16[16,2,128,448]{2,3,1,0:T(8,128)(2,1)}, u32[]{:S(2)}, u32[]{:S(2)}) %all-to-all-start.1) | async-done | bytes 3670048 | tf_op jit(solution)/shard_map/all_to_all | solution.py:46
  85.7 3.9 %gather_fusion.1 = bf16[12,128,448]{1,2,0:T(8,128)(2,1)} fusion(bf16[32,128,448]{1,2,0:T(8,128)(2,1)} %bitcast.5, s32[1024]{0:T(1024)S(1)} %pad_clamp_fusion), kind=kCustom, calls=%fused_computation.1 | custom fusion | bytes 2752560 | tf_op jit(solution)/shard_map/jit(_take)/gather | solution.py:48
  89.7 2.5 %copy.69 = bf16[12,128,448]{2,1,0:T(8,128)(2,1)} copy(bf16[12,128,448]{1,2,0:T(8,128)(2,1)} %gather_fusion.1) | data formatting | bytes 2752512 | tf_op jit(solution)/shard_map/jit(_take)/gather | solution.py:48
  92.2 2.8 %bitcast_select_fusion = bf16[1536,448]{1,0:T(8,128)(2,1)} fusion(bf16[12,128,448]{2,1,0:T(8,128)(2,1)} %copy.69, pred[1536]{0:T(1024)(128)(4,1)S(1)} %broadcast_bitcast_fusion.1), kind=kLoop, calls=%fused_computation.33 | loop fusion | flops 688128 | bytes 2754048 | tf_op jit(solution)/shard_map/jit(_take)/select_n | solution.py:48
  95.0 8.7 %all-gather.7.cloned.1.call-done = bf16[1,448,2048]{2,0,1:T(2,128)(2,1)} async-done(((bf16[1,28,2048]{2,0,1:T(2,128)(2,1)}), bf16[1,448,2048]{2,0,1:T(2,128)(2,1)}) %all-gather.7.cloned.1.call-update) | async-done | bytes 1835024 | tf_op jit(solution)/shard_map/all_gather | solution.py:51
  103.7 6.1 %fusion.15 = bf16[192,8,16,128]{3,1,2,0:T(8,128)(2,1)S(1)} fusion(bf16[1536,448]{1,0:T(8,128)(2,1)} %bitcast_select_fusion, bf16[1,448,2048]{2,0,1:T(2,128)(2,1)} %all-gather.7.cloned.1.call-done), kind=kOutput, calls=%fused_computation.27 | convolution fusion | flops 2821718016 | bytes 9502720 | tf_op jit(solution)/shard_map/dot_general | solution.py:54
  109.9 2.4 copy.79
  112.3 3.2 %select_reduce_fusion = (f32[6,16,64]{2,1,0:T(8,128)S(1)}, f32[6,16,64,256]{3,2,1,0:T(8,128)S(1)}) fusion(pred[6,256]{1,0:T(8,128)(4,1)S(1)} %get-tuple-element.8, bf16[6,256,16,128]{3,2,1,0:T(8,128)(2,1)S(1)} %bitcast.47, f32[6,64,16,128]{3,2,1,0:T(8,128)S(1)} %bitcast.49, f32[16,128]{1,0:T(8,128)S(1)} %bitcast.52, f32[6,64]{1,0:T(8,128)S(1)} %mul.58), kind=kOutput, calls=%fused_computation.10 | convolution fusion | flops 408938496 | bytes 15764480 | tf_op jit(solution)/shard_map/cthd,cshd->chts/dot_general | solution.py:64
  115.5 2.2 fusion.4
  118.1 56.7 %all-gather.5.cloned.1.call-done = bf16[1,448,2048]{2,0,1:T(2,128)(2,1)} async-done(((bf16[1,28,2048]{2,0,1:T(2,128)(2,1)}), bf16[1,448,2048]{2,0,1:T(2,128)(2,1)}) %all-gather.5.cloned.1.call-update) | async-done | bytes 1835024 | tf_op jit(solution)/shard_map/all_gather | solution.py:52
  174.8 8.8 %fusion.14 = bf16[192,8,16,128]{3,1,2,0:T(8,128)(2,1)} fusion(bf16[1536,448]{1,0:T(8,128)(2,1)} %bitcast_select_fusion, bf16[1,448,2048]{2,0,1:T(2,128)(2,1)} %all-gather.5.cloned.1.call-done), kind=kOutput, calls=%fused_computation.26 | convolution fusion | flops 2821718016 | bytes 9502720 | tf_op jit(solution)/shard_map/dot_general | solution.py:55
  183.6 5.3 %copy.80 = bf16[192,8,16,128]{3,2,1,0:T(8,128)(2,1)S(1)} copy(bf16[192,8,16,128]{3,1,2,0:T(8,128)(2,1)} %fusion.14) | data formatting | bytes 12582912
  188.9 3.3 %fusion.16 = f32[6,64,16,128]{3,1,2,0:T(8,128)S(1)} fusion(bf16[6,256,16,128]{3,2,1,0:T(8,128)(2,1)S(1)} %bitcast.50, f32[6,16,64,256]{3,2,1,0:T(8,128)S(1)} %copy-done.3, f32[6,16,64]{2,1,0:T(8,128)S(1)} %broadcast_maximum_fusion, f32[6,16,64]{2,1,0:T(8,128)S(1)} %broadcast_select_fusion.1, pred[6,256]{1,0:T(8,128)(4,1)S(1)} %get-tuple-element.8), kind=kOutput, calls=%fused_computation.28 | convolution fusion | flops 408944640 | bytes 15779328 | tf_op jit(solution)/shard_map/chts,cshd->cthd/dot_general | solution.py:75
  192.2 3.5 %copy.75 = f32[6,64,16,128]{3,2,1,0:T(8,128)} copy(f32[6,64,16,128]{3,1,2,0:T(8,128)S(1)} %fusion.16) | data formatting | bytes 6291456 | tf_op jit(solution)/shard_map/chts,cshd->cthd/transpose | solution.py:75
  195.7 4.6 %reshape.148 = f32[1,384,2048]{2,1,0:T(8,128)} reshape(f32[6,64,16,128]{3,2,1,0:T(8,128)} %copy.75) | data formatting | bytes 6291456 | tf_op jit(solution)/shard_map/reshape | solution.py:78
  200.2 2.5 %fusion.6 = bf16[1,384,2048]{2,1,0:T(8,128)(2,1)S(1)} fusion(f32[1,384,2048]{2,1,0:T(8,128)} %reshape.148, bf16[1,384,2048]{2,1,0:T(8,128)(2,1)S(1)} %copy-done.4), kind=kLoop, calls=%fused_computation.17 | loop fusion | flops 2359296 | bytes 6291456 | tf_op jit(solution)/shard_map/convert_element_type | solution.py:78
  202.8 1.9 collective-permute-start
  204.7 26.4 %collective-permute-done = bf16[1,384,2048]{2,1,0:T(8,128)(2,1)S(1)} collective-permute-done((bf16[1,384,2048]{2,1,0:T(8,128)(2,1)S(1)}, bf16[1,384,2048]{2,1,0:T(8,128)(2,1)S(1)}, u32[]{:S(2)}, u32[]{:S(2)}) %collective-permute-start) | collective-permute-done | bytes 1572896 | tf_op jit(solution)/shard_map/ppermute | solution.py:16
  (57 shorter events, 9.2 us)
Async XLA Ops:
  6.5 19.1 %copy-start = (bf16[6,128,448]{1,2,0:T(8,128)(2,1)S(1)}, bf16[6,128,448]{1,2,0:T(8,128)(2,1)}, u32[]{:S(2)}) copy-start(bf16[6,128,448]{1,2,0:T(8,128)(2,1)} %param.15) | copy-start | bytes 2064388
  6.5 97.2 %all-gather.7.cloned.1.call-start = ((), (), s32[]{:S(2)}) async-start(), calls=%async_computation.3 | async-start | bytes 3899392 | tf_op jit(solution)/shard_map/all_gather | solution.py:51
  32.8 6.8 %copy-start.6 = (bf16[1,28,2048]{2,1,0:T(8,128)(2,1)S(1)}, bf16[1,28,2048]{2,1,0:T(8,128)(2,1)}, u32[]{:S(2)}) copy-start(bf16[1,28,2048]{2,1,0:T(8,128)(2,1)} %param.11) | copy-start | bytes 344068
  32.8 7.7 %copy-start.8 = (s32[1,6,2]{1,2,0:T(2,128)S(1)}, s32[1,6,2]{1,2,0:T(2,128)}, u32[]{:S(2)}) copy-start(s32[1,6,2]{1,2,0:T(2,128)} %param.12) | copy-start | bytes 148
  32.8 7.9 %copy-start.4 = (bf16[1,384,2048]{2,1,0:T(8,128)(2,1)S(1)}, bf16[1,384,2048]{2,1,0:T(8,128)(2,1)}, u32[]{:S(2)}) copy-start(bf16[1,384,2048]{2,1,0:T(8,128)(2,1)} %param.8) | copy-start | bytes 4718596
  32.8 52.9 %all-to-all-start.1 = ((bf16[16,2,128,448]{2,3,1,0:T(8,128)(2,1)}), bf16[16,2,128,448]{2,3,1,0:T(8,128)(2,1)}, u32[]{:S(2)}, u32[]{:S(2)}) async-start(bf16[16,2,128,448]{2,3,1,0:T(8,128)(2,1)} %broadcast_select_fusion), calls=%async_computation.1 | async-start | bytes 7340032 | tf_op jit(solution)/shard_map/all_to_all | solution.py:46
  39.6 135.2 %all-gather.5.cloned.1.call-start = ((), (), s32[]{:S(2)}) async-start(), calls=%async_computation.2 | async-start | bytes 3899392 | tf_op jit(solution)/shard_map/all_gather | solution.py:52
  57.5 2.4 %copy-start.9 = (s32[1,6,2]{1,2,0:T(2,128)S(1)}, s32[1,6,2]{1,2,0:T(2,128)}, u32[]{:S(2)}) copy-start(s32[1,6,2]{1,2,0:T(2,128)} %param.14) | copy-start | bytes 148
  109.8 2.4 %copy-start.5 = (f32[48,8,16,128]{3,2,1,0:T(8,128)S(1)}, f32[48,8,16,128]{3,2,1,0:T(8,128)}, u32[]{:S(2)}) copy-start(f32[48,8,16,128]{3,2,1,0:T(8,128)} %copy.78) | copy-start | bytes 9437188
  109.8 2.4 %copy-start.7 = (f32[1,2048]{1,0:T(1,128)S(1)}, f32[1,2048]{1,0:T(1,128)}, u32[]{:S(2)}) copy-start(f32[1,2048]{1,0:T(1,128)} %param.9) | copy-start | bytes 24580
  115.5 2.7 %copy-start.2 = (f32[6,16,64,256]{3,2,1,0:T(8,128)}, f32[6,16,64,256]{3,2,1,0:T(8,128)S(1)}, u32[]{:S(2)}) copy-start(f32[6,16,64,256]{3,2,1,0:T(8,128)S(1)} %get-tuple-element.10) | copy-start | bytes 18874372
  183.6 5.3 %copy-start.3 = (f32[6,16,64,256]{3,2,1,0:T(8,128)S(1)}, f32[6,16,64,256]{3,2,1,0:T(8,128)}, u32[]{:S(2)}) copy-start(f32[6,16,64,256]{3,2,1,0:T(8,128)} %copy-done.2) | copy-start | bytes 18874372
  200.2 32.0 %copy-start.1 = (bf16[6,128,448]{1,2,0:T(8,128)(2,1)S(1)}, bf16[6,128,448]{1,2,0:T(8,128)(2,1)}, u32[]{:S(2)}) copy-start(bf16[6,128,448]{1,2,0:T(8,128)(2,1)} %param.15) | copy-start | bytes 2064388
  202.8 28.3 %collective-permute-start = (bf16[1,384,2048]{2,1,0:T(8,128)(2,1)S(1)}, bf16[1,384,2048]{2,1,0:T(8,128)(2,1)S(1)}, u32[]{:S(2)}, u32[]{:S(2)}) collective-permute-start(bf16[1,384,2048]{2,1,0:T(8,128)(2,1)S(1)} %fusion.6), channel_id=1, source_target_pairs={{0,32},{32,64},{64,96},{96,128},{128,160},{160,192},{192,224},{224... | collective-permute-start | bytes 4718600 | tf_op jit(solution)/shard_map/ppermute | solution.py:16
Sparse Core Ops, SparseCore 0:
  10.4 93.2 all-gather.6
  106.8 67.9 all-gather.4
where the time goes:
time: 240 us; the launch traced here: 239 us
  waiting for transfers between devices  117 us (49%)
  local copies, waits for them, and re-layouts  34.5 us (14%)
  blocking collectives  29.6 us (12%)
  matrix products  21.4 us (9%)
  other arithmetic  13.9 us (6%)
  between operations  13.6 us (6%)
  starting transfers between devices  8.71 us (4%)
    all_gather x1, waiting for transfers between devices, on_device(): lax.all_gather(value_weight[0], 'db', axis=0, tiled=True)  56.7 us
    ppermute x1, waiting for transfers between devices, from_behind(): return lax.ppermute(value, axis, pairs)  26.4 us
    all_to_all x1, waiting for transfers between devices, on_device(): lax.all_to_all(served_rows, 'db', split_axis=0, concat_axis=0, tiled=True)  25.6 us
    psum x1, blocking collectives, on_device(): square_total = lax.psum(jnp.sum(as_float * as_float, axis=1), 'mp')  15.9 us
    unnamed x28, local copies, waits for them, and re-layouts  15.7 us
    all_to_all x1, blocking collectives, on_device(): lax.all_to_all(wanted, 'db', split_axis=0, concat_axis=0, tiled=True)  13.7 us
    dot_general x1, matrix products, on_device(): jnp.dot(flat_enc, value_full, preferred_element_type=jnp.float32)  8.77 us
    all_gather x1, waiting for transfers between devices, on_device(): lax.all_gather(key_weight[0], 'db', axis=0, tiled=True)  8.69 us
  transfers between devices with their start and end apart: 4, of which 4 were waited for; matrix products, arithmetic and copies ran while one was open for 16% of the time, Pallas kernels for 0%

commit v1 on v0

v1 whole, which is shorter than its diff:
```python
import jax
import jax.numpy as jnp
from jax import lax
from jax.experimental import pallas as pl
from jax.experimental.pallas import tpu as pltpu
from jax.sharding import PartitionSpec as P

HD = 128
GROUP = 64
SIDE = 4
RING = SIDE * SIDE
eps_norm = 1e-06

W_PART = 28
W_PAD = 32
HEADS_HERE = 16
W_ROWS = HEADS_HERE * 2 * W_PAD
ENC = 448
ENC_PAD = RING * W_PAD
HALF = 64
TILES = 2 * ENC // HD
PAIRS = 3
D_ROWS = PAIRS * TILES * HALF
SLAB = ENC_PAD // HD * HALF
REQ = 12
HB = 2


def ring_pairs(segments, turn, along_x_core):
    pairs = []
    for seg in range(segments):
        for place in range(RING):
            x, y = divmod(place, SIDE)
            if seg % 2 == along_x_core:
                to = ((x + turn) % SIDE) * SIDE + y
            else:
                to = x * SIDE + (y + turn) % SIDE
            pairs.append((seg * RING + place, seg * RING + to))
    return pairs


def ring_groups(segments, along_x_core):
    groups = []
    for seg in range(segments):
        for line in range(SIDE):
            if seg % 2 == along_x_core:
                groups.append([seg * RING + x * SIDE + line for x in range(SIDE)])
            else:
                groups.append([seg * RING + line * SIDE + y for y in range(SIDE)])
    return groups


def turned(value, turn, along_x_core):
    pairs = ring_pairs(lax.axis_size("segment"), turn, along_x_core)
    return lax.ppermute(value, ("segment", "db"), pairs)


def to_next(value):
    count = lax.axis_size("segment")
    return lax.ppermute(value, "segment", [(s, (s + 1) % count) for s in range(count)])


def to_next_other_core(value):
    count = lax.axis_size("segment")
    return lax.ppermute(value, "segment", [(s, ((s + 1) % count) ^ 1) for s in range(count)])


def to_next_other_mp(value):
    count = lax.axis_size("segment")
    pairs = [(s * 2 + m, ((s + 1) % count) * 2 + 1 - m) for s in range(count) for m in range(2)]
    return lax.ppermute(value, ("segment", "mp"), pairs)


def other_core(value):
    count = lax.axis_size("segment")
    return lax.ppermute(value, "segment", [(s, s ^ 1) for s in range(count)])


def pick_kernel(table, c_ref, l_ref, r_ref, ol_ref, or_ref, s_own, s_other, own_out, other_out, slabs, sems):
    sources = (c_ref, l_ref, r_ref, ol_ref, or_ref)

    def begin(i, carry):
        which = table[0, i]
        row = pl.multiple_of(table[1, i], 64)
        for number, source in enumerate(sources):
            @pl.when(which == number)
            def _():
                pltpu.make_async_copy(source.at[pl.ds(row, SLAB)], slabs.at[i], sems.at[i]).start()
        return carry

    def finish(i, carry):
        pltpu.make_async_copy(c_ref.at[pl.ds(0, SLAB)], slabs.at[i], sems.at[i]).wait()
        return carry

    lax.fori_loop(0, 2 * REQ, begin, 0)
    for part, (spread, out) in enumerate(((s_own, own_out), (s_other, other_out))):
        lax.fori_loop(part * REQ, (part + 1) * REQ, finish, 0)
        rows = []
        for i in range(REQ):
            slab = slabs[part * REQ + i]
            rows.append(jnp.concatenate([slab[t * HALF:(t + 1) * HALF] for t in range(ENC_PAD // HD)], axis=1))
        stacked = jnp.concatenate(rows, axis=0)
        even = jnp.dot(stacked, spread[0], preferred_element_type=jnp.float32)
        odd = jnp.dot(stacked, spread[1], preferred_element_type=jnp.float32)
        for i in range(REQ):
            here = slice(i * HALF, (i + 1) * HALF)
            is_odd = table[2, part * REQ + i] == 1
            out[here] = jnp.where(is_odd, odd[here], even[here]).astype(jnp.bfloat16)


def pick(table, pieces, s_own, s_other):
    any_space = pl.BlockSpec(memory_space=pl.ANY)
    vmem = pl.BlockSpec(memory_space=pltpu.VMEM)
    shape = jax.ShapeDtypeStruct((REQ * HALF, ENC_PAD), jnp.bfloat16)
    return pl.pallas_call(
        pick_kernel,
        in_specs=[pl.BlockSpec(memory_space=pltpu.SMEM)] + [any_space] * 5 + [vmem] * 2,
        out_specs=[vmem] * 2,
        out_shape=[shape] * 2,
        scratch_shapes=[
            pltpu.VMEM((2 * REQ, SLAB, HD), jnp.bfloat16),
            pltpu.SemaphoreType.DMA((2 * REQ,)),
        ],
        compiler_params=pltpu.CompilerParams(vmem_limit_bytes=40 * 2**20),
        name="pick_encodings",
    )(table, *pieces, s_own, s_other)


def attend_kernel(live, own_ref, other_ref, w_ref, x_ref, inv_ref, gain_ref, out_ref):
    own, other = own_ref[...], other_ref[...]
    inv = inv_ref[...]
    groups = x_ref.shape[0] // GROUP
    column = lax.broadcasted_iota(jnp.int32, (1, HD), 1)
    masks = []
    for c in range(groups):
        first, second = live[2 * c], live[2 * c + 1]
        masks.append(jnp.where(column < HALF, first, second) > 0)
    for b in range(HB):
        base = b * 2 * W_PAD
        head = slice(b * HD, (b + 1) * HD)
        key_w = jnp.concatenate([w_ref[j, base:base + W_PAD] for j in range(RING)], axis=0)
        value_w = jnp.concatenate([w_ref[j, base + W_PAD:base + 2 * W_PAD] for j in range(RING)], axis=0)
        weight = jnp.concatenate([key_w, value_w], axis=1)
        kv_own = jnp.dot(own, weight, preferred_element_type=jnp.float32).astype(jnp.bfloat16)
        kv_other = jnp.dot(other, weight, preferred_element_type=jnp.float32).astype(jnp.bfloat16)
        x = x_ref[:, head].astype(jnp.float32)
        q = (x * inv * gain_ref[:, head] * HD ** (-0.5)).astype(jnp.bfloat16)
        for c in range(groups):
            rows = slice(c * GROUP, (c + 1) * GROUP)
            keys = slice(c * 2 * HALF, (c + 1) * 2 * HALF)
            key = jnp.concatenate([kv_own[keys, :HD], kv_other[keys, :HD]], axis=0)
            value = jnp.concatenate([kv_own[keys, HD:], kv_other[keys, HD:]], axis=0)
            scores = lax.dot_general(q[rows], key, (((1,), (1,)), ((), ())), preferred_element_type=jnp.float32)
            mask = jnp.concatenate([masks[c], masks[c]], axis=1)
            masked = jnp.where(mask, scores, -1e30)
            row_max = jnp.max(masked, axis=1, keepdims=True)
            row_max = jnp.where(row_max > -1e29, row_max, 0.0)
            expo = jnp.exp(masked - row_max)
            total = jnp.maximum(jnp.sum(expo, axis=1, keepdims=True), 1.0)
            probs = (expo * (1.0 / total)).astype(jnp.bfloat16)
            attended = jnp.dot(probs, value, preferred_element_type=jnp.float32)
            out_ref[rows, head] = (x[rows] + attended).astype(jnp.bfloat16)


def attend(live, own, other, weights, x, inv, gain):
    tokens, width = x.shape
    whole = lambda *shape: pl.BlockSpec(shape, lambda i, live: (0,) * len(shape))
    return pl.pallas_call(
        attend_kernel,
        grid_spec=pltpu.PrefetchScalarGridSpec(
            num_scalar_prefetch=1,
            grid=(HEADS_HERE // HB,),
            in_specs=[
                whole(REQ * HALF, ENC_PAD),
                whole(REQ * HALF, ENC_PAD),
                pl.BlockSpec((RING, HB * 2 * W_PAD, HD), lambda i, live: (0, i, 0)),
                pl.BlockSpec((tokens, HB * HD), lambda i, live: (0, i)),
                whole(tokens, 1),
                pl.BlockSpec((1, HB * HD), lambda i, live: (0, i)),
            ],
            out_specs=pl.BlockSpec((tokens, HB * HD), lambda i, live: (0, i)),
        ),
        out_shape=jax.ShapeDtypeStruct((tokens, width), jnp.bfloat16),
        compiler_params=pltpu.CompilerParams(vmem_limit_bytes=40 * 2**20),
        name="attend_heads",
    )(live, own, other, weights, x, inv, gain)


def spread_of(core, x, y):
    u = jnp.where(core == 0, x, y)
    channel = lax.broadcasted_iota(jnp.int32, (ENC_PAD, ENC_PAD), 0)
    column = lax.broadcasted_iota(jnp.int32, (ENC_PAD, ENC_PAD), 1)

    def put(source):
        owner, row = source // W_PART, source % W_PART
        ou = jnp.where(core == 0, owner // SIDE, owner % SIDE)
        ov = jnp.where(core == 0, owner % SIDE, owner // SIDE)
        place = (ov * SIDE + (ou - u) % SIDE) * W_PAD + row
        used = jnp.logical_and(source >= 0, source < ENC)
        return jnp.logical_and(used, place == column).astype(jnp.bfloat16)

    return jnp.stack([put(channel), put(channel - (ENC_PAD - ENC))])


def source_table(requests, core, x, y):
    u, v = jnp.where(core == 0, x, y), jnp.where(core == 0, y, x)
    owner, block = requests // 6, requests % 6
    ou = jnp.where(core == 0, owner // SIDE, owner % SIDE)
    ov = jnp.where(core == 0, owner % SIDE, owner // SIDE)
    k, far = (ou - u) % SIDE, (ov - v) % SIDE
    opposite = jnp.where(k < 2, 3, 4)
    which = jnp.where(far == 0, 0, jnp.where(far == 1, 2, jnp.where(far == 3, 1, opposite)))
    chunk = jnp.where(which == 4, k - 2, k)
    odd = block % 2
    row = chunk * D_ROWS + (block // 2) * (TILES * HALF) + odd * (TILES - ENC_PAD // HD) * HALF
    return jnp.stack([which, row, odd])


def on_device(stream, gain, key_weight, value_weight, owners, blocks, valid, database):
    segments = lax.axis_size("segment")
    core = lax.axis_index("segment") % 2
    place = lax.axis_index("db")
    x_at, y_at = place // SIDE, place % SIDE
    rows = stream[0]
    tokens, local_width = rows.shape
    full_width = local_width * lax.axis_size("mp")

    def pack_weight(w):
        return jnp.pad(w[0], ((0, W_PAD - W_PART), (0, 0)))

    packed_w = jnp.concatenate([pack_weight(key_weight), pack_weight(value_weight)], axis=0)
    packed_w = packed_w.reshape(2 * W_PAD, HEADS_HERE, HD).transpose(1, 0, 2).reshape(W_ROWS, HD)
    next_w = to_next(packed_w)

    as_float = rows.astype(jnp.float32)
    squares = jnp.sum(as_float * as_float, axis=1)
    requests = (owners[0] * 6 + blocks[0]).reshape(-1)
    info = jnp.concatenate(
        [squares, gain[0], valid[0].reshape(-1).astype(jnp.float32), requests.astype(jnp.float32)]
    )
    info = jnp.pad(info, (0, -info.shape[0] % 1024)).reshape(-1, HD)
    info_here = to_next(info).reshape(-1)
    squares_other = to_next_other_mp(squares.reshape(-1, HD)).reshape(-1)
    requests_other = to_next_other_core(requests)
    x_here = to_next(rows)

    half = lax.dynamic_slice(database, (0, core * HALF, 0), (2 * PAIRS, HALF, ENC))
    paired = jnp.concatenate([half[0::2], half[1::2]], axis=2)
    packed_d = paired.reshape(PAIRS, HALF, TILES, HD).transpose(0, 2, 1, 3).reshape(D_ROWS, HD)

    payload = jnp.concatenate([next_w, packed_d], axis=0)
    cut = payload.shape[0] // 2
    before, after = turned(payload, 1, 0), turned(payload, -1, 0)
    opposite = jnp.concatenate([turned(before[:cut], 1, 0), turned(after[cut:], -1, 0)], axis=0)
    line = (payload, after, opposite, before)
    line_w = jnp.concatenate([piece[:W_ROWS] for piece in line], axis=0)
    line_d = jnp.concatenate([piece[W_ROWS:] for piece in line], axis=0)

    all_w = lax.all_gather(
        line_w, ("segment", "db"), axis=0, tiled=True, axis_index_groups=ring_groups(segments, 1)
    ).reshape(RING, W_ROWS, HD)
    d_before, d_after = turned(line_d, 1, 1), turned(line_d, -1, 1)
    mid = line_d.shape[0] // 2
    far_before, far_after = turned(d_before[:mid], 1, 1), turned(d_after[mid:], -1, 1)

    squares_here = info_here[:tokens]
    gain_here = info_here[tokens:tokens + local_width]
    ints = info_here[tokens + local_width:tokens + local_width + 2 * REQ].astype(jnp.int32)
    live, requests_here = ints[:REQ], ints[REQ:]
    inv_rms = lax.rsqrt((squares_here + squares_other) / full_width + eps_norm)

    table = jnp.concatenate(
        [source_table(requests_here, core, x_at, y_at), source_table(requests_other, core, x_at, y_at)], axis=1
    )
    own, given = pick(
        table,
        (line_d, d_before, d_after, far_before, far_after),
        spread_of(core, x_at, y_at),
        spread_of(1 - core, x_at, y_at),
    )
    other = other_core(given)
    updated = attend(live, own, other, all_w, x_here, inv_rms[:, None], gain_here[None, :])
    return updated[None]


def solution(mesh):
    return jax.shard_map(
        on_device,
        mesh=mesh,
        in_specs=(
            P("segment", "db", "mp"),
            P("segment", "mp"),
            P("segment", "db", "mp"),
            P("segment", "db", "mp"),
            P("segment", "db", None),
            P("segment", "db", None),
            P("segment", "db", None),
            P("db", None, None),
        ),
        out_specs=P("segment", "db", "mp"),
        check_vma=False,
    )
```

time: 240 us -> 190 us (0.79)
  the two profiles are of different devices: /device:TPU:4 before, /device:TPU:1 now
where the time goes in v1:
time: 190 us; the launch traced here: 189 us
  waiting for transfers between devices  62.1 us (33%)
  starting transfers between devices  55.6 us (29%)
  Pallas kernels  44.1 us (23%)
  between operations  13.9 us (7%)
  local copies, waits for them, and re-layouts  7.11 us (4%)
  other arithmetic  6.33 us (3%)
    ppermute x8, waiting for transfers between devices, turned(): return lax.ppermute(value, ('segment', 'db'), pairs)  48.6 us
    pallas_call x1, Pallas kernels, attend(): pl.pallas_call(attend_kernel, grid_spec=pltpu.PrefetchScalarGridSpec(num_...  37.4 us
    ppermute x8, starting transfers between devices, turned(): return lax.ppermute(value, ('segment', 'db'), pairs)  23.6 us
    ppermute x1, starting transfers between devices, other_core(): return lax.ppermute(value, 'segment', [(s, s ^ 1) for s in range(count)])  14.6 us
    ppermute x3, starting transfers between devices, to_next(): lax.ppermute(value, 'segment', [(s, (s + 1) % count) for s in range(count)])  10.8 us
    ppermute x1, waiting for transfers between devices, to_next_other_mp(): return lax.ppermute(value, ('segment', 'mp'), pairs)  9.33 us
    pallas_call x1, Pallas kernels, pick(): pl.pallas_call(pick_kernel, in_specs=[pl.BlockSpec(memory_space=pltpu.SME...  6.65 us
    ppermute x1, starting transfers between devices, to_next_other_mp(): return lax.ppermute(value, ('segment', 'mp'), pairs)  4.28 us
  transfers between devices with their start and end apart: 15, of which 9 were waited for; matrix products, arithmetic and copies ran while one was open for 4% of the time, Pallas kernels for 4%

profile of v1, /device:TPU:1, one launch (start us, length us, event | category | flops | bytes accessed | tf_op | source)
XLA Modules:
  0.0 189.1 jit_solution(7916989289554159456)
XLA Ops:
  7.6 4.9 %collective-permute-start.2 = (bf16[1024,128]{1,0:T(8,128)(2,1)S(1)}, bf16[1024,128]{1,0:T(8,128)(2,1)S(1)}, u32[]{:S(2)}, u32[]{:S(2)}) collective-permute-start(bf16[1024,128]{1,0:T(8,128)(2,1)S(1)} %bitcast.48), channel_id=1, source_target_pairs={{0,32},{32,64},{64,96},{96,128},{128,160},{160,192},{192,224},{224... | collective-permute-start | bytes 786440 | tf_op jit(solution)/shard_map/ppermute | solution.py:60
  13.4 4.1 %collective-permute-done.2 = bf16[1024,128]{1,0:T(8,128)(2,1)S(1)} collective-permute-done((bf16[1024,128]{1,0:T(8,128)(2,1)S(1)}, bf16[1024,128]{1,0:T(8,128)(2,1)S(1)}, u32[]{:S(2)}, u32[]{:S(2)}) %collective-permute-start.2) | collective-permute-done | bytes 262176 | tf_op jit(solution)/shard_map/ppermute | solution.py:60
  20.3 4.6 %collective-permute-start.3 = (bf16[2368,128]{1,0:T(8,128)(2,1)S(1)}, bf16[2368,128]{1,0:T(8,128)(2,1)S(1)}, u32[]{:S(2)}, u32[]{:S(2)}) collective-permute-start(bf16[2368,128]{1,0:T(8,128)(2,1)S(1)} %pad_maximum_fusion.2), channel_id=1, source_target_pairs={{0,24},{2,26},{4,28},{6,30},{8,0},{10,2},{12,4},{14,6},{16,8},{18,... | collective-permute-start | bytes 1818632 | tf_op jit(solution)/shard_map/ppermute | solution.py:55
  24.8 5.5 %collective-permute-done.4 = bf16[2368,128]{1,0:T(8,128)(2,1)S(1)} collective-permute-done((bf16[2368,128]{1,0:T(8,128)(2,1)S(1)}, bf16[2368,128]{1,0:T(8,128)(2,1)S(1)}, u32[]{:S(2)}, u32[]{:S(2)}) %collective-permute-start.4) | collective-permute-done | bytes 606240 | tf_op jit(solution)/shard_map/ppermute | solution.py:55
  33.3 6.2 %collective-permute-done.5 = bf16[1184,128]{1,0:T(8,128)(2,1)S(1)} collective-permute-done((bf16[1184,128]{1,0:T(8,128)(2,1)S(1)}, bf16[1184,128]{1,0:T(8,128)(2,1)S(1)}, u32[]{:S(2)}, u32[]{:S(2)}) %collective-permute-start.5) | collective-permute-done | bytes 303136 | tf_op jit(solution)/shard_map/ppermute | solution.py:55
  40.8 2.3 %collective-permute-start.1 = (s32[12]{0:T(128)S(1)}, s32[12]{0:T(128)S(1)}, u32[]{:S(2)}, u32[]{:S(2)}) collective-permute-start(s32[12]{0:T(128)S(1)} %add.343), channel_id=1, source_target_pairs={{0,0},{32,96},{64,64},{96,160},{128,128},{160,224},{192,192},{224,... | collective-permute-start | bytes 152 | tf_op jit(solution)/shard_map/ppermute | solution.py:65
  43.8 3.1 %collective-permute-start = (f32[24,128]{1,0:T(8,128)S(1)}, f32[24,128]{1,0:T(8,128)S(1)}, u32[]{:S(2)}, u32[]{:S(2)}) collective-permute-start(f32[24,128]{1,0:T(8,128)S(1)} %pad_bitcast_fusion), channel_id=1, source_target_pairs={{0,32},{32,64},{64,96},{96,128},{128,160},{160,192},{192,224},{224... | collective-permute-start | bytes 36872 | tf_op jit(solution)/shard_map/ppermute | solution.py:60
  46.9 2.7 %collective-permute-start.12 = (bf16[384,2048]{1,0:T(8,128)(2,1)}, bf16[384,2048]{1,0:T(8,128)(2,1)S(1)}, u32[]{:S(2)}, u32[]{:S(2)}) collective-permute-start(bf16[384,2048]{1,0:T(8,128)(2,1)} %bitcast.47), channel_id=1, source_target_pairs={{0,32},{32,64},{64,96},{96,128},{128,160},{160,192},{192,224},{224... | collective-permute-start | bytes 4718600 | tf_op jit(solution)/shard_map/ppermute | solution.py:60
  50.8 3.9 %collective-permute-start.6 = (bf16[1184,128]{1,0:T(8,128)(2,1)S(1)}, bf16[1184,128]{1,0:T(8,128)(2,1)S(1)}, u32[]{:S(2)}, u32[]{:S(2)}) collective-permute-start(bf16[1184,128]{1,0:T(8,128)(2,1)S(1)} %slice.73), channel_id=1, source_target_pairs={{0,24},{2,26},{4,28},{6,30},{8,0},{10,2},{12,4},{14,6},{16,8},{18,... | collective-permute-start | bytes 909320 | tf_op jit(solution)/shard_map/ppermute | solution.py:55
  55.8 2.7 %collective-permute-done.6 = bf16[1184,128]{1,0:T(8,128)(2,1)S(1)} collective-permute-done((bf16[1184,128]{1,0:T(8,128)(2,1)S(1)}, bf16[1184,128]{1,0:T(8,128)(2,1)S(1)}, u32[]{:S(2)}, u32[]{:S(2)}) %collective-permute-start.6) | collective-permute-done | bytes 303136 | tf_op jit(solution)/shard_map/ppermute | solution.py:55
  58.5 2.5 %collective-permute-start.7 = (bf16[5376,128]{1,0:T(8,128)(2,1)S(1)}, bf16[5376,128]{1,0:T(8,128)(2,1)S(1)}, u32[]{:S(2)}, u32[]{:S(2)}) collective-permute-start(bf16[5376,128]{1,0:T(8,128)(2,1)S(1)} %fusion.4.c_ref), channel_id=1, source_target_pairs={{0,2},{2,4},{4,6},{6,0},{8,10},{10,12},{12,14},{14,8},{16,18},{18,... | collective-permute-start | bytes 4128776 | tf_op jit(solution)/shard_map/ppermute | solution.py:55
  61.0 4.0 %collective-permute-start.8 = (bf16[5376,128]{1,0:T(8,128)(2,1)S(1)}, bf16[5376,128]{1,0:T(8,128)(2,1)S(1)}, u32[]{:S(2)}, u32[]{:S(2)}) collective-permute-start(bf16[5376,128]{1,0:T(8,128)(2,1)S(1)} %fusion.4.c_ref), channel_id=1, source_target_pairs={{0,6},{2,0},{4,2},{6,4},{8,14},{10,8},{12,10},{14,12},{16,22},{18,... | collective-permute-start | bytes 4128776 | tf_op jit(solution)/shard_map/ppermute | solution.py:55
  65.0 2.6 %fusion.29 = (pred[1,512,512]{2,1,0:T(8,128)(4,1)S(1)}, pred[1,512,512]{2,1,0:T(8,128)(4,1)S(1)}, pred[1,512,512]{2,1,0:T(8,128)(4,1)S(1)}, pred[1,512,512]{2,1,0:T(8,128)(4,1)S(1)}) fusion(s32[]{:T(128)S(6)} %select_n.544, s32[512]{0:T(512)S(1)} %fusion.48, s32[512]{0:T(512)S(1)} %fusion.55, pred[512]{0:T(512)(128)(4,1)S(1)} %compare_and_fusion, ...), kind=kLoop, calls=%fused_computation.67 | loop fusion | flops 31981568 | bytes 1068042 | tf_op jit(solution)/shard_map/and | solution.py:200
  68.2 17.9 %collective-permute-done.7.l_ref = bf16[5376,128]{1,0:T(8,128)(2,1)S(1)} collective-permute-done((bf16[5376,128]{1,0:T(8,128)(2,1)S(1)}, bf16[5376,128]{1,0:T(8,128)(2,1)S(1)}, u32[]{:S(2)}, u32[]{:S(2)}) %collective-permute-start.7) | collective-permute-done | bytes 1376288 | tf_op jit(solution)/shard_map/ppermute | solution.py:55
  88.0 7.4 %collective-permute-done.8.r_ref = bf16[5376,128]{1,0:T(8,128)(2,1)S(1)} collective-permute-done((bf16[5376,128]{1,0:T(8,128)(2,1)S(1)}, bf16[5376,128]{1,0:T(8,128)(2,1)S(1)}, u32[]{:S(2)}, u32[]{:S(2)}) %collective-permute-start.8) | collective-permute-done | bytes 1376288 | tf_op jit(solution)/shard_map/ppermute | solution.py:55
  95.5 2.8 %collective-permute-start.10 = (bf16[2688,128]{1,0:T(8,128)(2,1)S(1)}, bf16[2688,128]{1,0:T(8,128)(2,1)S(1)}, u32[]{:S(2)}, u32[]{:S(2)}) collective-permute-start(bf16[2688,128]{1,0:T(8,128)(2,1)S(1)} %slice.76), channel_id=1, source_target_pairs={{0,6},{2,0},{4,2},{6,4},{8,14},{10,8},{12,10},{14,12},{16,22},{18,... | collective-permute-start | bytes 2064392 | tf_op jit(solution)/shard_map/ppermute | solution.py:55
  98.5 4.8 %collective-permute-done.9.ol_ref = bf16[2688,128]{1,0:T(8,128)(2,1)S(1)} collective-permute-done((bf16[2688,128]{1,0:T(8,128)(2,1)S(1)}, bf16[2688,128]{1,0:T(8,128)(2,1)S(1)}, u32[]{:S(2)}, u32[]{:S(2)}) %collective-permute-start.9) | collective-permute-done | bytes 688160 | tf_op jit(solution)/shard_map/ppermute | solution.py:55
  103.3 4.2 %collective-permute-done.10.or_ref = bf16[2688,128]{1,0:T(8,128)(2,1)S(1)} collective-permute-done((bf16[2688,128]{1,0:T(8,128)(2,1)S(1)}, bf16[2688,128]{1,0:T(8,128)(2,1)S(1)}, u32[]{:S(2)}, u32[]{:S(2)}) %collective-permute-start.10) | collective-permute-done | bytes 688160 | tf_op jit(solution)/shard_map/ppermute | solution.py:55
  107.5 6.6 %pick_encodings.1 = (bf16[768,512]{1,0:T(8,128)(2,1)S(1)}, bf16[768,512]{1,0:T(8,128)(2,1)}) custom-call(s32[3,24]{1,0:T(4,128)S(1)} %add_add_fusion.table, bf16[5376,128]{1,0:T(8,128)(2,1)S(1)} %fusion.4.c_ref, bf16[5376,128]{1,0:T(8,128)(2,1)S(1)} %collective-permute-done.7.l_ref, bf16[5376,128]{1,0:T(8,128)(2,1)S(1)} %collective-permute-done.8.r_ref, ...), custom_call_target="tpu_custom_call" | custom-call | tf_op jit(solution)/shard_map/pick_encodings/pallas_call | solution.py:115
  114.2 14.6 %collective-permute-start.11 = (bf16[768,512]{1,0:T(8,128)(2,1)}, bf16[768,512]{1,0:T(8,128)(2,1)}, u32[]{:S(2)}, u32[]{:S(2)}) collective-permute-start(bf16[768,512]{1,0:T(8,128)(2,1)} %get-tuple-element.8), channel_id=1, source_target_pairs={{0,32},{32,0},{64,96},{96,64},{128,160},{160,128},{192,224},{224,1... | collective-permute-start | bytes 2359304 | tf_op jit(solution)/shard_map/ppermute | solution.py:76
  128.8 4.3 %collective-permute-start.13 = (f32[3,128]{1,0:T(4,128)S(1)}, f32[3,128]{1,0:T(4,128)S(1)}, u32[]{:S(2)}, u32[]{:S(2)}) collective-permute-start(f32[3,128]{1,0:T(4,128)S(1)} %bitcast.52), channel_id=1, source_target_pairs={{0,33},{1,32},{32,65},{33,64},{64,97},{65,96},{96,129},{97,128},{1... | collective-permute-start | bytes 4616 | tf_op jit(solution)/shard_map/ppermute | solution.py:71
  133.1 9.3 %collective-permute-done.13 = f32[3,128]{1,0:T(4,128)S(1)} collective-permute-done((f32[3,128]{1,0:T(4,128)S(1)}, f32[3,128]{1,0:T(4,128)S(1)}, u32[]{:S(2)}, u32[]{:S(2)}) %collective-permute-start.13) | collective-permute-done | bytes 1568 | tf_op jit(solution)/shard_map/ppermute | solution.py:71
  142.7 2.2 %copy-done.1 = bf16[16384,128]{1,0:T(8,128)(2,1)S(1)} copy-done((bf16[16384,128]{1,0:T(8,128)(2,1)S(1)}, bf16[16384,128]{1,0:T(8,128)(2,1)}, u32[]{:S(2)}) %copy-start.1) | copy-done | bytes 4194328
  144.8 37.4 %attend_heads.1 = bf16[384,2048]{1,0:T(8,128)(2,1)} custom-call(s32[12]{0:T(128)S(1)} %get-tuple-element.26.live, bf16[768,512]{1,0:T(8,128)(2,1)S(1)} %get-tuple-element.7.own_ref, bf16[768,512]{1,0:T(8,128)(2,1)} %collective-permute-done.11.other_ref, bf16[16,1024,128]{2,1,0:T(8,128)(2,1)S(1)} %bitcast.41, ...), custom_call_target="tpu_custom_call" | custom-call | tf_op jit(solution)/shard_map/attend_heads/pallas_call | solution.py:168
  (83 shorter events, 14.6 us)
Async XLA Ops:
  6.5 6.1 %copy-start = (bf16[6,128,448]{1,2,0:T(8,128)(2,1)S(1)}, bf16[6,128,448]{1,2,0:T(8,128)(2,1)}, u32[]{:S(2)}) copy-start(bf16[6,128,448]{1,2,0:T(8,128)(2,1)} %param.15) | copy-start | bytes 2064388
  6.5 136.1 %all-gather.2.cloned.1.call-start = ((), (), s32[]{:S(2)}) async-start(), calls=%async_computation | async-start | bytes 5242880 | tf_op jit(solution)/shard_map/all_gather | solution.py:259
  7.6 9.8 %collective-permute-start.2 = (bf16[1024,128]{1,0:T(8,128)(2,1)S(1)}, bf16[1024,128]{1,0:T(8,128)(2,1)S(1)}, u32[]{:S(2)}, u32[]{:S(2)}) collective-permute-start(bf16[1024,128]{1,0:T(8,128)(2,1)S(1)} %bitcast.48), channel_id=1, source_target_pairs={{0,32},{32,64},{64,96},{96,128},{128,160},{160,192},{192,224},{224... | collective-permute-start | bytes 786440 | tf_op jit(solution)/shard_map/ppermute | solution.py:60
  18.2 21.3 %copy-start.5 = (bf16[1024,128]{1,0:T(8,128)(2,1)S(1)}, bf16[1024,128]{1,0:T(8,128)(2,1)}, u32[]{:S(2)}) copy-start(bf16[1024,128]{1,0:T(8,128)(2,1)} %copy-done.4) | copy-start | bytes 786436
  18.2 12.1 %collective-permute-start.4 = (bf16[2368,128]{1,0:T(8,128)(2,1)S(1)}, bf16[2368,128]{1,0:T(8,128)(2,1)S(1)}, u32[]{:S(2)}, u32[]{:S(2)}) collective-permute-start(bf16[2368,128]{1,0:T(8,128)(2,1)S(1)} %pad_maximum_fusion.2), channel_id=1, source_target_pairs={{0,8},{2,10},{4,12},{6,14},{8,16},{10,18},{12,20},{14,22},{16,24},... | collective-permute-start | bytes 1818632 | tf_op jit(solution)/shard_map/ppermute | solution.py:55
  20.3 12.1 %collective-permute-start.3 = (bf16[2368,128]{1,0:T(8,128)(2,1)S(1)}, bf16[2368,128]{1,0:T(8,128)(2,1)S(1)}, u32[]{:S(2)}, u32[]{:S(2)}) collective-permute-start(bf16[2368,128]{1,0:T(8,128)(2,1)S(1)} %pad_maximum_fusion.2), channel_id=1, source_target_pairs={{0,24},{2,26},{4,28},{6,30},{8,0},{10,2},{12,4},{14,6},{16,8},{18,... | collective-permute-start | bytes 1818632 | tf_op jit(solution)/shard_map/ppermute | solution.py:55
  30.4 9.1 %collective-permute-start.5 = (bf16[1184,128]{1,0:T(8,128)(2,1)S(1)}, bf16[1184,128]{1,0:T(8,128)(2,1)S(1)}, u32[]{:S(2)}, u32[]{:S(2)}) collective-permute-start(bf16[1184,128]{1,0:T(8,128)(2,1)S(1)} %slice.72), channel_id=1, source_target_pairs={{0,8},{2,10},{4,12},{6,14},{8,16},{10,18},{12,20},{14,22},{16,24},... | collective-permute-start | bytes 909320 | tf_op jit(solution)/shard_map/ppermute | solution.py:55
  32.3 8.2 %copy-start.7 = (s32[1,6,2]{1,2,0:T(2,128)S(1)}, s32[1,6,2]{1,2,0:T(2,128)}, u32[]{:S(2)}) copy-start(s32[1,6,2]{1,2,0:T(2,128)} %param.13) | copy-start | bytes 148
  32.3 8.2 %copy-start.8 = (s32[1,6,2]{1,2,0:T(2,128)S(1)}, s32[1,6,2]{1,2,0:T(2,128)}, u32[]{:S(2)}) copy-start(s32[1,6,2]{1,2,0:T(2,128)} %param.12) | copy-start | bytes 148
  32.4 10.7 %copy-start.9 = (s32[1,6,2]{1,2,0:T(2,128)S(1)}, s32[1,6,2]{1,2,0:T(2,128)}, u32[]{:S(2)}) copy-start(s32[1,6,2]{1,2,0:T(2,128)} %param.14) | copy-start | bytes 148
  32.4 10.9 %copy-start.2 = (bf16[1,384,2048]{2,1,0:T(8,128)(2,1)S(1)}, bf16[1,384,2048]{2,1,0:T(8,128)(2,1)}, u32[]{:S(2)}) copy-start(bf16[1,384,2048]{2,1,0:T(8,128)(2,1)} %param.8) | copy-start | bytes 4718596
  32.4 0.8 copy-start.3
  39.5 4.2 %copy-start.6 = (f32[1,2048]{1,0:T(1,128)S(1)}, f32[1,2048]{1,0:T(1,128)}, u32[]{:S(2)}) copy-start(f32[1,2048]{1,0:T(1,128)} %param.9) | copy-start | bytes 24580
  40.8 27.3 %collective-permute-start.1 = (s32[12]{0:T(128)S(1)}, s32[12]{0:T(128)S(1)}, u32[]{:S(2)}, u32[]{:S(2)}) collective-permute-start(s32[12]{0:T(128)S(1)} %add.343), channel_id=1, source_target_pairs={{0,0},{32,96},{64,64},{96,160},{128,128},{160,224},{192,192},{224,... | collective-permute-start | bytes 152 | tf_op jit(solution)/shard_map/ppermute | solution.py:65
  43.8 54.5 %collective-permute-start = (f32[24,128]{1,0:T(8,128)S(1)}, f32[24,128]{1,0:T(8,128)S(1)}, u32[]{:S(2)}, u32[]{:S(2)}) collective-permute-start(f32[24,128]{1,0:T(8,128)S(1)} %pad_bitcast_fusion), channel_id=1, source_target_pairs={{0,32},{32,64},{64,96},{96,128},{128,160},{160,192},{192,224},{224... | collective-permute-start | bytes 36872 | tf_op jit(solution)/shard_map/ppermute | solution.py:60
  46.9 95.7 %collective-permute-start.12 = (bf16[384,2048]{1,0:T(8,128)(2,1)}, bf16[384,2048]{1,0:T(8,128)(2,1)S(1)}, u32[]{:S(2)}, u32[]{:S(2)}) collective-permute-start(bf16[384,2048]{1,0:T(8,128)(2,1)} %bitcast.47), channel_id=1, source_target_pairs={{0,32},{32,64},{64,96},{96,128},{128,160},{160,192},{192,224},{224... | collective-permute-start | bytes 4718600 | tf_op jit(solution)/shard_map/ppermute | solution.py:60
  50.8 7.6 %collective-permute-start.6 = (bf16[1184,128]{1,0:T(8,128)(2,1)S(1)}, bf16[1184,128]{1,0:T(8,128)(2,1)S(1)}, u32[]{:S(2)}, u32[]{:S(2)}) collective-permute-start(bf16[1184,128]{1,0:T(8,128)(2,1)S(1)} %slice.73), channel_id=1, source_target_pairs={{0,24},{2,26},{4,28},{6,30},{8,0},{10,2},{12,4},{14,6},{16,8},{18,... | collective-permute-start | bytes 909320 | tf_op jit(solution)/shard_map/ppermute | solution.py:55
  58.5 27.5 %collective-permute-start.7 = (bf16[5376,128]{1,0:T(8,128)(2,1)S(1)}, bf16[5376,128]{1,0:T(8,128)(2,1)S(1)}, u32[]{:S(2)}, u32[]{:S(2)}) collective-permute-start(bf16[5376,128]{1,0:T(8,128)(2,1)S(1)} %fusion.4.c_ref), channel_id=1, source_target_pairs={{0,2},{2,4},{4,6},{6,0},{8,10},{10,12},{12,14},{14,8},{16,18},{18,... | collective-permute-start | bytes 4128776 | tf_op jit(solution)/shard_map/ppermute | solution.py:55
  61.0 34.4 %collective-permute-start.8 = (bf16[5376,128]{1,0:T(8,128)(2,1)S(1)}, bf16[5376,128]{1,0:T(8,128)(2,1)S(1)}, u32[]{:S(2)}, u32[]{:S(2)}) collective-permute-start(bf16[5376,128]{1,0:T(8,128)(2,1)S(1)} %fusion.4.c_ref), channel_id=1, source_target_pairs={{0,6},{2,0},{4,2},{6,4},{8,14},{10,8},{12,10},{14,12},{16,22},{18,... | collective-permute-start | bytes 4128776 | tf_op jit(solution)/shard_map/ppermute | solution.py:55
  86.1 17.2 %collective-permute-start.9 = (bf16[2688,128]{1,0:T(8,128)(2,1)S(1)}, bf16[2688,128]{1,0:T(8,128)(2,1)S(1)}, u32[]{:S(2)}, u32[]{:S(2)}) collective-permute-start(bf16[2688,128]{1,0:T(8,128)(2,1)S(1)} %slice.75), channel_id=1, source_target_pairs={{0,2},{2,4},{4,6},{6,0},{8,10},{10,12},{12,14},{14,8},{16,18},{18,... | collective-permute-start | bytes 2064392 | tf_op jit(solution)/shard_map/ppermute | solution.py:55
  95.5 12.0 %collective-permute-start.10 = (bf16[2688,128]{1,0:T(8,128)(2,1)S(1)}, bf16[2688,128]{1,0:T(8,128)(2,1)S(1)}, u32[]{:S(2)}, u32[]{:S(2)}) collective-permute-start(bf16[2688,128]{1,0:T(8,128)(2,1)S(1)} %slice.76), channel_id=1, source_target_pairs={{0,6},{2,0},{4,2},{6,4},{8,14},{10,8},{12,10},{14,12},{16,22},{18,... | collective-permute-start | bytes 2064392 | tf_op jit(solution)/shard_map/ppermute | solution.py:55
  114.2 28.4 %collective-permute-start.11 = (bf16[768,512]{1,0:T(8,128)(2,1)}, bf16[768,512]{1,0:T(8,128)(2,1)}, u32[]{:S(2)}, u32[]{:S(2)}) collective-permute-start(bf16[768,512]{1,0:T(8,128)(2,1)} %get-tuple-element.8), channel_id=1, source_target_pairs={{0,32},{32,0},{64,96},{96,64},{128,160},{160,128},{192,224},{224,1... | collective-permute-start | bytes 2359304 | tf_op jit(solution)/shard_map/ppermute | solution.py:76
  128.8 13.6 %collective-permute-start.13 = (f32[3,128]{1,0:T(4,128)S(1)}, f32[3,128]{1,0:T(4,128)S(1)}, u32[]{:S(2)}, u32[]{:S(2)}) collective-permute-start(f32[3,128]{1,0:T(4,128)S(1)} %bitcast.52), channel_id=1, source_target_pairs={{0,33},{1,32},{32,65},{33,64},{64,97},{65,96},{96,129},{97,128},{1... | collective-permute-start | bytes 4616 | tf_op jit(solution)/shard_map/ppermute | solution.py:71
  142.6 2.2 %copy-start.1 = (bf16[16384,128]{1,0:T(8,128)(2,1)S(1)}, bf16[16384,128]{1,0:T(8,128)(2,1)}, u32[]{:S(2)}) copy-start(bf16[16384,128]{1,0:T(8,128)(2,1)} %all-gather.2.cloned.1.call-done) | copy-start | bytes 12582916
  (1 other events, 0.7 us)
Sparse Core Ops, SparseCore 0:
  40.7 60.3 all-gather.1

commit v2 on v1

v2 whole, which is shorter than its diff:
```python
import jax
import jax.numpy as jnp
from jax import lax
from jax.experimental import pallas as pl
from jax.experimental.pallas import tpu as pltpu
from jax.sharding import PartitionSpec as P

HD = 128
GROUP = 64
SIDE = 4
RING = SIDE * SIDE
eps_norm = 1e-06

W_PART = 28
W_PAD = 32
HEADS_HERE = 16
W_ROWS = HEADS_HERE * 2 * W_PAD
ENC = 448
ENC_PAD = RING * W_PAD
HALF = 64
TILES = 2 * ENC // HD
PAIRS = 3
D_ROWS = PAIRS * TILES * HALF
SLAB = ENC_PAD // HD * HALF
REQ = 12
HB = 2


def ring_pairs(segments, turn, along_x_core):
    pairs = []
    for seg in range(segments):
        for place in range(RING):
            x, y = divmod(place, SIDE)
            if seg % 2 == along_x_core:
                to = ((x + turn) % SIDE) * SIDE + y
            else:
                to = x * SIDE + (y + turn) % SIDE
            pairs.append((seg * RING + place, seg * RING + to))
    return pairs


def ring_groups(segments, along_x_core):
    groups = []
    for seg in range(segments):
        for line in range(SIDE):
            if seg % 2 == along_x_core:
                groups.append([seg * RING + x * SIDE + line for x in range(SIDE)])
            else:
                groups.append([seg * RING + line * SIDE + y for y in range(SIDE)])
    return groups


def turned(value, turn, along_x_core):
    pairs = ring_pairs(lax.axis_size("segment"), turn, along_x_core)
    return lax.ppermute(value, ("segment", "db"), pairs)


def to_next_turned(value, turn):
    count = lax.axis_size("segment")
    behind = ring_pairs(count, turn, 0)
    pairs = [(((seg - 1) % count) * RING + place, to) for seg in range(count) for place, to in
             [(source % RING, target) for source, target in behind[seg * RING:(seg + 1) * RING]]]
    return lax.ppermute(value, ("segment", "db"), pairs)


def to_next(value):
    count = lax.axis_size("segment")
    return lax.ppermute(value, "segment", [(s, (s + 1) % count) for s in range(count)])


def to_next_other_core(value):
    count = lax.axis_size("segment")
    return lax.ppermute(value, "segment", [(s, ((s + 1) % count) ^ 1) for s in range(count)])


def other_mp(value):
    return lax.ppermute(value, "mp", [(0, 1), (1, 0)])


def other_core(value):
    count = lax.axis_size("segment")
    return lax.ppermute(value, "segment", [(s, s ^ 1) for s in range(count)])


def fetch(table, first, sources, slabs, sems):
    def begin(i, carry):
        which = table[0, first + i]
        row = pl.multiple_of(table[1, first + i], 64)
        for number, source in enumerate(sources):
            @pl.when(which == number)
            def _():
                pltpu.make_async_copy(source.at[pl.ds(row, SLAB)], slabs.at[i], sems.at[i]).start()
        return carry

    def finish(i, carry):
        pltpu.make_async_copy(sources[0].at[pl.ds(0, SLAB)], slabs.at[i], sems.at[i]).wait()
        return carry

    lax.fori_loop(0, REQ, begin, 0)
    lax.fori_loop(0, REQ, finish, 0)


def spread_slabs(table, slabs, spread):
    tiles = ENC_PAD // HD
    rows = []
    for i in range(REQ):
        slab = slabs[i]
        rows.append(jnp.concatenate([slab[t * HALF:(t + 1) * HALF] for t in range(tiles)], axis=1))
    stacked = jnp.concatenate(rows, axis=0)
    even = jnp.dot(stacked, spread[0], preferred_element_type=jnp.float32)
    odd = jnp.dot(stacked, spread[1], preferred_element_type=jnp.float32)
    placed = []
    for i in range(REQ):
        here = slice(i * HALF, (i + 1) * HALF)
        placed.append(jnp.where(table[2, i] == 1, odd[here], even[here]).astype(jnp.bfloat16))
    return placed


def give_kernel(table, c_ref, r_ref, ol_ref, or_ref, l_ref, out_ref, sems):
    fetch(table, REQ, (c_ref, r_ref, ol_ref, or_ref, l_ref), out_ref, sems)


def pick_kernel(table, c_ref, r_ref, ol_ref, or_ref, l_ref, spread, out_ref, slabs, sems):
    fetch(table, 0, (c_ref, r_ref, ol_ref, or_ref, l_ref), slabs, sems)
    for i, block in enumerate(spread_slabs(table, slabs, spread)):
        out_ref[i * HALF:(i + 1) * HALF] = block


SMEM = pl.BlockSpec(memory_space=pltpu.SMEM)
VMEM = pl.BlockSpec(memory_space=pltpu.VMEM)
ANY = pl.BlockSpec(memory_space=pl.ANY)


def give(table, pieces):
    return pl.pallas_call(
        give_kernel,
        in_specs=[SMEM] + [ANY] * 5,
        out_specs=VMEM,
        out_shape=jax.ShapeDtypeStruct((REQ, SLAB, HD), jnp.bfloat16),
        scratch_shapes=[pltpu.SemaphoreType.DMA((REQ,))],
        compiler_params=pltpu.CompilerParams(vmem_limit_bytes=16 * 2**20),
        name="give_encodings",
    )(table, *pieces)


def pick(table, pieces, spread):
    return pl.pallas_call(
        pick_kernel,
        in_specs=[SMEM] + [ANY] * 5 + [VMEM],
        out_specs=VMEM,
        out_shape=jax.ShapeDtypeStruct((REQ * HALF, ENC_PAD), jnp.bfloat16),
        scratch_shapes=[
            pltpu.VMEM((REQ, SLAB, HD), jnp.bfloat16),
            pltpu.SemaphoreType.DMA((REQ,)),
        ],
        compiler_params=pltpu.CompilerParams(vmem_limit_bytes=32 * 2**20),
        name="pick_encodings",
    )(table, *pieces, spread)


def attend_kernel(
    live, table, own_ref, slabs, spread, w_ref, x_ref, inv_ref, gain_ref, out_ref, other_ref
):

    @pl.when(pl.program_id(0) == 0)
    def _():
        for i, block in enumerate(spread_slabs(table, slabs, spread)):
            other_ref[i * HALF:(i + 1) * HALF] = block

    own, other = own_ref[...], other_ref[...]
    inv = inv_ref[...]
    groups = x_ref.shape[0] // GROUP
    column = lax.broadcasted_iota(jnp.int32, (1, HD), 1)
    biases = []
    for c in range(groups):
        bias = jnp.where(jnp.where(column < HALF, live[2 * c], live[2 * c + 1]) > 0, 0.0, -1e30)
        biases.append(jnp.broadcast_to(jnp.concatenate([bias, bias], axis=1), (GROUP, 4 * HALF)))
    bias = jnp.concatenate(biases, axis=0)
    for b in range(HB):
        base = b * 2 * W_PAD
        head = slice(b * HD, (b + 1) * HD)
        key_w = jnp.concatenate([w_ref[j, base:base + W_PAD] for j in range(RING)], axis=0)
        value_w = jnp.concatenate([w_ref[j, base + W_PAD:base + 2 * W_PAD] for j in range(RING)], axis=0)
        weight = jnp.concatenate([key_w, value_w], axis=1)
        kv_own = jnp.dot(own, weight, preferred_element_type=jnp.float32).astype(jnp.bfloat16)
        kv_other = jnp.dot(other, weight, preferred_element_type=jnp.float32).astype(jnp.bfloat16)
        x = x_ref[:, head].astype(jnp.float32)
        q = (x * inv * gain_ref[:, head] * HD ** (-0.5)).astype(jnp.bfloat16)
        scores, values = [], []
        for c in range(groups):
            keys = slice(c * 2 * HALF, (c + 1) * 2 * HALF)
            key = jnp.concatenate([kv_own[keys, :HD], kv_other[keys, :HD]], axis=0)
            values.append(jnp.concatenate([kv_own[keys, HD:], kv_other[keys, HD:]], axis=0))
            scores.append(
                lax.dot_general(
                    q[c * GROUP:(c + 1) * GROUP],
                    key,
                    (((1,), (1,)), ((), ())),
                    preferred_element_type=jnp.float32,
                )
            )
        masked = jnp.concatenate(scores, axis=0) + bias
        row_max = jnp.max(masked, axis=1, keepdims=True)
        row_max = jnp.where(row_max > -1e29, row_max, 0.0)
        expo = jnp.exp(masked - row_max)
        total = jnp.maximum(jnp.sum(expo, axis=1, keepdims=True), 1.0)
        probs = (expo * (1.0 / total)).astype(jnp.bfloat16)
        attended = [
            jnp.dot(probs[c * GROUP:(c + 1) * GROUP], values[c], preferred_element_type=jnp.float32)
            for c in range(groups)
        ]
        out_ref[:, head] = (x + jnp.concatenate(attended, axis=0)).astype(jnp.bfloat16)


def attend(live, table, own, slabs, spread, weights, x, inv, gain):
    tokens, width = x.shape
    whole = lambda *shape: pl.BlockSpec(shape, lambda i, live, table: (0,) * len(shape))
    return pl.pallas_call(
        attend_kernel,
        grid_spec=pltpu.PrefetchScalarGridSpec(
            num_scalar_prefetch=2,
            grid=(HEADS_HERE // HB,),
            in_specs=[
                whole(REQ * HALF, ENC_PAD),
                whole(REQ, SLAB, HD),
                whole(2, ENC_PAD, ENC_PAD),
                pl.BlockSpec((RING, HB * 2 * W_PAD, HD), lambda i, live, table: (0, i, 0)),
                pl.BlockSpec((tokens, HB * HD), lambda i, live, table: (0, i)),
                whole(tokens, 1),
                pl.BlockSpec((1, HB * HD), lambda i, live, table: (0, i)),
            ],
            out_specs=pl.BlockSpec((tokens, HB * HD), lambda i, live, table: (0, i)),
            scratch_shapes=[pltpu.VMEM((REQ * HALF, ENC_PAD), jnp.bfloat16)],
        ),
        out_shape=jax.ShapeDtypeStruct((tokens, width), jnp.bfloat16),
        compiler_params=pltpu.CompilerParams(vmem_limit_bytes=58 * 2**20),
        name="attend_heads",
    )(live, table, own, slabs, spread, weights, x, inv, gain)


def ring_place(owner, core):
    x, y = owner // SIDE, owner % SIDE
    return jnp.where(core == 0, x, y), jnp.where(core == 0, y, x)


def spread_of(core, here):
    channel = lax.broadcasted_iota(jnp.int32, (ENC_PAD, ENC_PAD), 0)
    column = lax.broadcasted_iota(jnp.int32, (ENC_PAD, ENC_PAD), 1)

    def put(source):
        near, far = ring_place(source // W_PART, core)
        near = (near - ring_place(here, core)[0]) % SIDE
        place = (far * SIDE + near) * W_PAD + source % W_PART
        used = jnp.logical_and(source >= 0, source < ENC)
        return jnp.logical_and(used, place == column).astype(jnp.bfloat16)

    return jnp.stack([put(channel), put(channel - (ENC_PAD - ENC))])


def source_table(requests, core, here):
    owner, block = requests // 6, requests % 6
    near, far = ring_place(owner, core)
    far = (far - ring_place(here, core)[1]) % SIDE
    which = jnp.where(far < 2, far, jnp.where(far == 3, 4, jnp.where(near < 2, 2, 3)))
    chunk = jnp.where(which == 3, near - 2, near)
    odd = block % 2
    row = chunk * D_ROWS + (block // 2) * (TILES * HALF) + odd * (TILES - ENC_PAD // HD) * HALF
    return jnp.stack([which, row, odd])


def first_ring(piece):
    groups = ring_groups(lax.axis_size("segment"), 0)
    copies = jnp.tile(piece, (SIDE, 1))
    return lax.all_to_all(
        copies, ("segment", "db"), split_axis=0, concat_axis=0, tiled=True, axis_index_groups=groups
    )


def on_device(stream, gain, key_weight, value_weight, owners, blocks, valid, database):
    core = lax.axis_index("segment") % 2
    place = lax.axis_index("db")
    rows = stream[0]
    tokens, local_width = rows.shape
    full_width = local_width * lax.axis_size("mp")

    def pack_weight(w):
        return jnp.pad(w[0], ((0, W_PAD - W_PART), (0, 0)))

    packed_w = jnp.concatenate([pack_weight(key_weight), pack_weight(value_weight)], axis=0)
    packed_w = packed_w.reshape(2 * W_PAD, HEADS_HERE, HD).transpose(1, 0, 2).reshape(W_ROWS, HD)

    half = lax.dynamic_slice(database, (0, core * HALF, 0), (2 * PAIRS, HALF, ENC))
    paired = jnp.concatenate([half[0::2], half[1::2]], axis=2)
    packed_d = paired.reshape(PAIRS, HALF, TILES, HD).transpose(0, 2, 1, 3).reshape(D_ROWS, HD)

    as_float = rows.astype(jnp.float32)
    squares = jnp.sum(as_float * as_float, axis=1)
    requests = (owners[0] * 6 + blocks[0]).reshape(-1)
    info = jnp.concatenate(
        [squares, gain[0], valid[0].reshape(-1).astype(jnp.float32), requests.astype(jnp.float32)]
    )
    info = jnp.pad(info, (0, -info.shape[0] % 1024)).reshape(-1, HD)
    info_here = to_next(info).reshape(-1)
    requests_other = to_next_other_core(requests)
    x_here = to_next(rows)

    line_d = first_ring(packed_d)
    pieces_w = [to_next_turned(packed_w, turn) for turn in (0, -1, 2, 1)]
    spread = spread_of(core, place)
    pieces_w, line_d, info_here, requests_other, spread = lax.optimization_barrier(
        (pieces_w, line_d, info_here, requests_other, spread)
    )
    all_w = lax.all_gather(
        jnp.concatenate(pieces_w, axis=0),
        ("segment", "db"),
        axis=0,
        tiled=True,
        axis_index_groups=ring_groups(lax.axis_size("segment"), 1),
    ).reshape(RING, W_ROWS, HD)
    d_before, d_after = turned(line_d, 1, 1), turned(line_d, -1, 1)
    mid_d = line_d.shape[0] // 2
    d_pieces = (line_d, d_after, turned(d_before[:mid_d], 1, 1), turned(d_after[mid_d:], -1, 1), d_before)

    squares_here = info_here[:tokens]
    squares_other = other_mp(squares_here.reshape(-1, HD)).reshape(-1)
    gain_here = info_here[tokens:tokens + local_width]
    ints = info_here[tokens + local_width:tokens + local_width + 2 * REQ].astype(jnp.int32)
    live, requests_here = ints[:REQ], ints[REQ:]
    table = jnp.concatenate(
        [source_table(requests_here, core, place), source_table(requests_other, core, place)], axis=1
    )

    given, squares_other, x_here = lax.optimization_barrier((give(table, d_pieces), squares_other, x_here))
    slabs = other_core(given)
    own = pick(table, d_pieces, spread)
    inv_rms = lax.rsqrt((squares_here + squares_other) / full_width + eps_norm)
    updated = attend(live, table, own, slabs, spread, all_w, x_here, inv_rms[:, None], gain_here[None, :])
    return updated[None]


def solution(mesh):
    return jax.shard_map(
        on_device,
        mesh=mesh,
        in_specs=(
            P("segment", "db", "mp"),
            P("segment", "mp"),
            P("segment", "db", "mp"),
            P("segment", "db", "mp"),
            P("segment", "db", None),
            P("segment", "db", None),
            P("segment", "db", None),
            P("db", None, None),
        ),
        out_specs=P("segment", "db", "mp"),
        check_vma=False,
    )
```

time: 190 us -> 139 us (0.73)
  waiting for transfers between devices: 62.1 us -> 15.8 us
  Pallas kernels: 44.1 us -> 25.5 us
  starting transfers between devices: 55.6 us -> 64.3 us
  other arithmetic: 6.33 us -> 11.3 us
    ppermute x8 -> x4, waiting for transfers between devices: 48.6 us -> 14.5 us  [turned(): return lax.ppermute(value, ('segment', 'db'), pairs)]
    ppermute x1 -> x5, starting transfers between devices: 4.28 us -> 31.1 us  [the longest x4 17.8 us: to_next_turned(): return lax.ppermute(value, ('segment', 'db'), pairs)]
    pallas_call x1, Pallas kernels: 37.4 us -> 19.9 us  [attend(): pl.pallas_call(attend_kernel, grid_spec=pltpu.PrefetchScalarGridSpec(num_...]
    ppermute x8 -> x4, starting transfers between devices: 23.6 us -> 13 us  [turned(): return lax.ppermute(value, ('segment', 'db'), pairs)]
    ppermute x1 -> x5, waiting for transfers between devices: 9.33 us -> 0.01 us  [the longest x4 0.01 us: to_next_turned(): return lax.ppermute(value, ('segment', 'db'), pairs)]
    ppermute x1, starting transfers between devices: 14.6 us -> 6.63 us  [other_core(): return lax.ppermute(value, 'segment', [(s, s ^ 1) for s in range(count)])]
    ppermute x3 -> x2, starting transfers between devices: 10.8 us -> 6.27 us  [to_next(): lax.ppermute(value, 'segment', [(s, (s + 1) % count) for s in range(count)])]
    ppermute x3 -> x2, waiting for transfers between devices: 4.09 us -> 0.01 us  [to_next(): lax.ppermute(value, 'segment', [(s, (s + 1) % count) for s in range(count)])]
  transfers between devices with their start and end apart: 15 -> 15, of which waited for: 9 -> 3; matrix products, arithmetic and copies ran while one was open for 4% -> 10% of each run, Pallas kernels for 4% -> 4%
where the time goes in v2:
time: 139 us
  starting transfers between devices  64.3 us (46%)
  Pallas kernels  25.5 us (18%)
  waiting for transfers between devices  15.8 us (11%)
  between operations  13.9 us (10%)
  other arithmetic  11.3 us (8%)
  local copies, waits for them, and re-layouts  7.79 us (6%)
    pallas_call x1, Pallas kernels, attend(): pl.pallas_call(attend_kernel, grid_spec=pltpu.PrefetchScalarGridSpec(num_...  19.9 us
    ppermute x4, starting transfers between devices, to_next_turned(): return lax.ppermute(value, ('segment', 'db'), pairs)  17.8 us
    ppermute x4, waiting for transfers between devices, turned(): return lax.ppermute(value, ('segment', 'db'), pairs)  14.5 us
    ppermute x1, starting transfers between devices, other_mp(): return lax.ppermute(value, 'mp', [(0, 1), (1, 0)])  13.3 us
    ppermute x4, starting transfers between devices, turned(): return lax.ppermute(value, ('segment', 'db'), pairs)  13 us
    ppermute x1, starting transfers between devices, other_core(): return lax.ppermute(value, 'segment', [(s, s ^ 1) for s in range(count)])  6.63 us
    ppermute x2, starting transfers between devices, to_next(): lax.ppermute(value, 'segment', [(s, (s + 1) % count) for s in range(count)])  6.27 us
    all_to_all x1, starting transfers between devices, first_ring(): lax.all_to_all(copies, ('segment', 'db'), split_axis=0, concat_axis=0, ti...  3.68 us
  transfers between devices with their start and end apart: 15, of which 3 were waited for; matrix products, arithmetic and copies ran while one was open for 10% of the time, Pallas kernels for 4%

profile of v2, /device:TPU:1, one launch (start us, length us, event | category | flops | bytes accessed | tf_op | source)
XLA Modules:
  0.0 138.5 jit_solution(12524670176957421593)
XLA Ops:
  8.4 4.9 %collective-permute-start = (bf16[1024,128]{1,0:T(8,128)(2,1)}, bf16[1024,128]{1,0:T(8,128)(2,1)}, u32[]{:S(2)}, u32[]{:S(2)}) collective-permute-start(bf16[1024,128]{1,0:T(8,128)(2,1)} %bitcast.3), channel_id=1, source_target_pairs={{480,0},{482,2},{484,4},{486,6},{488,8},{490,10},{492,12},{494,14}... | collective-permute-start | bytes 786440 | tf_op jit(solution)/shard_map/ppermute | solution.py:63
  13.3 4.1 %collective-permute-start.1 = (bf16[1024,128]{1,0:T(8,128)(2,1)}, bf16[1024,128]{1,0:T(8,128)(2,1)}, u32[]{:S(2)}, u32[]{:S(2)}) collective-permute-start(bf16[1024,128]{1,0:T(8,128)(2,1)} %bitcast.3), channel_id=1, source_target_pairs={{480,24},{482,26},{484,28},{486,30},{488,0},{490,2},{492,4},{494,6... | collective-permute-start | bytes 786440 | tf_op jit(solution)/shard_map/ppermute | solution.py:63
  17.5 6.8 %collective-permute-start.2 = (bf16[1024,128]{1,0:T(8,128)(2,1)}, bf16[1024,128]{1,0:T(8,128)(2,1)}, u32[]{:S(2)}, u32[]{:S(2)}) collective-permute-start(bf16[1024,128]{1,0:T(8,128)(2,1)} %bitcast.3), channel_id=1, source_target_pairs={{480,16},{482,18},{484,20},{486,22},{488,24},{490,26},{492,28},{49... | collective-permute-start | bytes 786440 | tf_op jit(solution)/shard_map/ppermute | solution.py:63
  24.3 1.9 %collective-permute-start.3 = (bf16[1024,128]{1,0:T(8,128)(2,1)}, bf16[1024,128]{1,0:T(8,128)(2,1)}, u32[]{:S(2)}, u32[]{:S(2)}) collective-permute-start(bf16[1024,128]{1,0:T(8,128)(2,1)} %bitcast.3), channel_id=1, source_target_pairs={{480,8},{482,10},{484,12},{486,14},{488,16},{490,18},{492,20},{494... | collective-permute-start | bytes 786440 | tf_op jit(solution)/shard_map/ppermute | solution.py:63
  27.0 1.3 tile.9
  28.3 3.7 %all-to-all-start = ((bf16[4,1344,128]{2,1,0:T(8,128)(2,1)}), bf16[4,1344,128]{2,1,0:T(8,128)(2,1)S(1)}, u32[]{:S(2)}, u32[]{:S(2)}) async-start(bf16[4,1344,128]{2,1,0:T(8,128)(2,1)} %tile.9), calls=%async_computation | async-start | bytes 2752512 | tf_op jit(solution)/shard_map/all_to_all | solution.py:274
  32.2 3.5 %collective-permute-start.5 = (s32[12]{0:T(128)S(1)}, s32[12]{0:T(128)S(1)}, u32[]{:S(2)}, u32[]{:S(2)}) collective-permute-start(s32[12]{0:T(128)S(1)} %add.214), channel_id=1, source_target_pairs={{0,0},{32,96},{64,64},{96,160},{128,128},{160,224},{192,192},{224,... | collective-permute-start | bytes 152 | tf_op jit(solution)/shard_map/ppermute | solution.py:73
  36.1 3.6 %fusion.18 = (pred[1,512,512]{2,1,0:T(8,128)(4,1)S(1)}, pred[1,512,512]{2,1,0:T(8,128)(4,1)}) fusion(s32[512]{0:T(512)S(1)} %fusion.29, s32[512]{0:T(512)S(1)} %fusion.36, s32[512]{0:T(512)S(1)} %fusion.28, s32[512]{0:T(512)S(1)} %broadcast_add_fusion, s32[]{:T(128)S(6)} %select_n.324, pred[512]{0:T(512)(128)(4,1)S(1)} %compare_and_fusion, ...), kind=kLoop, calls=%fused_computation.43 | loop fusion | flops 21495808 | bytes 543749 | tf_op jit(solution)/shard_map/and | solution.py:255
  39.7 1.8 %multiply_reduce_fusion = f32[384]{0:T(512)S(1)} fusion(bf16[1,384,2048]{2,1,0:T(8,128)(2,1)} %param.8), kind=kLoop, calls=%fused_computation | loop fusion | flops 2358912 | bytes 1574400 | tf_op jit(solution)/shard_map/reduce_sum | solution.py:297
  41.8 1.3 collective-permute-done.5
  43.1 1.9 %collective-permute-start.4 = (f32[24,128]{1,0:T(8,128)S(1)}, f32[24,128]{1,0:T(8,128)S(1)}, u32[]{:S(2)}, u32[]{:S(2)}) collective-permute-start(f32[24,128]{1,0:T(8,128)S(1)} %pad_bitcast_fusion), channel_id=1, source_target_pairs={{0,32},{32,64},{64,96},{96,128},{128,160},{160,192},{192,224},{224... | collective-permute-start | bytes 36872 | tf_op jit(solution)/shard_map/ppermute | solution.py:68
  46.3 2.5 %pad_maximum_fusion = bf16[4096,128]{1,0:T(8,128)(2,1)} fusion(bf16[1024,128]{1,0:T(8,128)(2,1)} %collective-permute-done.3, bf16[1024,128]{1,0:T(8,128)(2,1)} %collective-permute-done.2, bf16[1024,128]{1,0:T(8,128)(2,1)} %collective-permute-done.1, bf16[1024,128]{1,0:T(8,128)(2,1)} %collective-permute-done), kind=kLoop, calls=%fused_computation.40 | loop fusion | flops 4194304 | bytes 2097152 | tf_op jit(solution)/shard_map/concatenate | solution.py:314
  48.8 2.2 %collective-permute-start.7 = (bf16[5376,128]{1,0:T(8,128)(2,1)S(1)}, bf16[5376,128]{1,0:T(8,128)(2,1)}, u32[]{:S(2)}, u32[]{:S(2)}) collective-permute-start(bf16[5376,128]{1,0:T(8,128)(2,1)S(1)} %bitcast.36), channel_id=1, source_target_pairs={{0,2},{2,4},{4,6},{6,0},{8,10},{10,12},{12,14},{14,8},{16,18},{18,... | collective-permute-start | bytes 4128776 | tf_op jit(solution)/shard_map/ppermute | solution.py:55
  51.1 4.3 %collective-permute-start.6 = (bf16[5376,128]{1,0:T(8,128)(2,1)S(1)}, bf16[5376,128]{1,0:T(8,128)(2,1)}, u32[]{:S(2)}, u32[]{:S(2)}) collective-permute-start(bf16[5376,128]{1,0:T(8,128)(2,1)S(1)} %bitcast.37), channel_id=1, source_target_pairs={{0,6},{2,0},{4,2},{6,4},{8,14},{10,8},{12,10},{14,12},{16,22},{18,... | collective-permute-start | bytes 4128776 | tf_op jit(solution)/shard_map/ppermute | solution.py:55
  55.3 4.4 %collective-permute-start.11 = (bf16[384,2048]{1,0:T(8,128)(2,1)}, bf16[384,2048]{1,0:T(8,128)(2,1)}, u32[]{:S(2)}, u32[]{:S(2)}) collective-permute-start(bf16[384,2048]{1,0:T(8,128)(2,1)} %bitcast.42), channel_id=1, source_target_pairs={{0,32},{32,64},{64,96},{96,128},{128,160},{160,192},{192,224},{224... | collective-permute-start | bytes 4718600 | tf_op jit(solution)/shard_map/ppermute | solution.py:68
  59.7 13.3 %collective-permute-start.10 = (f32[3,128]{1,0:T(4,128)S(1)}, f32[3,128]{1,0:T(4,128)S(1)}, u32[]{:S(2)}, u32[]{:S(2)}) collective-permute-start(f32[3,128]{1,0:T(4,128)S(1)} %slice_bitcast_fusion), channel_id=1, source_target_pairs={{0,1},{1,0},{2,3},{3,2},{4,5},{5,4},{6,7},{7,6},{8,9},{9,8},{10,11... | collective-permute-start | bytes 4616 | tf_op jit(solution)/shard_map/ppermute | solution.py:77
  74.4 2.2 %collective-permute-start.8 = (bf16[2688,128]{1,0:T(8,128)(2,1)S(1)}, bf16[2688,128]{1,0:T(8,128)(2,1)S(1)}, u32[]{:S(2)}, u32[]{:S(2)}) collective-permute-start(bf16[2688,128]{1,0:T(8,128)(2,1)S(1)} %slice.47), channel_id=1, source_target_pairs={{0,2},{2,4},{4,6},{6,0},{8,10},{10,12},{12,14},{14,8},{16,18},{18,... | collective-permute-start | bytes 2064392 | tf_op jit(solution)/shard_map/ppermute | solution.py:55
  77.8 4.3 %collective-permute-start.9 = (bf16[2688,128]{1,0:T(8,128)(2,1)S(1)}, bf16[2688,128]{1,0:T(8,128)(2,1)S(1)}, u32[]{:S(2)}, u32[]{:S(2)}) collective-permute-start(bf16[2688,128]{1,0:T(8,128)(2,1)S(1)} %slice.48), channel_id=1, source_target_pairs={{0,6},{2,0},{4,2},{6,4},{8,14},{10,8},{12,10},{14,12},{16,22},{18,... | collective-permute-start | bytes 2064392 | tf_op jit(solution)/shard_map/ppermute | solution.py:55
  82.8 12.3 %collective-permute-done.8.ol_ref = bf16[2688,128]{1,0:T(8,128)(2,1)S(1)} collective-permute-done((bf16[2688,128]{1,0:T(8,128)(2,1)S(1)}, bf16[2688,128]{1,0:T(8,128)(2,1)S(1)}, u32[]{:S(2)}, u32[]{:S(2)}) %collective-permute-start.8) | collective-permute-done | bytes 688160 | tf_op jit(solution)/shard_map/ppermute | solution.py:55
  95.1 2.2 %collective-permute-done.9.or_ref = bf16[2688,128]{1,0:T(8,128)(2,1)S(1)} collective-permute-done((bf16[2688,128]{1,0:T(8,128)(2,1)S(1)}, bf16[2688,128]{1,0:T(8,128)(2,1)S(1)}, u32[]{:S(2)}, u32[]{:S(2)}) %collective-permute-start.9) | collective-permute-done | bytes 688160 | tf_op jit(solution)/shard_map/ppermute | solution.py:55
  97.2 2.4 %give_encodings.1 = bf16[12,256,128]{2,1,0:T(8,128)(2,1)S(1)} custom-call(s32[3,24]{1,0:T(4,128)S(1)} %add_add_fusion.table, bf16[5376,128]{1,0:T(8,128)(2,1)S(1)} %bitcast.38, bf16[5376,128]{1,0:T(8,128)(2,1)} %collective-permute-done.6.r_ref, bf16[2688,128]{1,0:T(8,128)(2,1)S(1)} %collective-permute-done.8.ol_ref, ...), custom_call_target="tpu_custom_call" | custom-call | tf_op jit(solution)/shard_map/give_encodings/pallas_call | solution.py:135
  99.6 6.6 %collective-permute-start.12 = (bf16[12,256,128]{2,1,0:T(8,128)(2,1)S(1)}, bf16[12,256,128]{2,1,0:T(8,128)(2,1)}, u32[]{:S(2)}, u32[]{:S(2)}) collective-permute-start(bf16[12,256,128]{2,1,0:T(8,128)(2,1)S(1)} %give_encodings.1), channel_id=1, source_target_pairs={{0,32},{32,0},{64,96},{96,64},{128,160},{160,128},{192,224},{224,1... | collective-permute-start | bytes 2359304 | tf_op jit(solution)/shard_map/ppermute | solution.py:82
  107.7 3.2 %pick_encodings.1.own_ref = bf16[768,512]{1,0:T(8,128)(2,1)S(1)} custom-call(s32[3,24]{1,0:T(4,128)S(1)} %add_add_fusion.table, bf16[5376,128]{1,0:T(8,128)(2,1)S(1)} %bitcast.39, bf16[5376,128]{1,0:T(8,128)(2,1)} %collective-permute-done.6.r_ref, bf16[2688,128]{1,0:T(8,128)(2,1)S(1)} %collective-permute-done.8.ol_ref, ...), custom_call_target="tpu_custom_call" | custom-call | tf_op jit(solution)/shard_map/pick_encodings/pallas_call | solution.py:147
  111.8 19.9 %attend_heads.1 = bf16[384,2048]{1,0:T(8,128)(2,1)} custom-call(s32[12]{0:T(128)} %get-tuple-element.38.live, s32[3,24]{1,0:T(4,128)} %copy-done.3, bf16[768,512]{1,0:T(8,128)(2,1)} %copy-done.2, bf16[12,256,128]{2,1,0:T(8,128)(2,1)} %collective-permute-done.12.slabs, bf16[2,512,512]{2,1,0:T(8,128)(2,1)} %copy-done.1, bf16[16,1024,128]{2,1,0:T(8,128)(2,1)} %bitcast.40, ...), custom_call_target="tpu_custom_call" | custom-call | tf_op jit(solution)/shard_map/attend_heads/pallas_call | solution.py:218
  (73 shorter events, 9.9 us)
Async XLA Ops:
  6.5 19.7 %copy-start = (bf16[6,128,448]{1,2,0:T(8,128)(2,1)S(1)}, bf16[6,128,448]{1,2,0:T(8,128)(2,1)}, u32[]{:S(2)}) copy-start(bf16[6,128,448]{1,2,0:T(8,128)(2,1)} %param.15) | copy-start | bytes 2064388
  8.4 37.8 %collective-permute-start = (bf16[1024,128]{1,0:T(8,128)(2,1)}, bf16[1024,128]{1,0:T(8,128)(2,1)}, u32[]{:S(2)}, u32[]{:S(2)}) collective-permute-start(bf16[1024,128]{1,0:T(8,128)(2,1)} %bitcast.3), channel_id=1, source_target_pairs={{480,0},{482,2},{484,4},{486,6},{488,8},{490,10},{492,12},{494,14}... | collective-permute-start | bytes 786440 | tf_op jit(solution)/shard_map/ppermute | solution.py:63
  13.3 32.9 %collective-permute-start.1 = (bf16[1024,128]{1,0:T(8,128)(2,1)}, bf16[1024,128]{1,0:T(8,128)(2,1)}, u32[]{:S(2)}, u32[]{:S(2)}) collective-permute-start(bf16[1024,128]{1,0:T(8,128)(2,1)} %bitcast.3), channel_id=1, source_target_pairs={{480,24},{482,26},{484,28},{486,30},{488,0},{490,2},{492,4},{494,6... | collective-permute-start | bytes 786440 | tf_op jit(solution)/shard_map/ppermute | solution.py:63
  17.5 28.8 %collective-permute-start.2 = (bf16[1024,128]{1,0:T(8,128)(2,1)}, bf16[1024,128]{1,0:T(8,128)(2,1)}, u32[]{:S(2)}, u32[]{:S(2)}) collective-permute-start(bf16[1024,128]{1,0:T(8,128)(2,1)} %bitcast.3), channel_id=1, source_target_pairs={{480,16},{482,18},{484,20},{486,22},{488,24},{490,26},{492,28},{49... | collective-permute-start | bytes 786440 | tf_op jit(solution)/shard_map/ppermute | solution.py:63
  24.3 21.9 %collective-permute-start.3 = (bf16[1024,128]{1,0:T(8,128)(2,1)}, bf16[1024,128]{1,0:T(8,128)(2,1)}, u32[]{:S(2)}, u32[]{:S(2)}) collective-permute-start(bf16[1024,128]{1,0:T(8,128)(2,1)} %bitcast.3), channel_id=1, source_target_pairs={{480,8},{482,10},{484,12},{486,14},{488,16},{490,18},{492,20},{494... | collective-permute-start | bytes 786440 | tf_op jit(solution)/shard_map/ppermute | solution.py:63
  28.3 3.8 %copy-start.5 = (s32[1,6,2]{1,2,0:T(2,128)S(1)}, s32[1,6,2]{1,2,0:T(2,128)}, u32[]{:S(2)}) copy-start(s32[1,6,2]{1,2,0:T(2,128)} %param.13) | copy-start | bytes 148
  28.3 3.8 %copy-start.6 = (s32[1,6,2]{1,2,0:T(2,128)S(1)}, s32[1,6,2]{1,2,0:T(2,128)}, u32[]{:S(2)}) copy-start(s32[1,6,2]{1,2,0:T(2,128)} %param.12) | copy-start | bytes 148
  28.3 18.0 %all-to-all-start = ((bf16[4,1344,128]{2,1,0:T(8,128)(2,1)}), bf16[4,1344,128]{2,1,0:T(8,128)(2,1)S(1)}, u32[]{:S(2)}, u32[]{:S(2)}) async-start(bf16[4,1344,128]{2,1,0:T(8,128)(2,1)} %tile.9), calls=%async_computation | async-start | bytes 2752512 | tf_op jit(solution)/shard_map/all_to_all | solution.py:274
  32.0 9.5 %copy-start.7 = (s32[1,6,2]{1,2,0:T(2,128)S(1)}, s32[1,6,2]{1,2,0:T(2,128)}, u32[]{:S(2)}) copy-start(s32[1,6,2]{1,2,0:T(2,128)} %param.14) | copy-start | bytes 148
  32.0 9.7 %copy-start.4 = (f32[1,2048]{1,0:T(1,128)S(1)}, f32[1,2048]{1,0:T(1,128)}, u32[]{:S(2)}) copy-start(f32[1,2048]{1,0:T(1,128)} %param.9) | copy-start | bytes 24580
  32.0 79.8 %all-gather.2.cloned.1.call-start = ((), (), s32[]{:S(2)}) async-start(), calls=%async_computation.1 | async-start | bytes 5242880 | tf_op jit(solution)/shard_map/all_gather | solution.py:313
  32.2 10.9 %collective-permute-start.5 = (s32[12]{0:T(128)S(1)}, s32[12]{0:T(128)S(1)}, u32[]{:S(2)}, u32[]{:S(2)}) collective-permute-start(s32[12]{0:T(128)S(1)} %add.214), channel_id=1, source_target_pairs={{0,0},{32,96},{64,64},{96,160},{128,128},{160,224},{192,192},{224,... | collective-permute-start | bytes 152 | tf_op jit(solution)/shard_map/ppermute | solution.py:73
  43.1 3.1 %collective-permute-start.4 = (f32[24,128]{1,0:T(8,128)S(1)}, f32[24,128]{1,0:T(8,128)S(1)}, u32[]{:S(2)}, u32[]{:S(2)}) collective-permute-start(f32[24,128]{1,0:T(8,128)S(1)} %pad_bitcast_fusion), channel_id=1, source_target_pairs={{0,32},{32,64},{64,96},{96,128},{128,160},{160,192},{192,224},{224... | collective-permute-start | bytes 36872 | tf_op jit(solution)/shard_map/ppermute | solution.py:68
  46.2 61.5 %copy-start.1 = (bf16[2,512,512]{2,1,0:T(8,128)(2,1)}, bf16[2,512,512]{2,1,0:T(8,128)(2,1)S(1)}, u32[]{:S(2)}) copy-start(bf16[2,512,512]{2,1,0:T(8,128)(2,1)S(1)} %add_convert_fusion.spread) | copy-start | bytes 3145732
  48.8 24.4 %collective-permute-start.7 = (bf16[5376,128]{1,0:T(8,128)(2,1)S(1)}, bf16[5376,128]{1,0:T(8,128)(2,1)}, u32[]{:S(2)}, u32[]{:S(2)}) collective-permute-start(bf16[5376,128]{1,0:T(8,128)(2,1)S(1)} %bitcast.36), channel_id=1, source_target_pairs={{0,2},{2,4},{4,6},{6,0},{8,10},{10,12},{12,14},{14,8},{16,18},{18,... | collective-permute-start | bytes 4128776 | tf_op jit(solution)/shard_map/ppermute | solution.py:55
  51.1 25.6 %collective-permute-start.6 = (bf16[5376,128]{1,0:T(8,128)(2,1)S(1)}, bf16[5376,128]{1,0:T(8,128)(2,1)}, u32[]{:S(2)}, u32[]{:S(2)}) collective-permute-start(bf16[5376,128]{1,0:T(8,128)(2,1)S(1)} %bitcast.37), channel_id=1, source_target_pairs={{0,6},{2,0},{4,2},{6,4},{8,14},{10,8},{12,10},{14,12},{16,22},{18,... | collective-permute-start | bytes 4128776 | tf_op jit(solution)/shard_map/ppermute | solution.py:55
  55.3 44.3 %collective-permute-start.11 = (bf16[384,2048]{1,0:T(8,128)(2,1)}, bf16[384,2048]{1,0:T(8,128)(2,1)}, u32[]{:S(2)}, u32[]{:S(2)}) collective-permute-start(bf16[384,2048]{1,0:T(8,128)(2,1)} %bitcast.42), channel_id=1, source_target_pairs={{0,32},{32,64},{64,96},{96,128},{128,160},{160,192},{192,224},{224... | collective-permute-start | bytes 4718600 | tf_op jit(solution)/shard_map/ppermute | solution.py:68
  59.7 39.9 %collective-permute-start.10 = (f32[3,128]{1,0:T(4,128)S(1)}, f32[3,128]{1,0:T(4,128)S(1)}, u32[]{:S(2)}, u32[]{:S(2)}) collective-permute-start(f32[3,128]{1,0:T(4,128)S(1)} %slice_bitcast_fusion), channel_id=1, source_target_pairs={{0,1},{1,0},{2,3},{3,2},{4,5},{5,4},{6,7},{7,6},{8,9},{9,8},{10,11... | collective-permute-start | bytes 4616 | tf_op jit(solution)/shard_map/ppermute | solution.py:77
  74.4 20.6 %collective-permute-start.8 = (bf16[2688,128]{1,0:T(8,128)(2,1)S(1)}, bf16[2688,128]{1,0:T(8,128)(2,1)S(1)}, u32[]{:S(2)}, u32[]{:S(2)}) collective-permute-start(bf16[2688,128]{1,0:T(8,128)(2,1)S(1)} %slice.47), channel_id=1, source_target_pairs={{0,2},{2,4},{4,6},{6,0},{8,10},{10,12},{12,14},{14,8},{16,18},{18,... | collective-permute-start | bytes 2064392 | tf_op jit(solution)/shard_map/ppermute | solution.py:55
  77.8 19.4 %collective-permute-start.9 = (bf16[2688,128]{1,0:T(8,128)(2,1)S(1)}, bf16[2688,128]{1,0:T(8,128)(2,1)S(1)}, u32[]{:S(2)}, u32[]{:S(2)}) collective-permute-start(bf16[2688,128]{1,0:T(8,128)(2,1)S(1)} %slice.48), channel_id=1, source_target_pairs={{0,6},{2,0},{4,2},{6,4},{8,14},{10,8},{12,10},{14,12},{16,22},{18,... | collective-permute-start | bytes 2064392 | tf_op jit(solution)/shard_map/ppermute | solution.py:55
  82.8 24.9 %copy-start.3 = (s32[3,24]{1,0:T(4,128)}, s32[3,24]{1,0:T(4,128)S(1)}, u32[]{:S(2)}) copy-start(s32[3,24]{1,0:T(4,128)S(1)} %add_add_fusion.table) | copy-start | bytes 868
  99.6 12.2 %collective-permute-start.12 = (bf16[12,256,128]{2,1,0:T(8,128)(2,1)S(1)}, bf16[12,256,128]{2,1,0:T(8,128)(2,1)}, u32[]{:S(2)}, u32[]{:S(2)}) collective-permute-start(bf16[12,256,128]{2,1,0:T(8,128)(2,1)S(1)} %give_encodings.1), channel_id=1, source_target_pairs={{0,32},{32,0},{64,96},{96,64},{128,160},{160,128},{192,224},{224,1... | collective-permute-start | bytes 2359304 | tf_op jit(solution)/shard_map/ppermute | solution.py:82
  110.9 0.9 copy-start.2
Sparse Core Ops, SparseCore 0:
  49.0 53.5 all-gather.1

commit v3 on v2

--- a/solution.py
+++ b/solution.py
@@ -17,13 +17,14 @@
 W_ROWS = HEADS_HERE * 2 * W_PAD
 ENC = 448
 ENC_PAD = RING * W_PAD
+SHIFT = ENC_PAD - ENC
 HALF = 64
 TILES = 2 * ENC // HD
 PAIRS = 3
 D_ROWS = PAIRS * TILES * HALF
 SLAB = ENC_PAD // HD * HALF
 REQ = 12
-HB = 2
+HB = 4
 
 
 def ring_pairs(segments, turn, along_x_core):
@@ -107,8 +108,8 @@
         slab = slabs[i]
         rows.append(jnp.concatenate([slab[t * HALF:(t + 1) * HALF] for t in range(tiles)], axis=1))
     stacked = jnp.concatenate(rows, axis=0)
-    even = jnp.dot(stacked, spread[0], preferred_element_type=jnp.float32)
-    odd = jnp.dot(stacked, spread[1], preferred_element_type=jnp.float32)
+    even = jnp.dot(stacked, spread[SHIFT:], preferred_element_type=jnp.float32)
+    odd = jnp.dot(stacked, spread[:ENC_PAD], preferred_element_type=jnp.float32)
     placed = []
     for i in range(REQ):
         here = slice(i * HALF, (i + 1) * HALF)
@@ -223,7 +224,7 @@
             in_specs=[
                 whole(REQ * HALF, ENC_PAD),
                 whole(REQ, SLAB, HD),
-                whole(2, ENC_PAD, ENC_PAD),
+                whole(SHIFT + ENC_PAD, ENC_PAD),
                 pl.BlockSpec((RING, HB * 2 * W_PAD, HD), lambda i, live, table: (0, i, 0)),
                 pl.BlockSpec((tokens, HB * HD), lambda i, live, table: (0, i)),
                 whole(tokens, 1),
@@ -244,23 +245,21 @@
 
 
 def spread_of(core, here):
-    channel = lax.broadcasted_iota(jnp.int32, (ENC_PAD, ENC_PAD), 0)
-    column = lax.broadcasted_iota(jnp.int32, (ENC_PAD, ENC_PAD), 1)
-
-    def put(source):
-        near, far = ring_place(source // W_PART, core)
-        near = (near - ring_place(here, core)[0]) % SIDE
-        place = (far * SIDE + near) * W_PAD + source % W_PART
-        used = jnp.logical_and(source >= 0, source < ENC)
-        return jnp.logical_and(used, place == column).astype(jnp.bfloat16)
-
-    return jnp.stack([put(channel), put(channel - (ENC_PAD - ENC))])
+    channel = jnp.arange(SHIFT + ENC_PAD) - SHIFT
+    near, far = ring_place(channel // W_PART, core)
+    near = (near - ring_place(here, core)[0]) % SIDE
+    place = (far * SIDE + near) * W_PAD + channel % W_PART
+    used = jnp.logical_and(channel >= 0, channel < ENC)
+    place = lax.optimization_barrier(jnp.where(used, place, -1))
+    column = lax.broadcasted_iota(jnp.int32, (SHIFT + ENC_PAD, ENC_PAD), 1)
+    return (place[:, None] == column).astype(jnp.bfloat16)
 
 
 def source_table(requests, core, here):
     owner, block = requests // 6, requests % 6
     near, far = ring_place(owner, core)
-    far = (far - ring_place(here, core)[1]) % SIDE
+    near_here, far_here = ring_place(here, core)
+    near, far = (near - near_here) % SIDE, (far - far_here) % SIDE
     which = jnp.where(far < 2, far, jnp.where(far == 3, 4, jnp.where(near < 2, 2, 3)))
     chunk = jnp.where(which == 3, near - 2, near)
     odd = block % 2
@@ -268,12 +267,18 @@
     return jnp.stack([which, row, odd])
 
 
-def first_ring(piece):
-    groups = ring_groups(lax.axis_size("segment"), 0)
-    copies = jnp.tile(piece, (SIDE, 1))
-    return lax.all_to_all(
-        copies, ("segment", "db"), split_axis=0, concat_axis=0, tiled=True, axis_index_groups=groups
-    )
+def in_three(value):
+    parts = []
+    for _ in range(3):
+        part = lax.reduce_precision(value, 8, 7)
+        parts.append(part.astype(jnp.bfloat16))
+        value = value - part
+    return jnp.stack(parts)
+
+
+def from_three(parts):
+    high, mid, low = parts.astype(jnp.float32)
+    return high + (mid + low)
 
 
 def on_device(stream, gain, key_weight, value_weight, owners, blocks, valid, database):
@@ -299,17 +304,17 @@
     info = jnp.concatenate(
         [squares, gain[0], valid[0].reshape(-1).astype(jnp.float32), requests.astype(jnp.float32)]
     )
-    info = jnp.pad(info, (0, -info.shape[0] % 1024)).reshape(-1, HD)
-    info_here = to_next(info).reshape(-1)
+    info_rows = -(-info.shape[0] // HD)
+    info = jnp.pad(info, (0, info_rows * HD - info.shape[0]))
+    sent = in_three(info).reshape(3 * info_rows, HD)
+    sent = jnp.pad(sent, ((0, -sent.shape[0] % 16), (0, 0)))
     requests_other = to_next_other_core(requests)
     x_here = to_next(rows)
 
-    line_d = first_ring(packed_d)
-    pieces_w = [to_next_turned(packed_w, turn) for turn in (0, -1, 2, 1)]
-    spread = spread_of(core, place)
-    pieces_w, line_d, info_here, requests_other, spread = lax.optimization_barrier(
-        (pieces_w, line_d, info_here, requests_other, spread)
-    )
+    pieces_d = [packed_d] + [turned(packed_d, turn, 0) for turn in (-1, 2, 1)]
+    line_d = jnp.concatenate(pieces_d, axis=0)
+    next_w = to_next_turned(jnp.concatenate([packed_w, sent], axis=0), 0)
+    pieces_w = [next_w[:W_ROWS]] + [to_next_turned(packed_w, turn) for turn in (-1, 2, 1)]
     all_w = lax.all_gather(
         jnp.concatenate(pieces_w, axis=0),
         ("segment", "db"),
@@ -318,6 +323,9 @@
         axis_index_groups=ring_groups(lax.axis_size("segment"), 1),
     ).reshape(RING, W_ROWS, HD)
     d_before, d_after = turned(line_d, 1, 1), turned(line_d, -1, 1)
+    info_here = from_three(next_w[W_ROWS:W_ROWS + 3 * info_rows].reshape(3, info_rows * HD))
+    spread = spread_of(core, place)
+    d_before, d_after, spread, requests_other = lax.optimization_barrier((d_before, d_after, spread, requests_other))
     mid_d = line_d.shape[0] // 2
     d_pieces = (line_d, d_after, turned(d_before[:mid_d], 1, 1), turned(d_after[mid_d:], -1, 1), d_before)
 

time: 139 us -> 152 us (1.094)
  starting transfers between devices: 64.3 us -> 75.5 us
  waiting for transfers between devices: 15.8 us -> 23.7 us
  other arithmetic: 11.3 us -> 7.35 us
  local copies, waits for them, and re-layouts: 7.79 us -> 5.66 us
    ppermute x4 -> x7, starting transfers between devices: 13 us -> 24.2 us  [turned(): return lax.ppermute(value, ('segment', 'db'), pairs)]
    ppermute x1, starting transfers between devices: 6.63 us -> 14.8 us  [other_core(): return lax.ppermute(value, 'segment', [(s, s ^ 1) for s in range(count)])]
    ppermute x4 -> x7, waiting for transfers between devices: 14.5 us -> 19.3 us  [turned(): return lax.ppermute(value, ('segment', 'db'), pairs)]
    ppermute x4, waiting for transfers between devices: 0.01 us -> 4.39 us  [to_next_turned(): return lax.ppermute(value, ('segment', 'db'), pairs)]
    ppermute x2 -> x1, starting transfers between devices: 6.27 us -> 1.92 us  [to_next(): lax.ppermute(value, 'segment', [(s, (s + 1) % count) for s in range(count)])]
    and x6 -> x0, other arithmetic: 3.71 us -> none  [the longest x1 3.65 us: put(): return jnp.logical_and(used, place == column).astype(jnp.bfloat16)]
    all_to_all x1 -> x0, starting transfers between devices: 3.68 us -> none  [first_ring(): lax.all_to_all(copies, ('segment', 'db'), split_axis=0, concat_axis=0, ti...]
  transfers between devices with their start and end apart: 15 -> 16, of which waited for: 3 -> 7; matrix products, arithmetic and copies ran while one was open for 10% -> 3% of each run, Pallas kernels for 4% -> 4%
where the time goes in v3:
time: 152 us; the launch traced here: 151 us
  starting transfers between devices  75.5 us (50%)
  Pallas kernels  24.8 us (16%)
  waiting for transfers between devices  23.7 us (16%)
  between operations  13.8 us (9%)
  other arithmetic  7.35 us (5%)
  local copies, waits for them, and re-layouts  5.66 us (4%)
    ppermute x7, starting transfers between devices, turned(): return lax.ppermute(value, ('segment', 'db'), pairs)  24.2 us
    ppermute x7, waiting for transfers between devices, turned(): return lax.ppermute(value, ('segment', 'db'), pairs)  19.3 us
    pallas_call x1, Pallas kernels, attend(): pl.pallas_call(attend_kernel, grid_spec=pltpu.PrefetchScalarGridSpec(num_...  19.2 us
    ppermute x4, starting transfers between devices, to_next_turned(): return lax.ppermute(value, ('segment', 'db'), pairs)  17.7 us
    ppermute x1, starting transfers between devices, other_core(): return lax.ppermute(value, 'segment', [(s, s ^ 1) for s in range(count)])  14.8 us
    ppermute x1, starting transfers between devices, other_mp(): return lax.ppermute(value, 'mp', [(0, 1), (1, 0)])  13.6 us
    ppermute x4, waiting for transfers between devices, to_next_turned(): return lax.ppermute(value, ('segment', 'db'), pairs)  4.39 us
    ppermute x1, starting transfers between devices, to_next_other_core(): lax.ppermute(value, 'segment', [(s, (s + 1) % count ^ 1) for s in range(c...  3.25 us
  transfers between devices with their start and end apart: 16, of which 7 were waited for; matrix products, arithmetic and copies ran while one was open for 3% of the time, Pallas kernels for 4%

profile of v3, /device:TPU:1, one launch (start us, length us, event | category | flops | bytes accessed | tf_op | source)
XLA Modules:
  0.0 150.9 jit_solution(17502056685371271220)
XLA Ops:
  6.5 1.9 %multiply_reduce_fusion = f32[384]{0:T(512)S(1)} fusion(bf16[1,384,2048]{2,1,0:T(8,128)(2,1)} %param.8), kind=kLoop, calls=%fused_computation | loop fusion | flops 2358912 | bytes 1574400 | tf_op jit(solution)/shard_map/reduce_sum | solution.py:302
  12.2 4.9 %collective-permute-start = (bf16[1088,128]{1,0:T(8,128)(2,1)S(1)}, bf16[1088,128]{1,0:T(8,128)(2,1)S(1)}, u32[]{:S(2)}, u32[]{:S(2)}) collective-permute-start(bf16[1088,128]{1,0:T(8,128)(2,1)S(1)} %fusion.4), channel_id=1, source_target_pairs={{480,0},{482,2},{484,4},{486,6},{488,8},{490,10},{492,12},{494,14}... | collective-permute-start | bytes 835592 | tf_op jit(solution)/shard_map/ppermute | solution.py:64
  17.1 2.8 %collective-permute-start.14 = (bf16[1024,128]{1,0:T(8,128)(2,1)S(1)}, bf16[1024,128]{1,0:T(8,128)(2,1)S(1)}, u32[]{:S(2)}, u32[]{:S(2)}) collective-permute-start(bf16[1024,128]{1,0:T(8,128)(2,1)S(1)} %bitcast.46), channel_id=1, source_target_pairs={{480,8},{482,10},{484,12},{486,14},{488,16},{490,18},{492,20},{494... | collective-permute-start | bytes 786440 | tf_op jit(solution)/shard_map/ppermute | solution.py:64
  20.0 6.6 %collective-permute-start.13 = (bf16[1024,128]{1,0:T(8,128)(2,1)S(1)}, bf16[1024,128]{1,0:T(8,128)(2,1)S(1)}, u32[]{:S(2)}, u32[]{:S(2)}) collective-permute-start(bf16[1024,128]{1,0:T(8,128)(2,1)S(1)} %bitcast.47), channel_id=1, source_target_pairs={{480,16},{482,18},{484,20},{486,22},{488,24},{490,26},{492,28},{49... | collective-permute-start | bytes 786440 | tf_op jit(solution)/shard_map/ppermute | solution.py:64
  26.6 3.3 %collective-permute-start.12 = (bf16[1024,128]{1,0:T(8,128)(2,1)S(1)}, bf16[1024,128]{1,0:T(8,128)(2,1)S(1)}, u32[]{:S(2)}, u32[]{:S(2)}) collective-permute-start(bf16[1024,128]{1,0:T(8,128)(2,1)S(1)} %bitcast.48), channel_id=1, source_target_pairs={{480,24},{482,26},{484,28},{486,30},{488,0},{490,2},{492,4},{494,6... | collective-permute-start | bytes 786440 | tf_op jit(solution)/shard_map/ppermute | solution.py:64
  30.6 4.0 %collective-permute-done.12 = bf16[1024,128]{1,0:T(8,128)(2,1)S(1)} collective-permute-done((bf16[1024,128]{1,0:T(8,128)(2,1)S(1)}, bf16[1024,128]{1,0:T(8,128)(2,1)S(1)}, u32[]{:S(2)}, u32[]{:S(2)}) %collective-permute-start.12) | collective-permute-done | bytes 262176 | tf_op jit(solution)/shard_map/ppermute | solution.py:64
  36.5 3.2 %collective-permute-start.3 = (bf16[1344,128]{1,0:T(8,128)(2,1)S(1)}, bf16[1344,128]{1,0:T(8,128)(2,1)S(1)}, u32[]{:S(2)}, u32[]{:S(2)}) collective-permute-start(bf16[1344,128]{1,0:T(8,128)(2,1)S(1)} %bitcast.41), channel_id=1, source_target_pairs={{0,8},{2,10},{4,12},{6,14},{8,16},{10,18},{12,20},{14,22},{16,24},... | collective-permute-start | bytes 1032200 | tf_op jit(solution)/shard_map/ppermute | solution.py:56
  39.7 4.4 %collective-permute-start.2 = (bf16[1344,128]{1,0:T(8,128)(2,1)S(1)}, bf16[1344,128]{1,0:T(8,128)(2,1)S(1)}, u32[]{:S(2)}, u32[]{:S(2)}) collective-permute-start(bf16[1344,128]{1,0:T(8,128)(2,1)S(1)} %bitcast.42), channel_id=1, source_target_pairs={{0,16},{2,18},{4,20},{6,22},{8,24},{10,26},{12,28},{14,30},{16,0},... | collective-permute-start | bytes 1032200 | tf_op jit(solution)/shard_map/ppermute | solution.py:56
  44.1 2.8 %collective-permute-start.1 = (bf16[1344,128]{1,0:T(8,128)(2,1)S(1)}, bf16[1344,128]{1,0:T(8,128)(2,1)S(1)}, u32[]{:S(2)}, u32[]{:S(2)}) collective-permute-start(bf16[1344,128]{1,0:T(8,128)(2,1)S(1)} %bitcast.43), channel_id=1, source_target_pairs={{0,24},{2,26},{4,28},{6,30},{8,0},{10,2},{12,4},{14,6},{16,8},{18,... | collective-permute-start | bytes 1032200 | tf_op jit(solution)/shard_map/ppermute | solution.py:56
  46.9 3.3 %collective-permute-start.6 = (s32[12]{0:T(128)S(1)}, s32[12]{0:T(128)S(1)}, u32[]{:S(2)}, u32[]{:S(2)}) collective-permute-start(s32[12]{0:T(128)S(1)} %add.140), channel_id=1, source_target_pairs={{0,0},{32,96},{64,64},{96,160},{128,128},{160,224},{192,192},{224,... | collective-permute-start | bytes 152 | tf_op jit(solution)/shard_map/ppermute | solution.py:74
  50.2 1.9 %collective-permute-start.10 = (bf16[384,2048]{1,0:T(8,128)(2,1)}, bf16[384,2048]{1,0:T(8,128)(2,1)}, u32[]{:S(2)}, u32[]{:S(2)}) collective-permute-start(bf16[384,2048]{1,0:T(8,128)(2,1)} %bitcast.4), channel_id=1, source_target_pairs={{0,32},{32,64},{64,96},{96,128},{128,160},{160,192},{192,224},{224... | collective-permute-start | bytes 4718600 | tf_op jit(solution)/shard_map/ppermute | solution.py:69
  52.5 2.0 %collective-permute-start.4 = (bf16[5376,128]{1,0:T(8,128)(2,1)S(1)}, bf16[5376,128]{1,0:T(8,128)(2,1)S(1)}, u32[]{:S(2)}, u32[]{:S(2)}) collective-permute-start(bf16[5376,128]{1,0:T(8,128)(2,1)S(1)} %pad_maximum_fusion.c_ref), channel_id=1, source_target_pairs={{0,2},{2,4},{4,6},{6,0},{8,10},{10,12},{12,14},{14,8},{16,18},{18,... | collective-permute-start | bytes 4128776 | tf_op jit(solution)/shard_map/ppermute | solution.py:56
  54.5 4.5 %collective-permute-start.5 = (bf16[5376,128]{1,0:T(8,128)(2,1)S(1)}, bf16[5376,128]{1,0:T(8,128)(2,1)}, u32[]{:S(2)}, u32[]{:S(2)}) collective-permute-start(bf16[5376,128]{1,0:T(8,128)(2,1)S(1)} %pad_maximum_fusion.c_ref), channel_id=1, source_target_pairs={{0,6},{2,0},{4,2},{6,4},{8,14},{10,8},{12,10},{14,12},{16,22},{18,... | collective-permute-start | bytes 4128776 | tf_op jit(solution)/shard_map/ppermute | solution.py:56
  60.0 13.6 %collective-permute-start.9 = (f32[3,128]{1,0:T(4,128)S(1)}, f32[3,128]{1,0:T(4,128)S(1)}, u32[]{:S(2)}, u32[]{:S(2)}) collective-permute-start(f32[3,128]{1,0:T(4,128)S(1)} %slice.55), channel_id=1, source_target_pairs={{0,1},{1,0},{2,3},{3,2},{4,5},{5,4},{6,7},{7,6},{8,9},{9,8},{10,11... | collective-permute-start | bytes 4616 | tf_op jit(solution)/shard_map/ppermute | solution.py:78
  73.8 7.1 %collective-permute-done.4.l_ref = bf16[5376,128]{1,0:T(8,128)(2,1)S(1)} collective-permute-done((bf16[5376,128]{1,0:T(8,128)(2,1)S(1)}, bf16[5376,128]{1,0:T(8,128)(2,1)S(1)}, u32[]{:S(2)}, u32[]{:S(2)}) %collective-permute-start.4) | collective-permute-done | bytes 1376288 | tf_op jit(solution)/shard_map/ppermute | solution.py:56
  80.8 4.5 %collective-permute-done.5.r_ref = bf16[5376,128]{1,0:T(8,128)(2,1)} collective-permute-done((bf16[5376,128]{1,0:T(8,128)(2,1)S(1)}, bf16[5376,128]{1,0:T(8,128)(2,1)}, u32[]{:S(2)}, u32[]{:S(2)}) %collective-permute-start.5) | collective-permute-done | bytes 1376288 | tf_op jit(solution)/shard_map/ppermute | solution.py:56
  85.3 3.9 %collective-permute-start.7 = (bf16[2688,128]{1,0:T(8,128)(2,1)S(1)}, bf16[2688,128]{1,0:T(8,128)(2,1)S(1)}, u32[]{:S(2)}, u32[]{:S(2)}) collective-permute-start(bf16[2688,128]{1,0:T(8,128)(2,1)S(1)} %slice.47), channel_id=1, source_target_pairs={{0,2},{2,4},{4,6},{6,0},{8,10},{10,12},{12,14},{14,8},{16,18},{18,... | collective-permute-start | bytes 2064392 | tf_op jit(solution)/shard_map/ppermute | solution.py:56
  90.4 3.4 %collective-permute-start.8 = (bf16[2688,128]{1,0:T(8,128)(2,1)S(1)}, bf16[2688,128]{1,0:T(8,128)(2,1)S(1)}, u32[]{:S(2)}, u32[]{:S(2)}) collective-permute-start(bf16[2688,128]{1,0:T(8,128)(2,1)S(1)} %slice.48), channel_id=1, source_target_pairs={{0,6},{2,0},{4,2},{6,4},{8,14},{10,8},{12,10},{14,12},{16,22},{18,... | collective-permute-start | bytes 2064392 | tf_op jit(solution)/shard_map/ppermute | solution.py:56
  94.5 4.5 %collective-permute-done.7.ol_ref = bf16[2688,128]{1,0:T(8,128)(2,1)S(1)} collective-permute-done((bf16[2688,128]{1,0:T(8,128)(2,1)S(1)}, bf16[2688,128]{1,0:T(8,128)(2,1)S(1)}, u32[]{:S(2)}, u32[]{:S(2)}) %collective-permute-start.7) | collective-permute-done | bytes 688160 | tf_op jit(solution)/shard_map/ppermute | solution.py:56
  99.0 3.0 %collective-permute-done.8.or_ref = bf16[2688,128]{1,0:T(8,128)(2,1)S(1)} collective-permute-done((bf16[2688,128]{1,0:T(8,128)(2,1)S(1)}, bf16[2688,128]{1,0:T(8,128)(2,1)S(1)}, u32[]{:S(2)}, u32[]{:S(2)}) %collective-permute-start.8) | collective-permute-done | bytes 688160 | tf_op jit(solution)/shard_map/ppermute | solution.py:56
  102.0 2.6 %give_encodings.1 = bf16[12,256,128]{2,1,0:T(8,128)(2,1)S(1)} custom-call(s32[3,24]{1,0:T(4,128)S(1)} %add_add_fusion.table, bf16[5376,128]{1,0:T(8,128)(2,1)S(1)} %pad_maximum_fusion.c_ref, bf16[5376,128]{1,0:T(8,128)(2,1)} %collective-permute-done.5.r_ref, bf16[2688,128]{1,0:T(8,128)(2,1)S(1)} %collective-permute-done.7.ol_ref, ...), custom_call_target="tpu_custom_call" | custom-call | tf_op jit(solution)/shard_map/give_encodings/pallas_call | solution.py:136
  104.6 14.8 %collective-permute-start.11 = (bf16[12,256,128]{2,1,0:T(8,128)(2,1)S(1)}, bf16[12,256,128]{2,1,0:T(8,128)(2,1)}, u32[]{:S(2)}, u32[]{:S(2)}) collective-permute-start(bf16[12,256,128]{2,1,0:T(8,128)(2,1)S(1)} %give_encodings.1), channel_id=1, source_target_pairs={{0,32},{32,0},{64,96},{96,64},{128,160},{160,128},{192,224},{224,1... | collective-permute-start | bytes 2359304 | tf_op jit(solution)/shard_map/ppermute | solution.py:83
  120.9 3.0 %pick_encodings.1.own_ref = bf16[768,512]{1,0:T(8,128)(2,1)S(1)} custom-call(s32[3,24]{1,0:T(4,128)S(1)} %add_add_fusion.table, bf16[5376,128]{1,0:T(8,128)(2,1)S(1)} %pad_maximum_fusion.c_ref, bf16[5376,128]{1,0:T(8,128)(2,1)} %collective-permute-done.5.r_ref, bf16[2688,128]{1,0:T(8,128)(2,1)S(1)} %collective-permute-done.7.ol_ref, ...), custom_call_target="tpu_custom_call" | custom-call | tf_op jit(solution)/shard_map/pick_encodings/pallas_call | solution.py:148
  124.8 19.2 %attend_heads.1 = bf16[384,2048]{1,0:T(8,128)(2,1)} custom-call(s32[12]{0:T(128)} %get-tuple-element.35.live, s32[3,24]{1,0:T(4,128)} %copy-done.3, bf16[768,512]{1,0:T(8,128)(2,1)} %copy-done.2, bf16[12,256,128]{2,1,0:T(8,128)(2,1)} %collective-permute-done.11.slabs, bf16[576,512]{1,0:T(8,128)(2,1)} %copy-done.1, bf16[16,1024,128]{2,1,0:T(8,128)(2,1)} %bitcast.39, ...), custom_call_target="tpu_custom_call" | custom-call | tf_op jit(solution)/shard_map/attend_heads/pallas_call | solution.py:219
  (65 shorter events, 11.8 us)
Async XLA Ops:
  6.5 29.2 %copy-start = (bf16[6,128,448]{1,2,0:T(8,128)(2,1)S(1)}, bf16[6,128,448]{1,2,0:T(8,128)(2,1)}, u32[]{:S(2)}) copy-start(bf16[6,128,448]{1,2,0:T(8,128)(2,1)} %param.15) | copy-start | bytes 2064388
  6.5 118.3 %all-gather.2.cloned.1.call-start = ((), (), s32[]{:S(2)}) async-start(), calls=%async_computation | async-start | bytes 5242880 | tf_op jit(solution)/shard_map/all_gather | solution.py:318
  12.2 17.7 %collective-permute-start = (bf16[1088,128]{1,0:T(8,128)(2,1)S(1)}, bf16[1088,128]{1,0:T(8,128)(2,1)S(1)}, u32[]{:S(2)}, u32[]{:S(2)}) collective-permute-start(bf16[1088,128]{1,0:T(8,128)(2,1)S(1)} %fusion.4), channel_id=1, source_target_pairs={{480,0},{482,2},{484,4},{486,6},{488,8},{490,10},{492,12},{494,14}... | collective-permute-start | bytes 835592 | tf_op jit(solution)/shard_map/ppermute | solution.py:64
  17.1 12.8 %collective-permute-start.14 = (bf16[1024,128]{1,0:T(8,128)(2,1)S(1)}, bf16[1024,128]{1,0:T(8,128)(2,1)S(1)}, u32[]{:S(2)}, u32[]{:S(2)}) collective-permute-start(bf16[1024,128]{1,0:T(8,128)(2,1)S(1)} %bitcast.46), channel_id=1, source_target_pairs={{480,8},{482,10},{484,12},{486,14},{488,16},{490,18},{492,20},{494... | collective-permute-start | bytes 786440 | tf_op jit(solution)/shard_map/ppermute | solution.py:64
  20.0 10.4 %collective-permute-start.13 = (bf16[1024,128]{1,0:T(8,128)(2,1)S(1)}, bf16[1024,128]{1,0:T(8,128)(2,1)S(1)}, u32[]{:S(2)}, u32[]{:S(2)}) collective-permute-start(bf16[1024,128]{1,0:T(8,128)(2,1)S(1)} %bitcast.47), channel_id=1, source_target_pairs={{480,16},{482,18},{484,20},{486,22},{488,24},{490,26},{492,28},{49... | collective-permute-start | bytes 786440 | tf_op jit(solution)/shard_map/ppermute | solution.py:64
  26.6 8.0 %collective-permute-start.12 = (bf16[1024,128]{1,0:T(8,128)(2,1)S(1)}, bf16[1024,128]{1,0:T(8,128)(2,1)S(1)}, u32[]{:S(2)}, u32[]{:S(2)}) collective-permute-start(bf16[1024,128]{1,0:T(8,128)(2,1)S(1)} %bitcast.48), channel_id=1, source_target_pairs={{480,24},{482,26},{484,28},{486,30},{488,0},{490,2},{492,4},{494,6... | collective-permute-start | bytes 786440 | tf_op jit(solution)/shard_map/ppermute | solution.py:64
  29.9 0.7 copy-start.4
  36.5 15.7 %collective-permute-start.3 = (bf16[1344,128]{1,0:T(8,128)(2,1)S(1)}, bf16[1344,128]{1,0:T(8,128)(2,1)S(1)}, u32[]{:S(2)}, u32[]{:S(2)}) collective-permute-start(bf16[1344,128]{1,0:T(8,128)(2,1)S(1)} %bitcast.41), channel_id=1, source_target_pairs={{0,8},{2,10},{4,12},{6,14},{8,16},{10,18},{12,20},{14,22},{16,24},... | collective-permute-start | bytes 1032200 | tf_op jit(solution)/shard_map/ppermute | solution.py:56
  39.7 12.5 %collective-permute-start.2 = (bf16[1344,128]{1,0:T(8,128)(2,1)S(1)}, bf16[1344,128]{1,0:T(8,128)(2,1)S(1)}, u32[]{:S(2)}, u32[]{:S(2)}) collective-permute-start(bf16[1344,128]{1,0:T(8,128)(2,1)S(1)} %bitcast.42), channel_id=1, source_target_pairs={{0,16},{2,18},{4,20},{6,22},{8,24},{10,26},{12,28},{14,30},{16,0},... | collective-permute-start | bytes 1032200 | tf_op jit(solution)/shard_map/ppermute | solution.py:56
  44.1 8.3 %collective-permute-start.1 = (bf16[1344,128]{1,0:T(8,128)(2,1)S(1)}, bf16[1344,128]{1,0:T(8,128)(2,1)S(1)}, u32[]{:S(2)}, u32[]{:S(2)}) collective-permute-start(bf16[1344,128]{1,0:T(8,128)(2,1)S(1)} %bitcast.43), channel_id=1, source_target_pairs={{0,24},{2,26},{4,28},{6,30},{8,0},{10,2},{12,4},{14,6},{16,8},{18,... | collective-permute-start | bytes 1032200 | tf_op jit(solution)/shard_map/ppermute | solution.py:56
  46.9 26.8 %collective-permute-start.6 = (s32[12]{0:T(128)S(1)}, s32[12]{0:T(128)S(1)}, u32[]{:S(2)}, u32[]{:S(2)}) collective-permute-start(s32[12]{0:T(128)S(1)} %add.140), channel_id=1, source_target_pairs={{0,0},{32,96},{64,64},{96,160},{128,128},{160,224},{192,192},{224,... | collective-permute-start | bytes 152 | tf_op jit(solution)/shard_map/ppermute | solution.py:74
  50.2 54.4 %collective-permute-start.10 = (bf16[384,2048]{1,0:T(8,128)(2,1)}, bf16[384,2048]{1,0:T(8,128)(2,1)}, u32[]{:S(2)}, u32[]{:S(2)}) collective-permute-start(bf16[384,2048]{1,0:T(8,128)(2,1)} %bitcast.4), channel_id=1, source_target_pairs={{0,32},{32,64},{64,96},{96,128},{128,160},{160,192},{192,224},{224... | collective-permute-start | bytes 4718600 | tf_op jit(solution)/shard_map/ppermute | solution.py:69
  52.5 28.4 %collective-permute-start.4 = (bf16[5376,128]{1,0:T(8,128)(2,1)S(1)}, bf16[5376,128]{1,0:T(8,128)(2,1)S(1)}, u32[]{:S(2)}, u32[]{:S(2)}) collective-permute-start(bf16[5376,128]{1,0:T(8,128)(2,1)S(1)} %pad_maximum_fusion.c_ref), channel_id=1, source_target_pairs={{0,2},{2,4},{4,6},{6,0},{8,10},{10,12},{12,14},{14,8},{16,18},{18,... | collective-permute-start | bytes 4128776 | tf_op jit(solution)/shard_map/ppermute | solution.py:56
  54.5 30.8 %collective-permute-start.5 = (bf16[5376,128]{1,0:T(8,128)(2,1)S(1)}, bf16[5376,128]{1,0:T(8,128)(2,1)}, u32[]{:S(2)}, u32[]{:S(2)}) collective-permute-start(bf16[5376,128]{1,0:T(8,128)(2,1)S(1)} %pad_maximum_fusion.c_ref), channel_id=1, source_target_pairs={{0,6},{2,0},{4,2},{6,4},{8,14},{10,8},{12,10},{14,12},{16,22},{18,... | collective-permute-start | bytes 4128776 | tf_op jit(solution)/shard_map/ppermute | solution.py:56
  59.2 61.7 %copy-start.1 = (bf16[576,512]{1,0:T(8,128)(2,1)}, bf16[576,512]{1,0:T(8,128)(2,1)S(1)}, u32[]{:S(2)}) copy-start(bf16[576,512]{1,0:T(8,128)(2,1)S(1)} %fusion.spread) | copy-start | bytes 1769476
  60.0 44.6 %collective-permute-start.9 = (f32[3,128]{1,0:T(4,128)S(1)}, f32[3,128]{1,0:T(4,128)S(1)}, u32[]{:S(2)}, u32[]{:S(2)}) collective-permute-start(f32[3,128]{1,0:T(4,128)S(1)} %slice.55), channel_id=1, source_target_pairs={{0,1},{1,0},{2,3},{3,2},{4,5},{5,4},{6,7},{7,6},{8,9},{9,8},{10,11... | collective-permute-start | bytes 4616 | tf_op jit(solution)/shard_map/ppermute | solution.py:78
  85.3 13.7 %collective-permute-start.7 = (bf16[2688,128]{1,0:T(8,128)(2,1)S(1)}, bf16[2688,128]{1,0:T(8,128)(2,1)S(1)}, u32[]{:S(2)}, u32[]{:S(2)}) collective-permute-start(bf16[2688,128]{1,0:T(8,128)(2,1)S(1)} %slice.47), channel_id=1, source_target_pairs={{0,2},{2,4},{4,6},{6,0},{8,10},{10,12},{12,14},{14,8},{16,18},{18,... | collective-permute-start | bytes 2064392 | tf_op jit(solution)/shard_map/ppermute | solution.py:56
  90.4 11.7 %collective-permute-start.8 = (bf16[2688,128]{1,0:T(8,128)(2,1)S(1)}, bf16[2688,128]{1,0:T(8,128)(2,1)S(1)}, u32[]{:S(2)}, u32[]{:S(2)}) collective-permute-start(bf16[2688,128]{1,0:T(8,128)(2,1)S(1)} %slice.48), channel_id=1, source_target_pairs={{0,6},{2,0},{4,2},{6,4},{8,14},{10,8},{12,10},{14,12},{16,22},{18,... | collective-permute-start | bytes 2064392 | tf_op jit(solution)/shard_map/ppermute | solution.py:56
  94.5 26.4 %copy-start.3 = (s32[3,24]{1,0:T(4,128)}, s32[3,24]{1,0:T(4,128)S(1)}, u32[]{:S(2)}) copy-start(s32[3,24]{1,0:T(4,128)S(1)} %add_add_fusion.table) | copy-start | bytes 868
  104.6 20.2 %collective-permute-start.11 = (bf16[12,256,128]{2,1,0:T(8,128)(2,1)S(1)}, bf16[12,256,128]{2,1,0:T(8,128)(2,1)}, u32[]{:S(2)}, u32[]{:S(2)}) collective-permute-start(bf16[12,256,128]{2,1,0:T(8,128)(2,1)S(1)} %give_encodings.1), channel_id=1, source_target_pairs={{0,32},{32,0},{64,96},{96,64},{128,160},{160,128},{192,224},{224,1... | collective-permute-start | bytes 2359304 | tf_op jit(solution)/shard_map/ppermute | solution.py:83
  123.9 0.9 copy-start.2
Sparse Core Ops, SparseCore 0:
  35.8 56.5 all-gather.1

commit v4 on v3

--- a/solution.py
+++ b/solution.py
@@ -258,8 +258,7 @@
 def source_table(requests, core, here):
     owner, block = requests // 6, requests % 6
     near, far = ring_place(owner, core)
-    near_here, far_here = ring_place(here, core)
-    near, far = (near - near_here) % SIDE, (far - far_here) % SIDE
+    far = (far - ring_place(here, core)[1]) % SIDE
     which = jnp.where(far < 2, far, jnp.where(far == 3, 4, jnp.where(near < 2, 2, 3)))
     chunk = jnp.where(which == 3, near - 2, near)
     odd = block % 2
@@ -267,18 +266,12 @@
     return jnp.stack([which, row, odd])
 
 
-def in_three(value):
-    parts = []
-    for _ in range(3):
-        part = lax.reduce_precision(value, 8, 7)
-        parts.append(part.astype(jnp.bfloat16))
-        value = value - part
-    return jnp.stack(parts)
-
-
-def from_three(parts):
-    high, mid, low = parts.astype(jnp.float32)
-    return high + (mid + low)
+def first_ring(piece):
+    groups = ring_groups(lax.axis_size("segment"), 0)
+    copies = jnp.tile(piece, (SIDE, 1))
+    return lax.all_to_all(
+        copies, ("segment", "db"), split_axis=0, concat_axis=0, tiled=True, axis_index_groups=groups
+    )
 
 
 def on_device(stream, gain, key_weight, value_weight, owners, blocks, valid, database):
@@ -304,17 +297,12 @@
     info = jnp.concatenate(
         [squares, gain[0], valid[0].reshape(-1).astype(jnp.float32), requests.astype(jnp.float32)]
     )
-    info_rows = -(-info.shape[0] // HD)
-    info = jnp.pad(info, (0, info_rows * HD - info.shape[0]))
-    sent = in_three(info).reshape(3 * info_rows, HD)
-    sent = jnp.pad(sent, ((0, -sent.shape[0] % 16), (0, 0)))
-    requests_other = to_next_other_core(requests)
-    x_here = to_next(rows)
-
-    pieces_d = [packed_d] + [turned(packed_d, turn, 0) for turn in (-1, 2, 1)]
-    line_d = jnp.concatenate(pieces_d, axis=0)
-    next_w = to_next_turned(jnp.concatenate([packed_w, sent], axis=0), 0)
-    pieces_w = [next_w[:W_ROWS]] + [to_next_turned(packed_w, turn) for turn in (-1, 2, 1)]
+    info = jnp.pad(info, (0, -info.shape[0] % 1024)).reshape(-1, HD)
+
+    pieces_w = [to_next_turned(packed_w, turn) for turn in (0, -1, 2, 1)]
+    pieces_w, line_d, info, requests, rows = lax.optimization_barrier(
+        (pieces_w, first_ring(packed_d), info, requests, rows)
+    )
     all_w = lax.all_gather(
         jnp.concatenate(pieces_w, axis=0),
         ("segment", "db"),
@@ -323,7 +311,9 @@
         axis_index_groups=ring_groups(lax.axis_size("segment"), 1),
     ).reshape(RING, W_ROWS, HD)
     d_before, d_after = turned(line_d, 1, 1), turned(line_d, -1, 1)
-    info_here = from_three(next_w[W_ROWS:W_ROWS + 3 * info_rows].reshape(3, info_rows * HD))
+    info_here = to_next(info).reshape(-1)
+    requests_other = to_next_other_core(requests)
+    x_here = to_next(rows)
     spread = spread_of(core, place)
     d_before, d_after, spread, requests_other = lax.optimization_barrier((d_before, d_after, spread, requests_other))
     mid_d = line_d.shape[0] // 2

time: 152 us -> 151 us (level)
  other arithmetic: 7.35 us -> 4.85 us
  starting transfers between devices: 75.5 us -> 77.5 us
  waiting for transfers between devices: 23.7 us -> 22.1 us
    ppermute x7 -> x4, waiting for transfers between devices: 19.3 us -> 7.18 us  [turned(): return lax.ppermute(value, ('segment', 'db'), pairs)]
    ppermute x7 -> x4, starting transfers between devices: 24.2 us -> 13 us  [turned(): return lax.ppermute(value, ('segment', 'db'), pairs)]
    ppermute x1 -> x2, waiting for transfers between devices: 0.01 us -> 9.27 us  [to_next(): lax.ppermute(value, 'segment', [(s, (s + 1) % count) for s in range(count)])]
    all_to_all x0 -> x1, starting transfers between devices: none -> 5.16 us  [first_ring(): lax.all_to_all(copies, ('segment', 'db'), split_axis=0, concat_axis=0, ti...]
    ppermute x1 -> x2, starting transfers between devices: 1.92 us -> 5.56 us  [to_next(): lax.ppermute(value, 'segment', [(s, (s + 1) % count) for s in range(count)])]
    ppermute x1, starting transfers between devices: 14.8 us -> 17.9 us  [other_core(): return lax.ppermute(value, 'segment', [(s, s ^ 1) for s in range(count)])]
  transfers between devices with their start and end apart: 16 -> 15, of which waited for: 7 -> 5; matrix products, arithmetic and copies ran while one was open for 3% -> 5% of each run, Pallas kernels for 4% -> 4%
where the time goes in v4:
time: 151 us; the launch traced here: 150 us
  starting transfers between devices  77.5 us (51%)
  Pallas kernels  25.2 us (17%)
  waiting for transfers between devices  22.1 us (15%)
  between operations  13.7 us (9%)
  local copies, waits for them, and re-layouts  7.03 us (5%)
  other arithmetic  4.85 us (3%)
    pallas_call x1, Pallas kernels, attend(): pl.pallas_call(attend_kernel, grid_spec=pltpu.PrefetchScalarGridSpec(num_...  19.3 us
    ppermute x1, starting transfers between devices, other_core(): return lax.ppermute(value, 'segment', [(s, s ^ 1) for s in range(count)])  17.9 us
    ppermute x4, starting transfers between devices, to_next_turned(): return lax.ppermute(value, ('segment', 'db'), pairs)  17.6 us
    ppermute x1, starting transfers between devices, other_mp(): return lax.ppermute(value, 'mp', [(0, 1), (1, 0)])  13.6 us
    ppermute x4, starting transfers between devices, turned(): return lax.ppermute(value, ('segment', 'db'), pairs)  13 us
    ppermute x2, waiting for transfers between devices, to_next(): lax.ppermute(value, 'segment', [(s, (s + 1) % count) for s in range(count)])  9.27 us
    ppermute x4, waiting for transfers between devices, turned(): return lax.ppermute(value, ('segment', 'db'), pairs)  7.18 us
    ppermute x2, starting transfers between devices, to_next(): lax.ppermute(value, 'segment', [(s, (s + 1) % count) for s in range(count)])  5.56 us
  transfers between devices with their start and end apart: 15, of which 5 were waited for; matrix products, arithmetic and copies ran while one was open for 5% of the time, Pallas kernels for 4%

profile of v4, /device:TPU:1, one launch (start us, length us, event | category | flops | bytes accessed | tf_op | source)
XLA Modules:
  0.0 150.4 jit_solution(5364223467720107725)
XLA Ops:
  8.4 1.3 tile.9
  9.7 5.2 %all-to-all-start = ((bf16[4,1344,128]{2,1,0:T(8,128)(2,1)}), bf16[4,1344,128]{2,1,0:T(8,128)(2,1)S(1)}, u32[]{:S(2)}, u32[]{:S(2)}) async-start(bf16[4,1344,128]{2,1,0:T(8,128)(2,1)} %tile.9), calls=%async_computation | async-start | bytes 2752512 | tf_op jit(solution)/shard_map/all_to_all | solution.py:272
  15.0 4.2 %collective-permute-start = (bf16[1024,128]{1,0:T(8,128)(2,1)S(1)}, bf16[1024,128]{1,0:T(8,128)(2,1)S(1)}, u32[]{:S(2)}, u32[]{:S(2)}) collective-permute-start(bf16[1024,128]{1,0:T(8,128)(2,1)S(1)} %bitcast.51), channel_id=1, source_target_pairs={{480,0},{482,2},{484,4},{486,6},{488,8},{490,10},{492,12},{494,14}... | collective-permute-start | bytes 786440 | tf_op jit(solution)/shard_map/ppermute | solution.py:64
  19.2 4.6 %collective-permute-start.1 = (bf16[1024,128]{1,0:T(8,128)(2,1)S(1)}, bf16[1024,128]{1,0:T(8,128)(2,1)S(1)}, u32[]{:S(2)}, u32[]{:S(2)}) collective-permute-start(bf16[1024,128]{1,0:T(8,128)(2,1)S(1)} %bitcast.52), channel_id=1, source_target_pairs={{480,24},{482,26},{484,28},{486,30},{488,0},{490,2},{492,4},{494,6... | collective-permute-start | bytes 786440 | tf_op jit(solution)/shard_map/ppermute | solution.py:64
  23.8 6.8 %collective-permute-start.2 = (bf16[1024,128]{1,0:T(8,128)(2,1)S(1)}, bf16[1024,128]{1,0:T(8,128)(2,1)S(1)}, u32[]{:S(2)}, u32[]{:S(2)}) collective-permute-start(bf16[1024,128]{1,0:T(8,128)(2,1)S(1)} %bitcast.53), channel_id=1, source_target_pairs={{480,16},{482,18},{484,20},{486,22},{488,24},{490,26},{492,28},{49... | collective-permute-start | bytes 786440 | tf_op jit(solution)/shard_map/ppermute | solution.py:64
  30.7 1.9 %collective-permute-start.3 = (bf16[1024,128]{1,0:T(8,128)(2,1)S(1)}, bf16[1024,128]{1,0:T(8,128)(2,1)S(1)}, u32[]{:S(2)}, u32[]{:S(2)}) collective-permute-start(bf16[1024,128]{1,0:T(8,128)(2,1)S(1)} %bitcast.54), channel_id=1, source_target_pairs={{480,8},{482,10},{484,12},{486,14},{488,16},{490,18},{492,20},{494... | collective-permute-start | bytes 786440 | tf_op jit(solution)/shard_map/ppermute | solution.py:64
  33.0 1.8 %multiply_reduce_fusion = f32[384]{0:T(512)S(1)} fusion(bf16[1,384,2048]{2,1,0:T(8,128)(2,1)} %param.8), kind=kLoop, calls=%fused_computation | loop fusion | flops 2358912 | bytes 1574400 | tf_op jit(solution)/shard_map/reduce_sum | solution.py:295
  34.9 5.0 %collective-permute-done.3 = bf16[1024,128]{1,0:T(8,128)(2,1)S(1)} collective-permute-done((bf16[1024,128]{1,0:T(8,128)(2,1)S(1)}, bf16[1024,128]{1,0:T(8,128)(2,1)S(1)}, u32[]{:S(2)}, u32[]{:S(2)}) %collective-permute-start.3) | collective-permute-done | bytes 262176 | tf_op jit(solution)/shard_map/ppermute | solution.py:64
  40.9 2.2 %collective-permute-start.5 = (bf16[5376,128]{1,0:T(8,128)(2,1)S(1)}, bf16[5376,128]{1,0:T(8,128)(2,1)S(1)}, u32[]{:S(2)}, u32[]{:S(2)}) collective-permute-start(bf16[5376,128]{1,0:T(8,128)(2,1)S(1)} %bitcast.42), channel_id=1, source_target_pairs={{0,2},{2,4},{4,6},{6,0},{8,10},{10,12},{12,14},{14,8},{16,18},{18,... | collective-permute-start | bytes 4128776 | tf_op jit(solution)/shard_map/ppermute | solution.py:56
  43.1 4.3 %collective-permute-start.6 = (bf16[5376,128]{1,0:T(8,128)(2,1)S(1)}, bf16[5376,128]{1,0:T(8,128)(2,1)}, u32[]{:S(2)}, u32[]{:S(2)}) collective-permute-start(bf16[5376,128]{1,0:T(8,128)(2,1)S(1)} %bitcast.43), channel_id=1, source_target_pairs={{0,6},{2,0},{4,2},{6,4},{8,14},{10,8},{12,10},{14,12},{16,22},{18,... | collective-permute-start | bytes 4128776 | tf_op jit(solution)/shard_map/ppermute | solution.py:56
  47.5 3.0 %collective-permute-start.11 = (bf16[384,2048]{1,0:T(8,128)(2,1)}, bf16[384,2048]{1,0:T(8,128)(2,1)}, u32[]{:S(2)}, u32[]{:S(2)}) collective-permute-start(bf16[384,2048]{1,0:T(8,128)(2,1)} %bitcast.48), channel_id=1, source_target_pairs={{0,32},{32,64},{64,96},{96,128},{128,160},{160,192},{192,224},{224... | collective-permute-start | bytes 4718600 | tf_op jit(solution)/shard_map/ppermute | solution.py:69
  50.5 2.6 %collective-permute-start.4 = (f32[24,128]{1,0:T(8,128)S(1)}, f32[24,128]{1,0:T(8,128)S(1)}, u32[]{:S(2)}, u32[]{:S(2)}) collective-permute-start(f32[24,128]{1,0:T(8,128)S(1)} %pad_bitcast_fusion), channel_id=1, source_target_pairs={{0,32},{32,64},{64,96},{96,128},{128,160},{160,192},{192,224},{224... | collective-permute-start | bytes 36872 | tf_op jit(solution)/shard_map/ppermute | solution.py:69
  54.1 4.7 %collective-permute-start.7 = (s32[12]{0:T(128)S(1)}, s32[12]{0:T(128)S(1)}, u32[]{:S(2)}, u32[]{:S(2)}) collective-permute-start(s32[12]{0:T(128)S(1)} %add.117), channel_id=1, source_target_pairs={{0,0},{32,96},{64,64},{96,160},{128,128},{160,224},{192,192},{224,... | collective-permute-start | bytes 152 | tf_op jit(solution)/shard_map/ppermute | solution.py:74
  58.9 9.3 %collective-permute-done.4 = f32[24,128]{1,0:T(8,128)S(1)} collective-permute-done((f32[24,128]{1,0:T(8,128)S(1)}, f32[24,128]{1,0:T(8,128)S(1)}, u32[]{:S(2)}, u32[]{:S(2)}) %collective-permute-start.4) | collective-permute-done | bytes 12320 | tf_op jit(solution)/shard_map/ppermute | solution.py:69
  68.2 13.6 %collective-permute-start.10 = (f32[3,128]{1,0:T(4,128)S(1)}, f32[3,128]{1,0:T(4,128)S(1)}, u32[]{:S(2)}, u32[]{:S(2)}) collective-permute-start(f32[3,128]{1,0:T(4,128)S(1)} %slice.42), channel_id=1, source_target_pairs={{0,1},{1,0},{2,3},{3,2},{4,5},{5,4},{6,7},{7,6},{8,9},{9,8},{10,11... | collective-permute-start | bytes 4616 | tf_op jit(solution)/shard_map/ppermute | solution.py:78
  82.6 2.0 %collective-permute-start.8 = (bf16[2688,128]{1,0:T(8,128)(2,1)S(1)}, bf16[2688,128]{1,0:T(8,128)(2,1)S(1)}, u32[]{:S(2)}, u32[]{:S(2)}) collective-permute-start(bf16[2688,128]{1,0:T(8,128)(2,1)S(1)} %slice.36), channel_id=1, source_target_pairs={{0,2},{2,4},{4,6},{6,0},{8,10},{10,12},{12,14},{14,8},{16,18},{18,... | collective-permute-start | bytes 2064392 | tf_op jit(solution)/shard_map/ppermute | solution.py:56
  84.6 1.1 slice.37
  85.8 4.5 %collective-permute-start.9 = (bf16[2688,128]{1,0:T(8,128)(2,1)S(1)}, bf16[2688,128]{1,0:T(8,128)(2,1)S(1)}, u32[]{:S(2)}, u32[]{:S(2)}) collective-permute-start(bf16[2688,128]{1,0:T(8,128)(2,1)S(1)} %slice.37), channel_id=1, source_target_pairs={{0,6},{2,0},{4,2},{6,4},{8,14},{10,8},{12,10},{14,12},{16,22},{18,... | collective-permute-start | bytes 2064392 | tf_op jit(solution)/shard_map/ppermute | solution.py:56
  90.9 4.8 %collective-permute-done.8.ol_ref = bf16[2688,128]{1,0:T(8,128)(2,1)S(1)} collective-permute-done((bf16[2688,128]{1,0:T(8,128)(2,1)S(1)}, bf16[2688,128]{1,0:T(8,128)(2,1)S(1)}, u32[]{:S(2)}, u32[]{:S(2)}) %collective-permute-start.8) | collective-permute-done | bytes 688160 | tf_op jit(solution)/shard_map/ppermute | solution.py:56
  95.8 2.3 %collective-permute-done.9.or_ref = bf16[2688,128]{1,0:T(8,128)(2,1)S(1)} collective-permute-done((bf16[2688,128]{1,0:T(8,128)(2,1)S(1)}, bf16[2688,128]{1,0:T(8,128)(2,1)S(1)}, u32[]{:S(2)}, u32[]{:S(2)}) %collective-permute-start.9) | collective-permute-done | bytes 688160 | tf_op jit(solution)/shard_map/ppermute | solution.py:56
  98.1 2.4 %give_encodings.1 = bf16[12,256,128]{2,1,0:T(8,128)(2,1)S(1)} custom-call(s32[3,24]{1,0:T(4,128)S(1)} %add_add_fusion.table, bf16[5376,128]{1,0:T(8,128)(2,1)S(1)} %bitcast.44, bf16[5376,128]{1,0:T(8,128)(2,1)} %collective-permute-done.6.r_ref, bf16[2688,128]{1,0:T(8,128)(2,1)S(1)} %collective-permute-done.8.ol_ref, ...), custom_call_target="tpu_custom_call" | custom-call | tf_op jit(solution)/shard_map/give_encodings/pallas_call | solution.py:136
  100.6 17.9 %collective-permute-start.12 = (bf16[12,256,128]{2,1,0:T(8,128)(2,1)S(1)}, bf16[12,256,128]{2,1,0:T(8,128)(2,1)}, u32[]{:S(2)}, u32[]{:S(2)}) collective-permute-start(bf16[12,256,128]{2,1,0:T(8,128)(2,1)S(1)} %give_encodings.1), channel_id=1, source_target_pairs={{0,32},{32,0},{64,96},{96,64},{128,160},{160,128},{192,224},{224,1... | collective-permute-start | bytes 2359304 | tf_op jit(solution)/shard_map/ppermute | solution.py:83
  119.9 3.5 %pick_encodings.1.own_ref = bf16[768,512]{1,0:T(8,128)(2,1)S(1)} custom-call(s32[3,24]{1,0:T(4,128)S(1)} %add_add_fusion.table, bf16[5376,128]{1,0:T(8,128)(2,1)S(1)} %bitcast.45, bf16[5376,128]{1,0:T(8,128)(2,1)} %collective-permute-done.6.r_ref, bf16[2688,128]{1,0:T(8,128)(2,1)S(1)} %collective-permute-done.8.ol_ref, ...), custom_call_target="tpu_custom_call" | custom-call | tf_op jit(solution)/shard_map/pick_encodings/pallas_call | solution.py:148
  124.2 19.3 %attend_heads.1 = bf16[384,2048]{1,0:T(8,128)(2,1)} custom-call(s32[12]{0:T(128)} %get-tuple-element.46.live, s32[3,24]{1,0:T(4,128)} %copy-done.3, bf16[768,512]{1,0:T(8,128)(2,1)} %copy-done.2, bf16[12,256,128]{2,1,0:T(8,128)(2,1)} %collective-permute-done.12.slabs, bf16[576,512]{1,0:T(8,128)(2,1)} %fusion.spread, bf16[16,1024,128]{2,1,0:T(8,128)(2,1)} %bitcast.46, ...), custom_call_target="tpu_custom_call" | custom-call | tf_op jit(solution)/shard_map/attend_heads/pallas_call | solution.py:219
  (63 shorter events, 8.4 us)
Async XLA Ops:
  6.5 1.1 copy-start
  9.7 5.2 %copy-start.4 = (bf16[1,28,2048]{2,1,0:T(8,128)(2,1)S(1)}, bf16[1,28,2048]{2,1,0:T(8,128)(2,1)}, u32[]{:S(2)}) copy-start(bf16[1,28,2048]{2,1,0:T(8,128)(2,1)} %param.11) | copy-start | bytes 344068
  9.7 5.2 %copy-start.5 = (bf16[1,28,2048]{2,1,0:T(8,128)(2,1)S(1)}, bf16[1,28,2048]{2,1,0:T(8,128)(2,1)}, u32[]{:S(2)}) copy-start(bf16[1,28,2048]{2,1,0:T(8,128)(2,1)} %param.10) | copy-start | bytes 344068
  9.7 23.0 %copy-start.9 = (s32[1,6,2]{1,2,0:T(2,128)S(1)}, s32[1,6,2]{1,2,0:T(2,128)}, u32[]{:S(2)}) copy-start(s32[1,6,2]{1,2,0:T(2,128)} %param.14) | copy-start | bytes 148
  9.7 23.1 %copy-start.7 = (s32[1,6,2]{1,2,0:T(2,128)S(1)}, s32[1,6,2]{1,2,0:T(2,128)}, u32[]{:S(2)}) copy-start(s32[1,6,2]{1,2,0:T(2,128)} %param.13) | copy-start | bytes 148
  9.7 23.1 %copy-start.8 = (s32[1,6,2]{1,2,0:T(2,128)S(1)}, s32[1,6,2]{1,2,0:T(2,128)}, u32[]{:S(2)}) copy-start(s32[1,6,2]{1,2,0:T(2,128)} %param.12) | copy-start | bytes 148
  9.7 30.2 %all-to-all-start = ((bf16[4,1344,128]{2,1,0:T(8,128)(2,1)}), bf16[4,1344,128]{2,1,0:T(8,128)(2,1)S(1)}, u32[]{:S(2)}, u32[]{:S(2)}) async-start(bf16[4,1344,128]{2,1,0:T(8,128)(2,1)} %tile.9), calls=%async_computation | async-start | bytes 2752512 | tf_op jit(solution)/shard_map/all_to_all | solution.py:272
  14.8 109.4 %all-gather.2.cloned.1.call-start = ((), (), s32[]{:S(2)}) async-start(), calls=%async_computation.1 | async-start | bytes 5242880 | tf_op jit(solution)/shard_map/all_gather | solution.py:306
  14.8 20.0 %copy-start.6 = (f32[1,2048]{1,0:T(1,128)S(1)}, f32[1,2048]{1,0:T(1,128)}, u32[]{:S(2)}) copy-start(f32[1,2048]{1,0:T(1,128)} %param.9) | copy-start | bytes 24580
  15.0 19.9 %collective-permute-start = (bf16[1024,128]{1,0:T(8,128)(2,1)S(1)}, bf16[1024,128]{1,0:T(8,128)(2,1)S(1)}, u32[]{:S(2)}, u32[]{:S(2)}) collective-permute-start(bf16[1024,128]{1,0:T(8,128)(2,1)S(1)} %bitcast.51), channel_id=1, source_target_pairs={{480,0},{482,2},{484,4},{486,6},{488,8},{490,10},{492,12},{494,14}... | collective-permute-start | bytes 786440 | tf_op jit(solution)/shard_map/ppermute | solution.py:64
  19.2 15.7 %collective-permute-start.1 = (bf16[1024,128]{1,0:T(8,128)(2,1)S(1)}, bf16[1024,128]{1,0:T(8,128)(2,1)S(1)}, u32[]{:S(2)}, u32[]{:S(2)}) collective-permute-start(bf16[1024,128]{1,0:T(8,128)(2,1)S(1)} %bitcast.52), channel_id=1, source_target_pairs={{480,24},{482,26},{484,28},{486,30},{488,0},{490,2},{492,4},{494,6... | collective-permute-start | bytes 786440 | tf_op jit(solution)/shard_map/ppermute | solution.py:64
  23.8 11.1 %collective-permute-start.2 = (bf16[1024,128]{1,0:T(8,128)(2,1)S(1)}, bf16[1024,128]{1,0:T(8,128)(2,1)S(1)}, u32[]{:S(2)}, u32[]{:S(2)}) collective-permute-start(bf16[1024,128]{1,0:T(8,128)(2,1)S(1)} %bitcast.53), channel_id=1, source_target_pairs={{480,16},{482,18},{484,20},{486,22},{488,24},{490,26},{492,28},{49... | collective-permute-start | bytes 786440 | tf_op jit(solution)/shard_map/ppermute | solution.py:64
  30.7 9.2 %collective-permute-start.3 = (bf16[1024,128]{1,0:T(8,128)(2,1)S(1)}, bf16[1024,128]{1,0:T(8,128)(2,1)S(1)}, u32[]{:S(2)}, u32[]{:S(2)}) collective-permute-start(bf16[1024,128]{1,0:T(8,128)(2,1)S(1)} %bitcast.54), channel_id=1, source_target_pairs={{480,8},{482,10},{484,12},{486,14},{488,16},{490,18},{492,20},{494... | collective-permute-start | bytes 786440 | tf_op jit(solution)/shard_map/ppermute | solution.py:64
  40.9 41.6 %collective-permute-start.5 = (bf16[5376,128]{1,0:T(8,128)(2,1)S(1)}, bf16[5376,128]{1,0:T(8,128)(2,1)S(1)}, u32[]{:S(2)}, u32[]{:S(2)}) collective-permute-start(bf16[5376,128]{1,0:T(8,128)(2,1)S(1)} %bitcast.42), channel_id=1, source_target_pairs={{0,2},{2,4},{4,6},{6,0},{8,10},{10,12},{12,14},{14,8},{16,18},{18,... | collective-permute-start | bytes 4128776 | tf_op jit(solution)/shard_map/ppermute | solution.py:56
  43.1 39.4 %collective-permute-start.6 = (bf16[5376,128]{1,0:T(8,128)(2,1)S(1)}, bf16[5376,128]{1,0:T(8,128)(2,1)}, u32[]{:S(2)}, u32[]{:S(2)}) collective-permute-start(bf16[5376,128]{1,0:T(8,128)(2,1)S(1)} %bitcast.43), channel_id=1, source_target_pairs={{0,6},{2,0},{4,2},{6,4},{8,14},{10,8},{12,10},{14,12},{16,22},{18,... | collective-permute-start | bytes 4128776 | tf_op jit(solution)/shard_map/ppermute | solution.py:56
  47.5 53.1 %collective-permute-start.11 = (bf16[384,2048]{1,0:T(8,128)(2,1)}, bf16[384,2048]{1,0:T(8,128)(2,1)}, u32[]{:S(2)}, u32[]{:S(2)}) collective-permute-start(bf16[384,2048]{1,0:T(8,128)(2,1)} %bitcast.48), channel_id=1, source_target_pairs={{0,32},{32,64},{64,96},{96,128},{128,160},{160,192},{192,224},{224... | collective-permute-start | bytes 4718600 | tf_op jit(solution)/shard_map/ppermute | solution.py:69
  50.5 17.6 %collective-permute-start.4 = (f32[24,128]{1,0:T(8,128)S(1)}, f32[24,128]{1,0:T(8,128)S(1)}, u32[]{:S(2)}, u32[]{:S(2)}) collective-permute-start(f32[24,128]{1,0:T(8,128)S(1)} %pad_bitcast_fusion), channel_id=1, source_target_pairs={{0,32},{32,64},{64,96},{96,128},{128,160},{160,192},{192,224},{224... | collective-permute-start | bytes 36872 | tf_op jit(solution)/shard_map/ppermute | solution.py:69
  54.1 28.4 %collective-permute-start.7 = (s32[12]{0:T(128)S(1)}, s32[12]{0:T(128)S(1)}, u32[]{:S(2)}, u32[]{:S(2)}) collective-permute-start(s32[12]{0:T(128)S(1)} %add.117), channel_id=1, source_target_pairs={{0,0},{32,96},{64,64},{96,160},{128,128},{160,224},{192,192},{224,... | collective-permute-start | bytes 152 | tf_op jit(solution)/shard_map/ppermute | solution.py:74
  68.2 32.4 %collective-permute-start.10 = (f32[3,128]{1,0:T(4,128)S(1)}, f32[3,128]{1,0:T(4,128)S(1)}, u32[]{:S(2)}, u32[]{:S(2)}) collective-permute-start(f32[3,128]{1,0:T(4,128)S(1)} %slice.42), channel_id=1, source_target_pairs={{0,1},{1,0},{2,3},{3,2},{4,5},{5,4},{6,7},{7,6},{8,9},{9,8},{10,11... | collective-permute-start | bytes 4616 | tf_op jit(solution)/shard_map/ppermute | solution.py:78
  82.6 13.2 %collective-permute-start.8 = (bf16[2688,128]{1,0:T(8,128)(2,1)S(1)}, bf16[2688,128]{1,0:T(8,128)(2,1)S(1)}, u32[]{:S(2)}, u32[]{:S(2)}) collective-permute-start(bf16[2688,128]{1,0:T(8,128)(2,1)S(1)} %slice.36), channel_id=1, source_target_pairs={{0,2},{2,4},{4,6},{6,0},{8,10},{10,12},{12,14},{14,8},{16,18},{18,... | collective-permute-start | bytes 2064392 | tf_op jit(solution)/shard_map/ppermute | solution.py:56
  85.8 12.3 %collective-permute-start.9 = (bf16[2688,128]{1,0:T(8,128)(2,1)S(1)}, bf16[2688,128]{1,0:T(8,128)(2,1)S(1)}, u32[]{:S(2)}, u32[]{:S(2)}) collective-permute-start(bf16[2688,128]{1,0:T(8,128)(2,1)S(1)} %slice.37), channel_id=1, source_target_pairs={{0,6},{2,0},{4,2},{6,4},{8,14},{10,8},{12,10},{14,12},{16,22},{18,... | collective-permute-start | bytes 2064392 | tf_op jit(solution)/shard_map/ppermute | solution.py:56
  90.9 28.9 %copy-start.3 = (s32[3,24]{1,0:T(4,128)}, s32[3,24]{1,0:T(4,128)S(1)}, u32[]{:S(2)}) copy-start(s32[3,24]{1,0:T(4,128)S(1)} %add_add_fusion.table) | copy-start | bytes 868
  90.9 28.9 %copy-start.1 = (bf16[576,512]{1,0:T(8,128)(2,1)S(1)}, bf16[576,512]{1,0:T(8,128)(2,1)}, u32[]{:S(2)}) copy-start(bf16[576,512]{1,0:T(8,128)(2,1)} %fusion.spread) | copy-start | bytes 1769476
  100.6 23.7 %collective-permute-start.12 = (bf16[12,256,128]{2,1,0:T(8,128)(2,1)S(1)}, bf16[12,256,128]{2,1,0:T(8,128)(2,1)}, u32[]{:S(2)}, u32[]{:S(2)}) collective-permute-start(bf16[12,256,128]{2,1,0:T(8,128)(2,1)S(1)} %give_encodings.1), channel_id=1, source_target_pairs={{0,32},{32,0},{64,96},{96,64},{128,160},{160,128},{192,224},{224,1... | collective-permute-start | bytes 2359304 | tf_op jit(solution)/shard_map/ppermute | solution.py:83
  (1 other events, 0.9 us)
Sparse Core Ops, SparseCore 0:
  41.1 44.2 all-gather.1

commit v5 on v4

--- a/solution.py
+++ b/solution.py
@@ -106,15 +106,11 @@
     rows = []
     for i in range(REQ):
         slab = slabs[i]
-        rows.append(jnp.concatenate([slab[t * HALF:(t + 1) * HALF] for t in range(tiles)], axis=1))
+        even = jnp.concatenate([slab[t * HALF:(t + 1) * HALF] for t in range(tiles)], axis=1)
+        odd = jnp.concatenate([even[:, SHIFT:], even[:, :SHIFT]], axis=1)
+        rows.append(jnp.where(table[2, i] == 1, odd, even))
     stacked = jnp.concatenate(rows, axis=0)
-    even = jnp.dot(stacked, spread[SHIFT:], preferred_element_type=jnp.float32)
-    odd = jnp.dot(stacked, spread[:ENC_PAD], preferred_element_type=jnp.float32)
-    placed = []
-    for i in range(REQ):
-        here = slice(i * HALF, (i + 1) * HALF)
-        placed.append(jnp.where(table[2, i] == 1, odd[here], even[here]).astype(jnp.bfloat16))
-    return placed
+    return jnp.dot(stacked, spread[...], preferred_element_type=jnp.float32).astype(jnp.bfloat16)
 
 
 def give_kernel(table, c_ref, r_ref, ol_ref, or_ref, l_ref, out_ref, sems):
@@ -123,8 +119,7 @@
 
 def pick_kernel(table, c_ref, r_ref, ol_ref, or_ref, l_ref, spread, out_ref, slabs, sems):
     fetch(table, 0, (c_ref, r_ref, ol_ref, or_ref, l_ref), slabs, sems)
-    for i, block in enumerate(spread_slabs(table, slabs, spread)):
-        out_ref[i * HALF:(i + 1) * HALF] = block
+    out_ref[...] = spread_slabs(table, slabs, spread)
 
 
 SMEM = pl.BlockSpec(memory_space=pltpu.SMEM)
@@ -165,8 +160,7 @@
 
     @pl.when(pl.program_id(0) == 0)
     def _():
-        for i, block in enumerate(spread_slabs(table, slabs, spread)):
-            other_ref[i * HALF:(i + 1) * HALF] = block
+        other_ref[...] = spread_slabs(table, slabs, spread)
 
     own, other = own_ref[...], other_ref[...]
     inv = inv_ref[...]
@@ -224,7 +218,7 @@
             in_specs=[
                 whole(REQ * HALF, ENC_PAD),
                 whole(REQ, SLAB, HD),
-                whole(SHIFT + ENC_PAD, ENC_PAD),
+                whole(ENC_PAD, ENC_PAD),
                 pl.BlockSpec((RING, HB * 2 * W_PAD, HD), lambda i, live, table: (0, i, 0)),
                 pl.BlockSpec((tokens, HB * HD), lambda i, live, table: (0, i)),
                 whole(tokens, 1),
@@ -245,13 +239,12 @@
 
 
 def spread_of(core, here):
-    channel = jnp.arange(SHIFT + ENC_PAD) - SHIFT
+    channel = jnp.arange(ENC_PAD)
     near, far = ring_place(channel // W_PART, core)
     near = (near - ring_place(here, core)[0]) % SIDE
     place = (far * SIDE + near) * W_PAD + channel % W_PART
-    used = jnp.logical_and(channel >= 0, channel < ENC)
-    place = lax.optimization_barrier(jnp.where(used, place, -1))
-    column = lax.broadcasted_iota(jnp.int32, (SHIFT + ENC_PAD, ENC_PAD), 1)
+    place = lax.optimization_barrier(jnp.where(channel < ENC, place, -1))
+    column = lax.broadcasted_iota(jnp.int32, (ENC_PAD, ENC_PAD), 1)
     return (place[:, None] == column).astype(jnp.bfloat16)
 
 
@@ -300,8 +293,8 @@
     info = jnp.pad(info, (0, -info.shape[0] % 1024)).reshape(-1, HD)
 
     pieces_w = [to_next_turned(packed_w, turn) for turn in (0, -1, 2, 1)]
-    pieces_w, line_d, info, requests, rows = lax.optimization_barrier(
-        (pieces_w, first_ring(packed_d), info, requests, rows)
+    pieces_w[0], line_d, info, requests = lax.optimization_barrier(
+        (pieces_w[0], first_ring(packed_d), info, requests)
     )
     all_w = lax.all_gather(
         jnp.concatenate(pieces_w, axis=0),
@@ -313,6 +306,7 @@
     d_before, d_after = turned(line_d, 1, 1), turned(line_d, -1, 1)
     info_here = to_next(info).reshape(-1)
     requests_other = to_next_other_core(requests)
+    info_here, rows = lax.optimization_barrier((info_here, rows))
     x_here = to_next(rows)
     spread = spread_of(core, place)
     d_before, d_after, spread, requests_other = lax.optimization_barrier((d_before, d_after, spread, requests_other))

time: 151 us -> 146 us (0.967)
  starting transfers between devices: 77.5 us -> 57.9 us
  waiting for transfers between devices: 22.1 us -> 37 us
    ppermute x1, waiting for transfers between devices: 0.64 us -> 19.4 us  [to_next_other_core(): lax.ppermute(value, 'segment', [(s, (s + 1) % count ^ 1) for s in range(c...]
    ppermute x1, starting transfers between devices: 17.9 us -> 1.92 us  [other_core(): return lax.ppermute(value, 'segment', [(s, s ^ 1) for s in range(count)])]
    ppermute x1, starting transfers between devices: 4.74 us -> 1.91 us  [to_next_other_core(): lax.ppermute(value, 'segment', [(s, (s + 1) % count ^ 1) for s in range(c...]
    ppermute x4, waiting for transfers between devices: 4.98 us -> 2.44 us  [to_next_turned(): return lax.ppermute(value, ('segment', 'db'), pairs)]
    ppermute x2, waiting for transfers between devices: 9.27 us -> 6.9 us  [to_next(): lax.ppermute(value, 'segment', [(s, (s + 1) % count) for s in range(count)])]
where the time goes in v5:
time: 146 us; the launch traced here: 145 us
  starting transfers between devices  57.9 us (40%)
  waiting for transfers between devices  37 us (25%)
  Pallas kernels  24.5 us (17%)
  between operations  13.7 us (9%)
  local copies, waits for them, and re-layouts  7 us (5%)
  other arithmetic  4.83 us (3%)
    ppermute x1, waiting for transfers between devices, to_next_other_core(): lax.ppermute(value, 'segment', [(s, (s + 1) % count ^ 1) for s in range(c...  19.4 us
    pallas_call x1, Pallas kernels, attend(): pl.pallas_call(attend_kernel, grid_spec=pltpu.PrefetchScalarGridSpec(num_...  18.9 us
    ppermute x4, starting transfers between devices, to_next_turned(): return lax.ppermute(value, ('segment', 'db'), pairs)  17.5 us
    ppermute x1, starting transfers between devices, other_mp(): return lax.ppermute(value, 'mp', [(0, 1), (1, 0)])  13 us
    ppermute x4, starting transfers between devices, turned(): return lax.ppermute(value, ('segment', 'db'), pairs)  13 us
    ppermute x4, waiting for transfers between devices, turned(): return lax.ppermute(value, ('segment', 'db'), pairs)  8.26 us
    ppermute x2, waiting for transfers between devices, to_next(): lax.ppermute(value, 'segment', [(s, (s + 1) % count) for s in range(count)])  6.9 us
    ppermute x2, starting transfers between devices, to_next(): lax.ppermute(value, 'segment', [(s, (s + 1) % count) for s in range(count)])  5.48 us
  transfers between devices with their start and end apart: 15, of which 5 were waited for; matrix products, arithmetic and copies ran while one was open for 5% of the time, Pallas kernels for 4%

profile of v5, /device:TPU:1, one launch (start us, length us, event | category | flops | bytes accessed | tf_op | source)
XLA Modules:
  0.0 145.0 jit_solution(5115886461043686726)
XLA Ops:
  8.4 1.3 tile.9
  9.7 5.2 %all-to-all-start = ((bf16[4,1344,128]{2,1,0:T(8,128)(2,1)}), bf16[4,1344,128]{2,1,0:T(8,128)(2,1)S(1)}, u32[]{:S(2)}, u32[]{:S(2)}) async-start(bf16[4,1344,128]{2,1,0:T(8,128)(2,1)} %tile.9), calls=%async_computation | async-start | bytes 2752512 | tf_op jit(solution)/shard_map/all_to_all | solution.py:265
  15.0 4.2 %collective-permute-start = (bf16[1024,128]{1,0:T(8,128)(2,1)S(1)}, bf16[1024,128]{1,0:T(8,128)(2,1)S(1)}, u32[]{:S(2)}, u32[]{:S(2)}) collective-permute-start(bf16[1024,128]{1,0:T(8,128)(2,1)S(1)} %bitcast.45), channel_id=1, source_target_pairs={{480,0},{482,2},{484,4},{486,6},{488,8},{490,10},{492,12},{494,14}... | collective-permute-start | bytes 786440 | tf_op jit(solution)/shard_map/ppermute | solution.py:64
  19.2 3.4 %collective-permute-start.12 = (bf16[1024,128]{1,0:T(8,128)(2,1)S(1)}, bf16[1024,128]{1,0:T(8,128)(2,1)S(1)}, u32[]{:S(2)}, u32[]{:S(2)}) collective-permute-start(bf16[1024,128]{1,0:T(8,128)(2,1)S(1)} %bitcast.46), channel_id=1, source_target_pairs={{480,8},{482,10},{484,12},{486,14},{488,16},{490,18},{492,20},{494... | collective-permute-start | bytes 786440 | tf_op jit(solution)/shard_map/ppermute | solution.py:64
  22.6 6.6 %collective-permute-start.11 = (bf16[1024,128]{1,0:T(8,128)(2,1)S(1)}, bf16[1024,128]{1,0:T(8,128)(2,1)S(1)}, u32[]{:S(2)}, u32[]{:S(2)}) collective-permute-start(bf16[1024,128]{1,0:T(8,128)(2,1)S(1)} %bitcast.47), channel_id=1, source_target_pairs={{480,16},{482,18},{484,20},{486,22},{488,24},{490,26},{492,28},{49... | collective-permute-start | bytes 786440 | tf_op jit(solution)/shard_map/ppermute | solution.py:64
  29.2 3.2 %collective-permute-start.10 = (bf16[1024,128]{1,0:T(8,128)(2,1)S(1)}, bf16[1024,128]{1,0:T(8,128)(2,1)S(1)}, u32[]{:S(2)}, u32[]{:S(2)}) collective-permute-start(bf16[1024,128]{1,0:T(8,128)(2,1)S(1)} %bitcast.48), channel_id=1, source_target_pairs={{480,24},{482,26},{484,28},{486,30},{488,0},{490,2},{492,4},{494,6... | collective-permute-start | bytes 786440 | tf_op jit(solution)/shard_map/ppermute | solution.py:64
  32.9 1.8 %multiply_reduce_fusion = f32[384]{0:T(512)S(1)} fusion(bf16[1,384,2048]{2,1,0:T(8,128)(2,1)} %param.8), kind=kLoop, calls=%fused_computation | loop fusion | flops 2358912 | bytes 1574400 | tf_op jit(solution)/shard_map/reduce_sum | solution.py:288
  34.8 2.4 %collective-permute-done.10 = bf16[1024,128]{1,0:T(8,128)(2,1)S(1)} collective-permute-done((bf16[1024,128]{1,0:T(8,128)(2,1)S(1)}, bf16[1024,128]{1,0:T(8,128)(2,1)S(1)}, u32[]{:S(2)}, u32[]{:S(2)}) %collective-permute-start.10) | collective-permute-done | bytes 262176 | tf_op jit(solution)/shard_map/ppermute | solution.py:64
  38.3 2.2 %collective-permute-start.2 = (bf16[5376,128]{1,0:T(8,128)(2,1)S(1)}, bf16[5376,128]{1,0:T(8,128)(2,1)S(1)}, u32[]{:S(2)}, u32[]{:S(2)}) collective-permute-start(bf16[5376,128]{1,0:T(8,128)(2,1)S(1)} %bitcast.36), channel_id=1, source_target_pairs={{0,2},{2,4},{4,6},{6,0},{8,10},{10,12},{12,14},{14,8},{16,18},{18,... | collective-permute-start | bytes 4128776 | tf_op jit(solution)/shard_map/ppermute | solution.py:56
  40.5 4.3 %collective-permute-start.3 = (bf16[5376,128]{1,0:T(8,128)(2,1)S(1)}, bf16[5376,128]{1,0:T(8,128)(2,1)}, u32[]{:S(2)}, u32[]{:S(2)}) collective-permute-start(bf16[5376,128]{1,0:T(8,128)(2,1)S(1)} %bitcast.37), channel_id=1, source_target_pairs={{0,6},{2,0},{4,2},{6,4},{8,14},{10,8},{12,10},{14,12},{16,22},{18,... | collective-permute-start | bytes 4128776 | tf_op jit(solution)/shard_map/ppermute | solution.py:56
  44.8 3.6 %collective-permute-start.1 = (f32[24,128]{1,0:T(8,128)S(1)}, f32[24,128]{1,0:T(8,128)S(1)}, u32[]{:S(2)}, u32[]{:S(2)}) collective-permute-start(f32[24,128]{1,0:T(8,128)S(1)} %pad_bitcast_fusion), channel_id=1, source_target_pairs={{0,32},{32,64},{64,96},{96,128},{128,160},{160,192},{192,224},{224... | collective-permute-start | bytes 36872 | tf_op jit(solution)/shard_map/ppermute | solution.py:69
  48.4 6.9 %collective-permute-done.1 = f32[24,128]{1,0:T(8,128)S(1)} collective-permute-done((f32[24,128]{1,0:T(8,128)S(1)}, f32[24,128]{1,0:T(8,128)S(1)}, u32[]{:S(2)}, u32[]{:S(2)}) %collective-permute-start.1) | collective-permute-done | bytes 12320 | tf_op jit(solution)/shard_map/ppermute | solution.py:69
  55.3 1.9 %collective-permute-start.8 = (bf16[384,2048]{1,0:T(8,128)(2,1)}, bf16[384,2048]{1,0:T(8,128)(2,1)}, u32[]{:S(2)}, u32[]{:S(2)}) collective-permute-start(bf16[384,2048]{1,0:T(8,128)(2,1)} %bitcast.42), channel_id=1, source_target_pairs={{0,32},{32,64},{64,96},{96,128},{128,160},{160,192},{192,224},{224... | collective-permute-start | bytes 4718600 | tf_op jit(solution)/shard_map/ppermute | solution.py:69
  58.3 1.9 %collective-permute-start.4 = (s32[12]{0:T(128)S(1)}, s32[12]{0:T(128)S(1)}, u32[]{:S(2)}, u32[]{:S(2)}) collective-permute-start(s32[12]{0:T(128)S(1)} %add.116), channel_id=1, source_target_pairs={{0,0},{32,96},{64,64},{96,160},{128,128},{160,224},{192,192},{224,... | collective-permute-start | bytes 152 | tf_op jit(solution)/shard_map/ppermute | solution.py:74
  60.2 13.0 %collective-permute-start.7 = (f32[3,128]{1,0:T(4,128)S(1)}, f32[3,128]{1,0:T(4,128)S(1)}, u32[]{:S(2)}, u32[]{:S(2)}) collective-permute-start(f32[3,128]{1,0:T(4,128)S(1)} %slice_bitcast_fusion), channel_id=1, source_target_pairs={{0,1},{1,0},{2,3},{3,2},{4,5},{5,4},{6,7},{7,6},{8,9},{9,8},{10,11... | collective-permute-start | bytes 4616 | tf_op jit(solution)/shard_map/ppermute | solution.py:78
  73.3 19.4 %collective-permute-done.4 = s32[12]{0:T(128)S(1)} collective-permute-done((s32[12]{0:T(128)S(1)}, s32[12]{0:T(128)S(1)}, u32[]{:S(2)}, u32[]{:S(2)}) %collective-permute-start.4) | collective-permute-done | bytes 80 | tf_op jit(solution)/shard_map/ppermute | solution.py:74
  92.7 3.8 %collective-permute-start.5 = (bf16[2688,128]{1,0:T(8,128)(2,1)S(1)}, bf16[2688,128]{1,0:T(8,128)(2,1)S(1)}, u32[]{:S(2)}, u32[]{:S(2)}) collective-permute-start(bf16[2688,128]{1,0:T(8,128)(2,1)S(1)} %slice.42), channel_id=1, source_target_pairs={{0,2},{2,4},{4,6},{6,0},{8,10},{10,12},{12,14},{14,8},{16,18},{18,... | collective-permute-start | bytes 2064392 | tf_op jit(solution)/shard_map/ppermute | solution.py:56
  97.7 2.7 %collective-permute-start.6 = (bf16[2688,128]{1,0:T(8,128)(2,1)S(1)}, bf16[2688,128]{1,0:T(8,128)(2,1)S(1)}, u32[]{:S(2)}, u32[]{:S(2)}) collective-permute-start(bf16[2688,128]{1,0:T(8,128)(2,1)S(1)} %slice.43), channel_id=1, source_target_pairs={{0,6},{2,0},{4,2},{6,4},{8,14},{10,8},{12,10},{14,12},{16,22},{18,... | collective-permute-start | bytes 2064392 | tf_op jit(solution)/shard_map/ppermute | solution.py:56
  101.1 4.5 %collective-permute-done.5.ol_ref = bf16[2688,128]{1,0:T(8,128)(2,1)S(1)} collective-permute-done((bf16[2688,128]{1,0:T(8,128)(2,1)S(1)}, bf16[2688,128]{1,0:T(8,128)(2,1)S(1)}, u32[]{:S(2)}, u32[]{:S(2)}) %collective-permute-start.5) | collective-permute-done | bytes 688160 | tf_op jit(solution)/shard_map/ppermute | solution.py:56
  105.6 3.7 %collective-permute-done.6.or_ref = bf16[2688,128]{1,0:T(8,128)(2,1)S(1)} collective-permute-done((bf16[2688,128]{1,0:T(8,128)(2,1)S(1)}, bf16[2688,128]{1,0:T(8,128)(2,1)S(1)}, u32[]{:S(2)}, u32[]{:S(2)}) %collective-permute-start.6) | collective-permute-done | bytes 688160 | tf_op jit(solution)/shard_map/ppermute | solution.py:56
  109.3 2.5 %give_encodings.1 = bf16[12,256,128]{2,1,0:T(8,128)(2,1)S(1)} custom-call(s32[3,24]{1,0:T(4,128)S(1)} %add_add_fusion.table, bf16[5376,128]{1,0:T(8,128)(2,1)S(1)} %bitcast.38, bf16[5376,128]{1,0:T(8,128)(2,1)} %collective-permute-done.3.r_ref, bf16[2688,128]{1,0:T(8,128)(2,1)S(1)} %collective-permute-done.5.ol_ref, ...), custom_call_target="tpu_custom_call" | custom-call | tf_op jit(solution)/shard_map/give_encodings/pallas_call | solution.py:131
  111.8 1.9 %collective-permute-start.9 = (bf16[12,256,128]{2,1,0:T(8,128)(2,1)S(1)}, bf16[12,256,128]{2,1,0:T(8,128)(2,1)}, u32[]{:S(2)}, u32[]{:S(2)}) collective-permute-start(bf16[12,256,128]{2,1,0:T(8,128)(2,1)S(1)} %give_encodings.1), channel_id=1, source_target_pairs={{0,32},{32,0},{64,96},{96,64},{128,160},{160,128},{192,224},{224,1... | collective-permute-start | bytes 2359304 | tf_op jit(solution)/shard_map/ppermute | solution.py:83
  115.2 3.2 %pick_encodings.1.own_ref = bf16[768,512]{1,0:T(8,128)(2,1)S(1)} custom-call(s32[3,24]{1,0:T(4,128)S(1)} %add_add_fusion.table, bf16[5376,128]{1,0:T(8,128)(2,1)S(1)} %bitcast.39, bf16[5376,128]{1,0:T(8,128)(2,1)} %collective-permute-done.3.r_ref, bf16[2688,128]{1,0:T(8,128)(2,1)S(1)} %collective-permute-done.5.ol_ref, ...), custom_call_target="tpu_custom_call" | custom-call | tf_op jit(solution)/shard_map/pick_encodings/pallas_call | solution.py:143
  119.2 18.9 %attend_heads.1 = bf16[384,2048]{1,0:T(8,128)(2,1)} custom-call(s32[12]{0:T(128)} %get-tuple-element.42.live, s32[3,24]{1,0:T(4,128)} %copy-done.3, bf16[768,512]{1,0:T(8,128)(2,1)} %copy-done.2, bf16[12,256,128]{2,1,0:T(8,128)(2,1)} %collective-permute-done.9.slabs, bf16[512,512]{1,0:T(8,128)(2,1)} %fusion.spread, bf16[16,1024,128]{2,1,0:T(8,128)(2,1)} %bitcast.40, ...), custom_call_target="tpu_custom_call" | custom-call | tf_op jit(solution)/shard_map/attend_heads/pallas_call | solution.py:213
  (63 shorter events, 8.8 us)
Async XLA Ops:
  6.5 1.1 copy-start
  9.7 5.2 %copy-start.4 = (bf16[1,28,2048]{2,1,0:T(8,128)(2,1)S(1)}, bf16[1,28,2048]{2,1,0:T(8,128)(2,1)}, u32[]{:S(2)}) copy-start(bf16[1,28,2048]{2,1,0:T(8,128)(2,1)} %param.11) | copy-start | bytes 344068
  9.7 5.2 %copy-start.5 = (bf16[1,28,2048]{2,1,0:T(8,128)(2,1)S(1)}, bf16[1,28,2048]{2,1,0:T(8,128)(2,1)}, u32[]{:S(2)}) copy-start(bf16[1,28,2048]{2,1,0:T(8,128)(2,1)} %param.10) | copy-start | bytes 344068
  9.7 22.8 %copy-start.9 = (s32[1,6,2]{1,2,0:T(2,128)S(1)}, s32[1,6,2]{1,2,0:T(2,128)}, u32[]{:S(2)}) copy-start(s32[1,6,2]{1,2,0:T(2,128)} %param.14) | copy-start | bytes 148
  9.7 23.0 %copy-start.7 = (s32[1,6,2]{1,2,0:T(2,128)S(1)}, s32[1,6,2]{1,2,0:T(2,128)}, u32[]{:S(2)}) copy-start(s32[1,6,2]{1,2,0:T(2,128)} %param.13) | copy-start | bytes 148
  9.7 23.0 %copy-start.8 = (s32[1,6,2]{1,2,0:T(2,128)S(1)}, s32[1,6,2]{1,2,0:T(2,128)}, u32[]{:S(2)}) copy-start(s32[1,6,2]{1,2,0:T(2,128)} %param.12) | copy-start | bytes 148
  9.7 25.1 %all-to-all-start = ((bf16[4,1344,128]{2,1,0:T(8,128)(2,1)}), bf16[4,1344,128]{2,1,0:T(8,128)(2,1)S(1)}, u32[]{:S(2)}, u32[]{:S(2)}) async-start(bf16[4,1344,128]{2,1,0:T(8,128)(2,1)} %tile.9), calls=%async_computation | async-start | bytes 2752512 | tf_op jit(solution)/shard_map/all_to_all | solution.py:265
  14.8 104.4 %all-gather.2.cloned.1.call-start = ((), (), s32[]{:S(2)}) async-start(), calls=%async_computation.1 | async-start | bytes 5242880 | tf_op jit(solution)/shard_map/all_gather | solution.py:299
  14.8 19.8 %copy-start.6 = (f32[1,2048]{1,0:T(1,128)S(1)}, f32[1,2048]{1,0:T(1,128)}, u32[]{:S(2)}) copy-start(f32[1,2048]{1,0:T(1,128)} %param.9) | copy-start | bytes 24580
  15.0 19.8 %collective-permute-start = (bf16[1024,128]{1,0:T(8,128)(2,1)S(1)}, bf16[1024,128]{1,0:T(8,128)(2,1)S(1)}, u32[]{:S(2)}, u32[]{:S(2)}) collective-permute-start(bf16[1024,128]{1,0:T(8,128)(2,1)S(1)} %bitcast.45), channel_id=1, source_target_pairs={{480,0},{482,2},{484,4},{486,6},{488,8},{490,10},{492,12},{494,14}... | collective-permute-start | bytes 786440 | tf_op jit(solution)/shard_map/ppermute | solution.py:64
  19.2 15.5 %collective-permute-start.12 = (bf16[1024,128]{1,0:T(8,128)(2,1)S(1)}, bf16[1024,128]{1,0:T(8,128)(2,1)S(1)}, u32[]{:S(2)}, u32[]{:S(2)}) collective-permute-start(bf16[1024,128]{1,0:T(8,128)(2,1)S(1)} %bitcast.46), channel_id=1, source_target_pairs={{480,8},{482,10},{484,12},{486,14},{488,16},{490,18},{492,20},{494... | collective-permute-start | bytes 786440 | tf_op jit(solution)/shard_map/ppermute | solution.py:64
  22.6 12.2 %collective-permute-start.11 = (bf16[1024,128]{1,0:T(8,128)(2,1)S(1)}, bf16[1024,128]{1,0:T(8,128)(2,1)S(1)}, u32[]{:S(2)}, u32[]{:S(2)}) collective-permute-start(bf16[1024,128]{1,0:T(8,128)(2,1)S(1)} %bitcast.47), channel_id=1, source_target_pairs={{480,16},{482,18},{484,20},{486,22},{488,24},{490,26},{492,28},{49... | collective-permute-start | bytes 786440 | tf_op jit(solution)/shard_map/ppermute | solution.py:64
  29.2 8.0 %collective-permute-start.10 = (bf16[1024,128]{1,0:T(8,128)(2,1)S(1)}, bf16[1024,128]{1,0:T(8,128)(2,1)S(1)}, u32[]{:S(2)}, u32[]{:S(2)}) collective-permute-start(bf16[1024,128]{1,0:T(8,128)(2,1)S(1)} %bitcast.48), channel_id=1, source_target_pairs={{480,24},{482,26},{484,28},{486,30},{488,0},{490,2},{492,4},{494,6... | collective-permute-start | bytes 786440 | tf_op jit(solution)/shard_map/ppermute | solution.py:64
  38.3 54.4 %collective-permute-start.2 = (bf16[5376,128]{1,0:T(8,128)(2,1)S(1)}, bf16[5376,128]{1,0:T(8,128)(2,1)S(1)}, u32[]{:S(2)}, u32[]{:S(2)}) collective-permute-start(bf16[5376,128]{1,0:T(8,128)(2,1)S(1)} %bitcast.36), channel_id=1, source_target_pairs={{0,2},{2,4},{4,6},{6,0},{8,10},{10,12},{12,14},{14,8},{16,18},{18,... | collective-permute-start | bytes 4128776 | tf_op jit(solution)/shard_map/ppermute | solution.py:56
  40.5 52.2 %collective-permute-start.3 = (bf16[5376,128]{1,0:T(8,128)(2,1)S(1)}, bf16[5376,128]{1,0:T(8,128)(2,1)}, u32[]{:S(2)}, u32[]{:S(2)}) collective-permute-start(bf16[5376,128]{1,0:T(8,128)(2,1)S(1)} %bitcast.37), channel_id=1, source_target_pairs={{0,6},{2,0},{4,2},{6,4},{8,14},{10,8},{12,10},{14,12},{16,22},{18,... | collective-permute-start | bytes 4128776 | tf_op jit(solution)/shard_map/ppermute | solution.py:56
  44.8 10.5 %collective-permute-start.1 = (f32[24,128]{1,0:T(8,128)S(1)}, f32[24,128]{1,0:T(8,128)S(1)}, u32[]{:S(2)}, u32[]{:S(2)}) collective-permute-start(f32[24,128]{1,0:T(8,128)S(1)} %pad_bitcast_fusion), channel_id=1, source_target_pairs={{0,32},{32,64},{64,96},{96,128},{128,160},{160,192},{192,224},{224... | collective-permute-start | bytes 36872 | tf_op jit(solution)/shard_map/ppermute | solution.py:69
  55.3 56.5 %collective-permute-start.8 = (bf16[384,2048]{1,0:T(8,128)(2,1)}, bf16[384,2048]{1,0:T(8,128)(2,1)}, u32[]{:S(2)}, u32[]{:S(2)}) collective-permute-start(bf16[384,2048]{1,0:T(8,128)(2,1)} %bitcast.42), channel_id=1, source_target_pairs={{0,32},{32,64},{64,96},{96,128},{128,160},{160,192},{192,224},{224... | collective-permute-start | bytes 4718600 | tf_op jit(solution)/shard_map/ppermute | solution.py:69
  58.3 34.4 %collective-permute-start.4 = (s32[12]{0:T(128)S(1)}, s32[12]{0:T(128)S(1)}, u32[]{:S(2)}, u32[]{:S(2)}) collective-permute-start(s32[12]{0:T(128)S(1)} %add.116), channel_id=1, source_target_pairs={{0,0},{32,96},{64,64},{96,160},{128,128},{160,224},{192,192},{224,... | collective-permute-start | bytes 152 | tf_op jit(solution)/shard_map/ppermute | solution.py:74
  60.2 51.6 %collective-permute-start.7 = (f32[3,128]{1,0:T(4,128)S(1)}, f32[3,128]{1,0:T(4,128)S(1)}, u32[]{:S(2)}, u32[]{:S(2)}) collective-permute-start(f32[3,128]{1,0:T(4,128)S(1)} %slice_bitcast_fusion), channel_id=1, source_target_pairs={{0,1},{1,0},{2,3},{3,2},{4,5},{5,4},{6,7},{7,6},{8,9},{9,8},{10,11... | collective-permute-start | bytes 4616 | tf_op jit(solution)/shard_map/ppermute | solution.py:78
  92.7 12.9 %collective-permute-start.5 = (bf16[2688,128]{1,0:T(8,128)(2,1)S(1)}, bf16[2688,128]{1,0:T(8,128)(2,1)S(1)}, u32[]{:S(2)}, u32[]{:S(2)}) collective-permute-start(bf16[2688,128]{1,0:T(8,128)(2,1)S(1)} %slice.42), channel_id=1, source_target_pairs={{0,2},{2,4},{4,6},{6,0},{8,10},{10,12},{12,14},{14,8},{16,18},{18,... | collective-permute-start | bytes 2064392 | tf_op jit(solution)/shard_map/ppermute | solution.py:56
  97.7 11.7 %collective-permute-start.6 = (bf16[2688,128]{1,0:T(8,128)(2,1)S(1)}, bf16[2688,128]{1,0:T(8,128)(2,1)S(1)}, u32[]{:S(2)}, u32[]{:S(2)}) collective-permute-start(bf16[2688,128]{1,0:T(8,128)(2,1)S(1)} %slice.43), channel_id=1, source_target_pairs={{0,6},{2,0},{4,2},{6,4},{8,14},{10,8},{12,10},{14,12},{16,22},{18,... | collective-permute-start | bytes 2064392 | tf_op jit(solution)/shard_map/ppermute | solution.py:56
  101.1 14.1 %copy-start.3 = (s32[3,24]{1,0:T(4,128)}, s32[3,24]{1,0:T(4,128)S(1)}, u32[]{:S(2)}) copy-start(s32[3,24]{1,0:T(4,128)S(1)} %add_add_fusion.table) | copy-start | bytes 868
  101.1 14.1 %copy-start.1 = (bf16[512,512]{1,0:T(8,128)(2,1)S(1)}, bf16[512,512]{1,0:T(8,128)(2,1)}, u32[]{:S(2)}) copy-start(bf16[512,512]{1,0:T(8,128)(2,1)} %fusion.spread) | copy-start | bytes 1572868
  111.8 7.4 %collective-permute-start.9 = (bf16[12,256,128]{2,1,0:T(8,128)(2,1)S(1)}, bf16[12,256,128]{2,1,0:T(8,128)(2,1)}, u32[]{:S(2)}, u32[]{:S(2)}) collective-permute-start(bf16[12,256,128]{2,1,0:T(8,128)(2,1)S(1)} %give_encodings.1), channel_id=1, source_target_pairs={{0,32},{32,0},{64,96},{96,64},{128,160},{160,128},{192,224},{224,1... | collective-permute-start | bytes 2359304 | tf_op jit(solution)/shard_map/ppermute | solution.py:83
  (1 other events, 0.9 us)
Sparse Core Ops, SparseCore 0:
  38.4 47.3 all-gather.1

commit v6 on v5

--- a/solution.py
+++ b/solution.py
@@ -306,7 +306,7 @@
     d_before, d_after = turned(line_d, 1, 1), turned(line_d, -1, 1)
     info_here = to_next(info).reshape(-1)
     requests_other = to_next_other_core(requests)
-    info_here, rows = lax.optimization_barrier((info_here, rows))
+    info_here, requests_other, rows = lax.optimization_barrier((info_here, requests_other, rows))
     x_here = to_next(rows)
     spread = spread_of(core, place)
     d_before, d_after, spread, requests_other = lax.optimization_barrier((d_before, d_after, spread, requests_other))

time: 146 us -> 136 us (0.932)
  waiting for transfers between devices: 37 us -> 22.6 us
  starting transfers between devices: 57.9 us -> 62.2 us
    ppermute x1, waiting for transfers between devices: 19.4 us -> 12.3 us  [to_next_other_core(): lax.ppermute(value, 'segment', [(s, (s + 1) % count ^ 1) for s in range(c...]
    ppermute x2, waiting for transfers between devices: 6.9 us -> 0.01 us  [to_next(): lax.ppermute(value, 'segment', [(s, (s + 1) % count) for s in range(count)])]
    ppermute x1, starting transfers between devices: 1.91 us -> 4.75 us  [to_next_other_core(): lax.ppermute(value, 'segment', [(s, (s + 1) % count ^ 1) for s in range(c...]
    ppermute x1, starting transfers between devices: 1.92 us -> 3.39 us  [other_core(): return lax.ppermute(value, 'segment', [(s, s ^ 1) for s in range(count)])]
  transfers between devices with their start and end apart: 15 -> 15, of which waited for: 5 -> 4; matrix products, arithmetic and copies ran while one was open for 5% -> 5% of each run, Pallas kernels for 4% -> 4%
where the time goes in v6:
time: 136 us; the launch traced here: 135 us
  starting transfers between devices  62.2 us (46%)
  Pallas kernels  24.6 us (18%)
  waiting for transfers between devices  22.6 us (17%)
  between operations  13.7 us (10%)
  local copies, waits for them, and re-layouts  7 us (5%)
  other arithmetic  4.83 us (4%)
    pallas_call x1, Pallas kernels, attend(): pl.pallas_call(attend_kernel, grid_spec=pltpu.PrefetchScalarGridSpec(num_...  18.9 us
    ppermute x4, starting transfers between devices, to_next_turned(): return lax.ppermute(value, ('segment', 'db'), pairs)  17.5 us
    ppermute x4, starting transfers between devices, turned(): return lax.ppermute(value, ('segment', 'db'), pairs)  13 us
    ppermute x1, starting transfers between devices, other_mp(): return lax.ppermute(value, 'mp', [(0, 1), (1, 0)])  13 us
    ppermute x1, waiting for transfers between devices, to_next_other_core(): lax.ppermute(value, 'segment', [(s, (s + 1) % count ^ 1) for s in range(c...  12.3 us
    ppermute x4, waiting for transfers between devices, turned(): return lax.ppermute(value, ('segment', 'db'), pairs)  7.83 us
    ppermute x2, starting transfers between devices, to_next(): lax.ppermute(value, 'segment', [(s, (s + 1) % count) for s in range(count)])  5.48 us
    all_to_all x1, starting transfers between devices, first_ring(): lax.all_to_all(copies, ('segment', 'db'), split_axis=0, concat_axis=0, ti...  5.16 us
  transfers between devices with their start and end apart: 15, of which 4 were waited for; matrix products, arithmetic and copies ran while one was open for 5% of the time, Pallas kernels for 4%

profile of v6, /device:TPU:1, one launch (start us, length us, event | category | flops | bytes accessed | tf_op | source)
XLA Modules:
  0.0 135.0 jit_solution(12967943417457322825)
XLA Ops:
  8.4 1.3 tile.9
  9.7 5.2 %all-to-all-start = ((bf16[4,1344,128]{2,1,0:T(8,128)(2,1)}), bf16[4,1344,128]{2,1,0:T(8,128)(2,1)S(1)}, u32[]{:S(2)}, u32[]{:S(2)}) async-start(bf16[4,1344,128]{2,1,0:T(8,128)(2,1)} %tile.9), calls=%async_computation | async-start | bytes 2752512 | tf_op jit(solution)/shard_map/all_to_all | solution.py:265
  15.0 4.2 %collective-permute-start = (bf16[1024,128]{1,0:T(8,128)(2,1)S(1)}, bf16[1024,128]{1,0:T(8,128)(2,1)S(1)}, u32[]{:S(2)}, u32[]{:S(2)}) collective-permute-start(bf16[1024,128]{1,0:T(8,128)(2,1)S(1)} %bitcast.45), channel_id=1, source_target_pairs={{480,0},{482,2},{484,4},{486,6},{488,8},{490,10},{492,12},{494,14}... | collective-permute-start | bytes 786440 | tf_op jit(solution)/shard_map/ppermute | solution.py:64
  19.2 3.4 %collective-permute-start.12 = (bf16[1024,128]{1,0:T(8,128)(2,1)S(1)}, bf16[1024,128]{1,0:T(8,128)(2,1)S(1)}, u32[]{:S(2)}, u32[]{:S(2)}) collective-permute-start(bf16[1024,128]{1,0:T(8,128)(2,1)S(1)} %bitcast.46), channel_id=1, source_target_pairs={{480,8},{482,10},{484,12},{486,14},{488,16},{490,18},{492,20},{494... | collective-permute-start | bytes 786440 | tf_op jit(solution)/shard_map/ppermute | solution.py:64
  22.6 6.6 %collective-permute-start.11 = (bf16[1024,128]{1,0:T(8,128)(2,1)S(1)}, bf16[1024,128]{1,0:T(8,128)(2,1)S(1)}, u32[]{:S(2)}, u32[]{:S(2)}) collective-permute-start(bf16[1024,128]{1,0:T(8,128)(2,1)S(1)} %bitcast.47), channel_id=1, source_target_pairs={{480,16},{482,18},{484,20},{486,22},{488,24},{490,26},{492,28},{49... | collective-permute-start | bytes 786440 | tf_op jit(solution)/shard_map/ppermute | solution.py:64
  29.2 3.2 %collective-permute-start.10 = (bf16[1024,128]{1,0:T(8,128)(2,1)S(1)}, bf16[1024,128]{1,0:T(8,128)(2,1)S(1)}, u32[]{:S(2)}, u32[]{:S(2)}) collective-permute-start(bf16[1024,128]{1,0:T(8,128)(2,1)S(1)} %bitcast.48), channel_id=1, source_target_pairs={{480,24},{482,26},{484,28},{486,30},{488,0},{490,2},{492,4},{494,6... | collective-permute-start | bytes 786440 | tf_op jit(solution)/shard_map/ppermute | solution.py:64
  32.9 1.8 %multiply_reduce_fusion = f32[384]{0:T(512)S(1)} fusion(bf16[1,384,2048]{2,1,0:T(8,128)(2,1)} %param.8), kind=kLoop, calls=%fused_computation | loop fusion | flops 2358912 | bytes 1574400 | tf_op jit(solution)/shard_map/reduce_sum | solution.py:288
  34.8 2.4 %collective-permute-done.10 = bf16[1024,128]{1,0:T(8,128)(2,1)S(1)} collective-permute-done((bf16[1024,128]{1,0:T(8,128)(2,1)S(1)}, bf16[1024,128]{1,0:T(8,128)(2,1)S(1)}, u32[]{:S(2)}, u32[]{:S(2)}) %collective-permute-start.10) | collective-permute-done | bytes 262176 | tf_op jit(solution)/shard_map/ppermute | solution.py:64
  38.3 2.2 %collective-permute-start.3 = (bf16[5376,128]{1,0:T(8,128)(2,1)S(1)}, bf16[5376,128]{1,0:T(8,128)(2,1)S(1)}, u32[]{:S(2)}, u32[]{:S(2)}) collective-permute-start(bf16[5376,128]{1,0:T(8,128)(2,1)S(1)} %bitcast.36), channel_id=1, source_target_pairs={{0,2},{2,4},{4,6},{6,0},{8,10},{10,12},{12,14},{14,8},{16,18},{18,... | collective-permute-start | bytes 4128776 | tf_op jit(solution)/shard_map/ppermute | solution.py:56
  40.5 4.3 %collective-permute-start.4 = (bf16[5376,128]{1,0:T(8,128)(2,1)S(1)}, bf16[5376,128]{1,0:T(8,128)(2,1)}, u32[]{:S(2)}, u32[]{:S(2)}) collective-permute-start(bf16[5376,128]{1,0:T(8,128)(2,1)S(1)} %bitcast.37), channel_id=1, source_target_pairs={{0,6},{2,0},{4,2},{6,4},{8,14},{10,8},{12,10},{14,12},{16,22},{18,... | collective-permute-start | bytes 4128776 | tf_op jit(solution)/shard_map/ppermute | solution.py:56
  44.8 3.6 %collective-permute-start.1 = (f32[24,128]{1,0:T(8,128)S(1)}, f32[24,128]{1,0:T(8,128)S(1)}, u32[]{:S(2)}, u32[]{:S(2)}) collective-permute-start(f32[24,128]{1,0:T(8,128)S(1)} %pad_bitcast_fusion), channel_id=1, source_target_pairs={{0,32},{32,64},{64,96},{96,128},{128,160},{160,192},{192,224},{224... | collective-permute-start | bytes 36872 | tf_op jit(solution)/shard_map/ppermute | solution.py:69
  48.4 4.8 %collective-permute-start.2 = (s32[12]{0:T(128)S(1)}, s32[12]{0:T(128)S(1)}, u32[]{:S(2)}, u32[]{:S(2)}) collective-permute-start(s32[12]{0:T(128)S(1)} %add.116), channel_id=1, source_target_pairs={{0,0},{32,96},{64,64},{96,160},{128,128},{160,224},{192,192},{224,... | collective-permute-start | bytes 152 | tf_op jit(solution)/shard_map/ppermute | solution.py:74
  53.2 12.3 %collective-permute-done.2 = s32[12]{0:T(128)S(1)} collective-permute-done((s32[12]{0:T(128)S(1)}, s32[12]{0:T(128)S(1)}, u32[]{:S(2)}, u32[]{:S(2)}) %collective-permute-start.2) | collective-permute-done | bytes 80 | tf_op jit(solution)/shard_map/ppermute | solution.py:74
  65.5 1.9 %collective-permute-start.8 = (bf16[384,2048]{1,0:T(8,128)(2,1)}, bf16[384,2048]{1,0:T(8,128)(2,1)}, u32[]{:S(2)}, u32[]{:S(2)}) collective-permute-start(bf16[384,2048]{1,0:T(8,128)(2,1)} %bitcast.42), channel_id=1, source_target_pairs={{0,32},{32,64},{64,96},{96,128},{128,160},{160,192},{192,224},{224... | collective-permute-start | bytes 4718600 | tf_op jit(solution)/shard_map/ppermute | solution.py:69
  68.4 13.0 %collective-permute-start.7 = (f32[3,128]{1,0:T(4,128)S(1)}, f32[3,128]{1,0:T(4,128)S(1)}, u32[]{:S(2)}, u32[]{:S(2)}) collective-permute-start(f32[3,128]{1,0:T(4,128)S(1)} %slice_bitcast_fusion), channel_id=1, source_target_pairs={{0,1},{1,0},{2,3},{3,2},{4,5},{5,4},{6,7},{7,6},{8,9},{9,8},{10,11... | collective-permute-start | bytes 4616 | tf_op jit(solution)/shard_map/ppermute | solution.py:78
  81.6 3.1 %collective-permute-start.5 = (bf16[2688,128]{1,0:T(8,128)(2,1)S(1)}, bf16[2688,128]{1,0:T(8,128)(2,1)S(1)}, u32[]{:S(2)}, u32[]{:S(2)}) collective-permute-start(bf16[2688,128]{1,0:T(8,128)(2,1)S(1)} %slice.42), channel_id=1, source_target_pairs={{0,2},{2,4},{4,6},{6,0},{8,10},{10,12},{12,14},{14,8},{16,18},{18,... | collective-permute-start | bytes 2064392 | tf_op jit(solution)/shard_map/ppermute | solution.py:56
  84.7 1.1 slice.43
  85.8 3.4 %collective-permute-start.6 = (bf16[2688,128]{1,0:T(8,128)(2,1)S(1)}, bf16[2688,128]{1,0:T(8,128)(2,1)S(1)}, u32[]{:S(2)}, u32[]{:S(2)}) collective-permute-start(bf16[2688,128]{1,0:T(8,128)(2,1)S(1)} %slice.43), channel_id=1, source_target_pairs={{0,6},{2,0},{4,2},{6,4},{8,14},{10,8},{12,10},{14,12},{16,22},{18,... | collective-permute-start | bytes 2064392 | tf_op jit(solution)/shard_map/ppermute | solution.py:56
  90.0 4.8 %collective-permute-done.5.ol_ref = bf16[2688,128]{1,0:T(8,128)(2,1)S(1)} collective-permute-done((bf16[2688,128]{1,0:T(8,128)(2,1)S(1)}, bf16[2688,128]{1,0:T(8,128)(2,1)S(1)}, u32[]{:S(2)}, u32[]{:S(2)}) %collective-permute-start.5) | collective-permute-done | bytes 688160 | tf_op jit(solution)/shard_map/ppermute | solution.py:56
  94.8 3.0 %collective-permute-done.6.or_ref = bf16[2688,128]{1,0:T(8,128)(2,1)S(1)} collective-permute-done((bf16[2688,128]{1,0:T(8,128)(2,1)S(1)}, bf16[2688,128]{1,0:T(8,128)(2,1)S(1)}, u32[]{:S(2)}, u32[]{:S(2)}) %collective-permute-start.6) | collective-permute-done | bytes 688160 | tf_op jit(solution)/shard_map/ppermute | solution.py:56
  97.8 2.5 %give_encodings.1 = bf16[12,256,128]{2,1,0:T(8,128)(2,1)S(1)} custom-call(s32[3,24]{1,0:T(4,128)S(1)} %add_add_fusion.table, bf16[5376,128]{1,0:T(8,128)(2,1)S(1)} %bitcast.38, bf16[5376,128]{1,0:T(8,128)(2,1)} %collective-permute-done.4.r_ref, bf16[2688,128]{1,0:T(8,128)(2,1)S(1)} %collective-permute-done.5.ol_ref, ...), custom_call_target="tpu_custom_call" | custom-call | tf_op jit(solution)/shard_map/give_encodings/pallas_call | solution.py:131
  100.4 3.4 %collective-permute-start.9 = (bf16[12,256,128]{2,1,0:T(8,128)(2,1)S(1)}, bf16[12,256,128]{2,1,0:T(8,128)(2,1)}, u32[]{:S(2)}, u32[]{:S(2)}) collective-permute-start(bf16[12,256,128]{2,1,0:T(8,128)(2,1)S(1)} %give_encodings.1), channel_id=1, source_target_pairs={{0,32},{32,0},{64,96},{96,64},{128,160},{160,128},{192,224},{224,1... | collective-permute-start | bytes 2359304 | tf_op jit(solution)/shard_map/ppermute | solution.py:83
  105.2 3.2 %pick_encodings.1.own_ref = bf16[768,512]{1,0:T(8,128)(2,1)S(1)} custom-call(s32[3,24]{1,0:T(4,128)S(1)} %add_add_fusion.table, bf16[5376,128]{1,0:T(8,128)(2,1)S(1)} %bitcast.39, bf16[5376,128]{1,0:T(8,128)(2,1)} %collective-permute-done.4.r_ref, bf16[2688,128]{1,0:T(8,128)(2,1)S(1)} %collective-permute-done.5.ol_ref, ...), custom_call_target="tpu_custom_call" | custom-call | tf_op jit(solution)/shard_map/pick_encodings/pallas_call | solution.py:143
  109.3 18.9 %attend_heads.1 = bf16[384,2048]{1,0:T(8,128)(2,1)} custom-call(s32[12]{0:T(128)} %get-tuple-element.44.live, s32[3,24]{1,0:T(4,128)} %copy-done.3, bf16[768,512]{1,0:T(8,128)(2,1)} %copy-done.2, bf16[12,256,128]{2,1,0:T(8,128)(2,1)} %collective-permute-done.9.slabs, bf16[512,512]{1,0:T(8,128)(2,1)} %fusion.spread, bf16[16,1024,128]{2,1,0:T(8,128)(2,1)} %bitcast.40, ...), custom_call_target="tpu_custom_call" | custom-call | tf_op jit(solution)/shard_map/attend_heads/pallas_call | solution.py:213
  (63 shorter events, 7.7 us)
Async XLA Ops:
  6.5 1.1 copy-start
  9.7 5.2 %copy-start.4 = (bf16[1,28,2048]{2,1,0:T(8,128)(2,1)S(1)}, bf16[1,28,2048]{2,1,0:T(8,128)(2,1)}, u32[]{:S(2)}) copy-start(bf16[1,28,2048]{2,1,0:T(8,128)(2,1)} %param.11) | copy-start | bytes 344068
  9.7 5.2 %copy-start.5 = (bf16[1,28,2048]{2,1,0:T(8,128)(2,1)S(1)}, bf16[1,28,2048]{2,1,0:T(8,128)(2,1)}, u32[]{:S(2)}) copy-start(bf16[1,28,2048]{2,1,0:T(8,128)(2,1)} %param.10) | copy-start | bytes 344068
  9.7 22.8 %copy-start.9 = (s32[1,6,2]{1,2,0:T(2,128)S(1)}, s32[1,6,2]{1,2,0:T(2,128)}, u32[]{:S(2)}) copy-start(s32[1,6,2]{1,2,0:T(2,128)} %param.14) | copy-start | bytes 148
  9.7 23.0 %copy-start.7 = (s32[1,6,2]{1,2,0:T(2,128)S(1)}, s32[1,6,2]{1,2,0:T(2,128)}, u32[]{:S(2)}) copy-start(s32[1,6,2]{1,2,0:T(2,128)} %param.13) | copy-start | bytes 148
  9.7 23.0 %copy-start.8 = (s32[1,6,2]{1,2,0:T(2,128)S(1)}, s32[1,6,2]{1,2,0:T(2,128)}, u32[]{:S(2)}) copy-start(s32[1,6,2]{1,2,0:T(2,128)} %param.12) | copy-start | bytes 148
  9.7 25.1 %all-to-all-start = ((bf16[4,1344,128]{2,1,0:T(8,128)(2,1)}), bf16[4,1344,128]{2,1,0:T(8,128)(2,1)S(1)}, u32[]{:S(2)}, u32[]{:S(2)}) async-start(bf16[4,1344,128]{2,1,0:T(8,128)(2,1)} %tile.9), calls=%async_computation | async-start | bytes 2752512 | tf_op jit(solution)/shard_map/all_to_all | solution.py:265
  14.8 94.4 %all-gather.2.cloned.1.call-start = ((), (), s32[]{:S(2)}) async-start(), calls=%async_computation.1 | async-start | bytes 5242880 | tf_op jit(solution)/shard_map/all_gather | solution.py:299
  14.8 19.8 %copy-start.6 = (f32[1,2048]{1,0:T(1,128)S(1)}, f32[1,2048]{1,0:T(1,128)}, u32[]{:S(2)}) copy-start(f32[1,2048]{1,0:T(1,128)} %param.9) | copy-start | bytes 24580
  15.0 19.8 %collective-permute-start = (bf16[1024,128]{1,0:T(8,128)(2,1)S(1)}, bf16[1024,128]{1,0:T(8,128)(2,1)S(1)}, u32[]{:S(2)}, u32[]{:S(2)}) collective-permute-start(bf16[1024,128]{1,0:T(8,128)(2,1)S(1)} %bitcast.45), channel_id=1, source_target_pairs={{480,0},{482,2},{484,4},{486,6},{488,8},{490,10},{492,12},{494,14}... | collective-permute-start | bytes 786440 | tf_op jit(solution)/shard_map/ppermute | solution.py:64
  19.2 15.5 %collective-permute-start.12 = (bf16[1024,128]{1,0:T(8,128)(2,1)S(1)}, bf16[1024,128]{1,0:T(8,128)(2,1)S(1)}, u32[]{:S(2)}, u32[]{:S(2)}) collective-permute-start(bf16[1024,128]{1,0:T(8,128)(2,1)S(1)} %bitcast.46), channel_id=1, source_target_pairs={{480,8},{482,10},{484,12},{486,14},{488,16},{490,18},{492,20},{494... | collective-permute-start | bytes 786440 | tf_op jit(solution)/shard_map/ppermute | solution.py:64
  22.6 12.2 %collective-permute-start.11 = (bf16[1024,128]{1,0:T(8,128)(2,1)S(1)}, bf16[1024,128]{1,0:T(8,128)(2,1)S(1)}, u32[]{:S(2)}, u32[]{:S(2)}) collective-permute-start(bf16[1024,128]{1,0:T(8,128)(2,1)S(1)} %bitcast.47), channel_id=1, source_target_pairs={{480,16},{482,18},{484,20},{486,22},{488,24},{490,26},{492,28},{49... | collective-permute-start | bytes 786440 | tf_op jit(solution)/shard_map/ppermute | solution.py:64
  29.2 8.0 %collective-permute-start.10 = (bf16[1024,128]{1,0:T(8,128)(2,1)S(1)}, bf16[1024,128]{1,0:T(8,128)(2,1)S(1)}, u32[]{:S(2)}, u32[]{:S(2)}) collective-permute-start(bf16[1024,128]{1,0:T(8,128)(2,1)S(1)} %bitcast.48), channel_id=1, source_target_pairs={{480,24},{482,26},{484,28},{486,30},{488,0},{490,2},{492,4},{494,6... | collective-permute-start | bytes 786440 | tf_op jit(solution)/shard_map/ppermute | solution.py:64
  38.3 43.2 %collective-permute-start.3 = (bf16[5376,128]{1,0:T(8,128)(2,1)S(1)}, bf16[5376,128]{1,0:T(8,128)(2,1)S(1)}, u32[]{:S(2)}, u32[]{:S(2)}) collective-permute-start(bf16[5376,128]{1,0:T(8,128)(2,1)S(1)} %bitcast.36), channel_id=1, source_target_pairs={{0,2},{2,4},{4,6},{6,0},{8,10},{10,12},{12,14},{14,8},{16,18},{18,... | collective-permute-start | bytes 4128776 | tf_op jit(solution)/shard_map/ppermute | solution.py:56
  40.5 41.0 %collective-permute-start.4 = (bf16[5376,128]{1,0:T(8,128)(2,1)S(1)}, bf16[5376,128]{1,0:T(8,128)(2,1)}, u32[]{:S(2)}, u32[]{:S(2)}) collective-permute-start(bf16[5376,128]{1,0:T(8,128)(2,1)S(1)} %bitcast.37), channel_id=1, source_target_pairs={{0,6},{2,0},{4,2},{6,4},{8,14},{10,8},{12,10},{14,12},{16,22},{18,... | collective-permute-start | bytes 4128776 | tf_op jit(solution)/shard_map/ppermute | solution.py:56
  44.8 20.7 %collective-permute-start.1 = (f32[24,128]{1,0:T(8,128)S(1)}, f32[24,128]{1,0:T(8,128)S(1)}, u32[]{:S(2)}, u32[]{:S(2)}) collective-permute-start(f32[24,128]{1,0:T(8,128)S(1)} %pad_bitcast_fusion), channel_id=1, source_target_pairs={{0,32},{32,64},{64,96},{96,128},{128,160},{160,192},{192,224},{224... | collective-permute-start | bytes 36872 | tf_op jit(solution)/shard_map/ppermute | solution.py:69
  48.4 17.1 %collective-permute-start.2 = (s32[12]{0:T(128)S(1)}, s32[12]{0:T(128)S(1)}, u32[]{:S(2)}, u32[]{:S(2)}) collective-permute-start(s32[12]{0:T(128)S(1)} %add.116), channel_id=1, source_target_pairs={{0,0},{32,96},{64,64},{96,160},{128,128},{160,224},{192,192},{224,... | collective-permute-start | bytes 152 | tf_op jit(solution)/shard_map/ppermute | solution.py:74
  65.5 34.8 %collective-permute-start.8 = (bf16[384,2048]{1,0:T(8,128)(2,1)}, bf16[384,2048]{1,0:T(8,128)(2,1)}, u32[]{:S(2)}, u32[]{:S(2)}) collective-permute-start(bf16[384,2048]{1,0:T(8,128)(2,1)} %bitcast.42), channel_id=1, source_target_pairs={{0,32},{32,64},{64,96},{96,128},{128,160},{160,192},{192,224},{224... | collective-permute-start | bytes 4718600 | tf_op jit(solution)/shard_map/ppermute | solution.py:69
  68.4 31.9 %collective-permute-start.7 = (f32[3,128]{1,0:T(4,128)S(1)}, f32[3,128]{1,0:T(4,128)S(1)}, u32[]{:S(2)}, u32[]{:S(2)}) collective-permute-start(f32[3,128]{1,0:T(4,128)S(1)} %slice_bitcast_fusion), channel_id=1, source_target_pairs={{0,1},{1,0},{2,3},{3,2},{4,5},{5,4},{6,7},{7,6},{8,9},{9,8},{10,11... | collective-permute-start | bytes 4616 | tf_op jit(solution)/shard_map/ppermute | solution.py:78
  81.6 13.2 %collective-permute-start.5 = (bf16[2688,128]{1,0:T(8,128)(2,1)S(1)}, bf16[2688,128]{1,0:T(8,128)(2,1)S(1)}, u32[]{:S(2)}, u32[]{:S(2)}) collective-permute-start(bf16[2688,128]{1,0:T(8,128)(2,1)S(1)} %slice.42), channel_id=1, source_target_pairs={{0,2},{2,4},{4,6},{6,0},{8,10},{10,12},{12,14},{14,8},{16,18},{18,... | collective-permute-start | bytes 2064392 | tf_op jit(solution)/shard_map/ppermute | solution.py:56
  85.8 12.0 %collective-permute-start.6 = (bf16[2688,128]{1,0:T(8,128)(2,1)S(1)}, bf16[2688,128]{1,0:T(8,128)(2,1)S(1)}, u32[]{:S(2)}, u32[]{:S(2)}) collective-permute-start(bf16[2688,128]{1,0:T(8,128)(2,1)S(1)} %slice.43), channel_id=1, source_target_pairs={{0,6},{2,0},{4,2},{6,4},{8,14},{10,8},{12,10},{14,12},{16,22},{18,... | collective-permute-start | bytes 2064392 | tf_op jit(solution)/shard_map/ppermute | solution.py:56
  90.0 15.2 %copy-start.3 = (s32[3,24]{1,0:T(4,128)}, s32[3,24]{1,0:T(4,128)S(1)}, u32[]{:S(2)}) copy-start(s32[3,24]{1,0:T(4,128)S(1)} %add_add_fusion.table) | copy-start | bytes 868
  90.0 15.2 %copy-start.1 = (bf16[512,512]{1,0:T(8,128)(2,1)S(1)}, bf16[512,512]{1,0:T(8,128)(2,1)}, u32[]{:S(2)}) copy-start(bf16[512,512]{1,0:T(8,128)(2,1)} %fusion.spread) | copy-start | bytes 1572868
  100.4 8.9 %collective-permute-start.9 = (bf16[12,256,128]{2,1,0:T(8,128)(2,1)S(1)}, bf16[12,256,128]{2,1,0:T(8,128)(2,1)}, u32[]{:S(2)}, u32[]{:S(2)}) collective-permute-start(bf16[12,256,128]{2,1,0:T(8,128)(2,1)S(1)} %give_encodings.1), channel_id=1, source_target_pairs={{0,32},{32,0},{64,96},{96,64},{128,160},{160,128},{192,224},{224,1... | collective-permute-start | bytes 2359304 | tf_op jit(solution)/shard_map/ppermute | solution.py:83
  (1 other events, 0.9 us)
Sparse Core Ops, SparseCore 0:
  38.4 47.3 all-gather.1

commit v7 on v6

--- a/solution.py
+++ b/solution.py
@@ -69,13 +69,10 @@
     return lax.ppermute(value, "segment", [(s, (s + 1) % count) for s in range(count)])
 
 
-def to_next_other_core(value):
+def to_next_other_mp(value):
     count = lax.axis_size("segment")
-    return lax.ppermute(value, "segment", [(s, ((s + 1) % count) ^ 1) for s in range(count)])
-
-
-def other_mp(value):
-    return lax.ppermute(value, "mp", [(0, 1), (1, 0)])
+    pairs = [(s * 2 + m, ((s + 1) % count) * 2 + 1 - m) for s in range(count) for m in range(2)]
+    return lax.ppermute(value, ("segment", "mp"), pairs)
 
 
 def other_core(value):
@@ -293,8 +290,8 @@
     info = jnp.pad(info, (0, -info.shape[0] % 1024)).reshape(-1, HD)
 
     pieces_w = [to_next_turned(packed_w, turn) for turn in (0, -1, 2, 1)]
-    pieces_w[0], line_d, info, requests = lax.optimization_barrier(
-        (pieces_w[0], first_ring(packed_d), info, requests)
+    pieces_w[0], line_d, info, squares = lax.optimization_barrier(
+        (pieces_w[0], first_ring(packed_d), info, squares)
     )
     all_w = lax.all_gather(
         jnp.concatenate(pieces_w, axis=0),
@@ -305,24 +302,24 @@
     ).reshape(RING, W_ROWS, HD)
     d_before, d_after = turned(line_d, 1, 1), turned(line_d, -1, 1)
     info_here = to_next(info).reshape(-1)
-    requests_other = to_next_other_core(requests)
-    info_here, requests_other, rows = lax.optimization_barrier((info_here, requests_other, rows))
+    squares_other = to_next_other_mp(squares.reshape(-1, HD)).reshape(-1)
+    squares_here = info_here[:tokens]
+    gain_here = info_here[tokens:tokens + local_width]
+    ints = info_here[tokens + local_width:tokens + local_width + 2 * REQ].astype(jnp.int32)
+    live, requests_here = ints[:REQ], ints[REQ:]
+    requests_other = other_core(requests_here)
+    requests_other, squares_other, rows = lax.optimization_barrier((requests_other, squares_other, rows))
     x_here = to_next(rows)
     spread = spread_of(core, place)
     d_before, d_after, spread, requests_other = lax.optimization_barrier((d_before, d_after, spread, requests_other))
     mid_d = line_d.shape[0] // 2
     d_pieces = (line_d, d_after, turned(d_before[:mid_d], 1, 1), turned(d_after[mid_d:], -1, 1), d_before)
 
-    squares_here = info_here[:tokens]
-    squares_other = other_mp(squares_here.reshape(-1, HD)).reshape(-1)
-    gain_here = info_here[tokens:tokens + local_width]
-    ints = info_here[tokens + local_width:tokens + local_width + 2 * REQ].astype(jnp.int32)
-    live, requests_here = ints[:REQ], ints[REQ:]
     table = jnp.concatenate(
         [source_table(requests_here, core, place), source_table(requests_other, core, place)], axis=1
     )
 
-    given, squares_other, x_here = lax.optimization_barrier((give(table, d_pieces), squares_other, x_here))
+    given, x_here = lax.optimization_barrier((give(table, d_pieces), x_here))
     slabs = other_core(given)
     own = pick(table, d_pieces, spread)
     inv_rms = lax.rsqrt((squares_here + squares_other) / full_width + eps_norm)

time: 136 us -> 135 us (level); the launches traced: 135 us -> 133 us
  waiting for transfers between devices: 22.6 us -> 20.6 us
    ppermute x2 -> x1, waiting for transfers between devices: 12.3 us -> 4.67 us  [to_next_other_mp(): return lax.ppermute(value, ('segment', 'mp'), pairs)]
    ppermute x1 -> x2, starting transfers between devices: 3.39 us -> 9.53 us  [other_core(): return lax.ppermute(value, 'segment', [(s, s ^ 1) for s in range(count)])]
    ppermute x4, waiting for transfers between devices: 7.83 us -> 13.4 us  [turned(): return lax.ppermute(value, ('segment', 'db'), pairs)]
    ppermute x2 -> x1, starting transfers between devices: 17.7 us -> 12.8 us  [to_next_other_mp(): return lax.ppermute(value, ('segment', 'mp'), pairs)]
  transfers between devices with their start and end apart: 15 -> 15, of which waited for: 4 -> 4; matrix products, arithmetic and copies ran while one was open for 5% -> 4% of each run, Pallas kernels for 4% -> 4%
where the time goes in v7:
time: 135 us; the launch traced here: 133 us
  starting transfers between devices  62.9 us (47%)
  Pallas kernels  24.4 us (18%)
  waiting for transfers between devices  20.6 us (15%)
  between operations  13.8 us (10%)
  local copies, waits for them, and re-layouts  7.01 us (5%)
  other arithmetic  3.98 us (3%)
    pallas_call x1, Pallas kernels, attend(): pl.pallas_call(attend_kernel, grid_spec=pltpu.PrefetchScalarGridSpec(num_...  18.9 us
    ppermute x4, starting transfers between devices, to_next_turned(): return lax.ppermute(value, ('segment', 'db'), pairs)  17.5 us
    ppermute x4, waiting for transfers between devices, turned(): return lax.ppermute(value, ('segment', 'db'), pairs)  13.4 us
    ppermute x4, starting transfers between devices, turned(): return lax.ppermute(value, ('segment', 'db'), pairs)  13 us
    ppermute x1, starting transfers between devices, to_next_other_mp(): return lax.ppermute(value, ('segment', 'mp'), pairs)  12.8 us
    ppermute x2, starting transfers between devices, other_core(): return lax.ppermute(value, 'segment', [(s, s ^ 1) for s in range(count)])  9.53 us
    all_to_all x1, starting transfers between devices, first_ring(): lax.all_to_all(copies, ('segment', 'db'), split_axis=0, concat_axis=0, ti...  5.16 us
    ppermute x2, starting transfers between devices, to_next(): lax.ppermute(value, 'segment', [(s, (s + 1) % count) for s in range(count)])  4.92 us
  transfers between devices with their start and end apart: 15, of which 4 were waited for; matrix products, arithmetic and copies ran while one was open for 4% of the time, Pallas kernels for 4%

profile of v7, /device:TPU:1, one launch (start us, length us, event | category | flops | bytes accessed | tf_op | source)
XLA Modules:
  0.0 132.6 jit_solution(10443039971988260625)
XLA Ops:
  6.5 1.1 copy-done
  8.4 1.3 tile.9
  9.7 5.2 %all-to-all-start = ((bf16[4,1344,128]{2,1,0:T(8,128)(2,1)}), bf16[4,1344,128]{2,1,0:T(8,128)(2,1)S(1)}, u32[]{:S(2)}, u32[]{:S(2)}) async-start(bf16[4,1344,128]{2,1,0:T(8,128)(2,1)} %tile.9), calls=%async_computation | async-start | bytes 2752512 | tf_op jit(solution)/shard_map/all_to_all | solution.py:262
  15.0 4.2 %collective-permute-start = (bf16[1024,128]{1,0:T(8,128)(2,1)S(1)}, bf16[1024,128]{1,0:T(8,128)(2,1)S(1)}, u32[]{:S(2)}, u32[]{:S(2)}) collective-permute-start(bf16[1024,128]{1,0:T(8,128)(2,1)S(1)} %bitcast.54), channel_id=1, source_target_pairs={{480,0},{482,2},{484,4},{486,6},{488,8},{490,10},{492,12},{494,14}... | collective-permute-start | bytes 786440 | tf_op jit(solution)/shard_map/ppermute | solution.py:64
  19.2 3.4 %collective-permute-start.12 = (bf16[1024,128]{1,0:T(8,128)(2,1)S(1)}, bf16[1024,128]{1,0:T(8,128)(2,1)S(1)}, u32[]{:S(2)}, u32[]{:S(2)}) collective-permute-start(bf16[1024,128]{1,0:T(8,128)(2,1)S(1)} %bitcast.55), channel_id=1, source_target_pairs={{480,8},{482,10},{484,12},{486,14},{488,16},{490,18},{492,20},{494... | collective-permute-start | bytes 786440 | tf_op jit(solution)/shard_map/ppermute | solution.py:64
  22.6 6.6 %collective-permute-start.11 = (bf16[1024,128]{1,0:T(8,128)(2,1)S(1)}, bf16[1024,128]{1,0:T(8,128)(2,1)S(1)}, u32[]{:S(2)}, u32[]{:S(2)}) collective-permute-start(bf16[1024,128]{1,0:T(8,128)(2,1)S(1)} %bitcast.56), channel_id=1, source_target_pairs={{480,16},{482,18},{484,20},{486,22},{488,24},{490,26},{492,28},{49... | collective-permute-start | bytes 786440 | tf_op jit(solution)/shard_map/ppermute | solution.py:64
  29.2 3.2 %collective-permute-start.10 = (bf16[1024,128]{1,0:T(8,128)(2,1)S(1)}, bf16[1024,128]{1,0:T(8,128)(2,1)S(1)}, u32[]{:S(2)}, u32[]{:S(2)}) collective-permute-start(bf16[1024,128]{1,0:T(8,128)(2,1)S(1)} %bitcast.57), channel_id=1, source_target_pairs={{480,24},{482,26},{484,28},{486,30},{488,0},{490,2},{492,4},{494,6... | collective-permute-start | bytes 786440 | tf_op jit(solution)/shard_map/ppermute | solution.py:64
  32.9 1.8 %multiply_reduce_fusion = f32[384]{0:T(512)S(1)} fusion(bf16[1,384,2048]{2,1,0:T(8,128)(2,1)} %param.8), kind=kLoop, calls=%fused_computation | loop fusion | flops 2358912 | bytes 1574400 | tf_op jit(solution)/shard_map/reduce_sum | solution.py:285
  34.8 2.4 %collective-permute-done.10 = bf16[1024,128]{1,0:T(8,128)(2,1)S(1)} collective-permute-done((bf16[1024,128]{1,0:T(8,128)(2,1)S(1)}, bf16[1024,128]{1,0:T(8,128)(2,1)S(1)}, u32[]{:S(2)}, u32[]{:S(2)}) %collective-permute-start.10) | collective-permute-done | bytes 262176 | tf_op jit(solution)/shard_map/ppermute | solution.py:64
  38.3 3.0 %collective-permute-start.1 = (f32[24,128]{1,0:T(8,128)S(1)}, f32[24,128]{1,0:T(8,128)S(1)}, u32[]{:S(2)}, u32[]{:S(2)}) collective-permute-start(f32[24,128]{1,0:T(8,128)S(1)} %pad_bitcast_fusion), channel_id=1, source_target_pairs={{0,32},{32,64},{64,96},{96,128},{128,160},{160,192},{192,224},{224... | collective-permute-start | bytes 36872 | tf_op jit(solution)/shard_map/ppermute | solution.py:69
  41.3 2.7 %collective-permute-start.2 = (bf16[5376,128]{1,0:T(8,128)(2,1)S(1)}, bf16[5376,128]{1,0:T(8,128)(2,1)S(1)}, u32[]{:S(2)}, u32[]{:S(2)}) collective-permute-start(bf16[5376,128]{1,0:T(8,128)(2,1)S(1)} %bitcast.45), channel_id=1, source_target_pairs={{0,2},{2,4},{4,6},{6,0},{8,10},{10,12},{12,14},{14,8},{16,18},{18,... | collective-permute-start | bytes 4128776 | tf_op jit(solution)/shard_map/ppermute | solution.py:56
  44.1 3.8 %collective-permute-start.3 = (bf16[5376,128]{1,0:T(8,128)(2,1)S(1)}, bf16[5376,128]{1,0:T(8,128)(2,1)}, u32[]{:S(2)}, u32[]{:S(2)}) collective-permute-start(bf16[5376,128]{1,0:T(8,128)(2,1)S(1)} %bitcast.46), channel_id=1, source_target_pairs={{0,6},{2,0},{4,2},{6,4},{8,14},{10,8},{12,10},{14,12},{16,22},{18,... | collective-permute-start | bytes 4128776 | tf_op jit(solution)/shard_map/ppermute | solution.py:56
  47.8 12.8 %collective-permute-start.5 = (f32[3,128]{1,0:T(4,128)S(1)}, f32[3,128]{1,0:T(4,128)S(1)}, u32[]{:S(2)}, u32[]{:S(2)}) collective-permute-start(f32[3,128]{1,0:T(4,128)S(1)} %bitcast.62), channel_id=1, source_target_pairs={{0,33},{1,32},{32,65},{33,64},{64,97},{65,96},{96,129},{97,128},{1... | collective-permute-start | bytes 4616 | tf_op jit(solution)/shard_map/ppermute | solution.py:75
  61.3 2.8 %collective-permute-start.4 = (s32[12]{0:T(128)S(1)}, s32[12]{0:T(128)S(1)}, u32[]{:S(2)}, u32[]{:S(2)}) collective-permute-start(s32[12]{0:T(128)S(1)} %get-tuple-element.42), channel_id=1, source_target_pairs={{0,32},{32,0},{64,96},{96,64},{128,160},{160,128},{192,224},{224,1... | collective-permute-start | bytes 152 | tf_op jit(solution)/shard_map/ppermute | solution.py:80
  64.2 4.7 %collective-permute-done.5 = f32[3,128]{1,0:T(4,128)S(1)} collective-permute-done((f32[3,128]{1,0:T(4,128)S(1)}, f32[3,128]{1,0:T(4,128)S(1)}, u32[]{:S(2)}, u32[]{:S(2)}) %collective-permute-start.5) | collective-permute-done | bytes 1568 | tf_op jit(solution)/shard_map/ppermute | solution.py:75
  68.8 1.9 %collective-permute-start.8 = (bf16[384,2048]{1,0:T(8,128)(2,1)}, bf16[384,2048]{1,0:T(8,128)(2,1)}, u32[]{:S(2)}, u32[]{:S(2)}) collective-permute-start(bf16[384,2048]{1,0:T(8,128)(2,1)} %bitcast.51), channel_id=1, source_target_pairs={{0,32},{32,64},{64,96},{96,128},{128,160},{160,192},{192,224},{224... | collective-permute-start | bytes 4718600 | tf_op jit(solution)/shard_map/ppermute | solution.py:69
  71.0 3.1 %collective-permute-start.6 = (bf16[2688,128]{1,0:T(8,128)(2,1)S(1)}, bf16[2688,128]{1,0:T(8,128)(2,1)S(1)}, u32[]{:S(2)}, u32[]{:S(2)}) collective-permute-start(bf16[2688,128]{1,0:T(8,128)(2,1)S(1)} %slice.36), channel_id=1, source_target_pairs={{0,2},{2,4},{4,6},{6,0},{8,10},{10,12},{12,14},{14,8},{16,18},{18,... | collective-permute-start | bytes 2064392 | tf_op jit(solution)/shard_map/ppermute | solution.py:56
  74.1 1.2 slice.37
  75.3 3.4 %collective-permute-start.7 = (bf16[2688,128]{1,0:T(8,128)(2,1)S(1)}, bf16[2688,128]{1,0:T(8,128)(2,1)S(1)}, u32[]{:S(2)}, u32[]{:S(2)}) collective-permute-start(bf16[2688,128]{1,0:T(8,128)(2,1)S(1)} %slice.37), channel_id=1, source_target_pairs={{0,6},{2,0},{4,2},{6,4},{8,14},{10,8},{12,10},{14,12},{16,22},{18,... | collective-permute-start | bytes 2064392 | tf_op jit(solution)/shard_map/ppermute | solution.py:56
  78.9 12.8 %collective-permute-done.6.ol_ref = bf16[2688,128]{1,0:T(8,128)(2,1)S(1)} collective-permute-done((bf16[2688,128]{1,0:T(8,128)(2,1)S(1)}, bf16[2688,128]{1,0:T(8,128)(2,1)S(1)}, u32[]{:S(2)}, u32[]{:S(2)}) %collective-permute-start.6) | collective-permute-done | bytes 688160 | tf_op jit(solution)/shard_map/ppermute | solution.py:56
  92.3 2.5 %give_encodings.1 = bf16[12,256,128]{2,1,0:T(8,128)(2,1)S(1)} custom-call(s32[3,24]{1,0:T(4,128)S(1)} %add_add_fusion.table, bf16[5376,128]{1,0:T(8,128)(2,1)S(1)} %bitcast.47, bf16[5376,128]{1,0:T(8,128)(2,1)} %collective-permute-done.3.r_ref, bf16[2688,128]{1,0:T(8,128)(2,1)S(1)} %collective-permute-done.6.ol_ref, ...), custom_call_target="tpu_custom_call" | custom-call | tf_op jit(solution)/shard_map/give_encodings/pallas_call | solution.py:128
  94.8 6.7 %collective-permute-start.9 = (bf16[12,256,128]{2,1,0:T(8,128)(2,1)S(1)}, bf16[12,256,128]{2,1,0:T(8,128)(2,1)}, u32[]{:S(2)}, u32[]{:S(2)}) collective-permute-start(bf16[12,256,128]{2,1,0:T(8,128)(2,1)S(1)} %give_encodings.1), channel_id=1, source_target_pairs={{0,32},{32,0},{64,96},{96,64},{128,160},{160,128},{192,224},{224,1... | collective-permute-start | bytes 2359304 | tf_op jit(solution)/shard_map/ppermute | solution.py:80
  102.9 3.1 %pick_encodings.1.own_ref = bf16[768,512]{1,0:T(8,128)(2,1)S(1)} custom-call(s32[3,24]{1,0:T(4,128)S(1)} %add_add_fusion.table, bf16[5376,128]{1,0:T(8,128)(2,1)S(1)} %bitcast.48, bf16[5376,128]{1,0:T(8,128)(2,1)} %collective-permute-done.3.r_ref, bf16[2688,128]{1,0:T(8,128)(2,1)S(1)} %collective-permute-done.6.ol_ref, ...), custom_call_target="tpu_custom_call" | custom-call | tf_op jit(solution)/shard_map/pick_encodings/pallas_call | solution.py:140
  106.9 18.9 %attend_heads.1 = bf16[384,2048]{1,0:T(8,128)(2,1)} custom-call(s32[12]{0:T(128)} %get-tuple-element.43.live, s32[3,24]{1,0:T(4,128)} %copy-done.3, bf16[768,512]{1,0:T(8,128)(2,1)} %copy-done.2, bf16[12,256,128]{2,1,0:T(8,128)(2,1)} %collective-permute-done.9.slabs, bf16[512,512]{1,0:T(8,128)(2,1)} %copy-done.1, bf16[16,1024,128]{2,1,0:T(8,128)(2,1)} %bitcast.49, ...), custom_call_target="tpu_custom_call" | custom-call | tf_op jit(solution)/shard_map/attend_heads/pallas_call | solution.py:210
  (61 shorter events, 6.3 us)
Async XLA Ops:
  6.5 1.1 copy-start
  9.7 5.2 %copy-start.4 = (bf16[1,28,2048]{2,1,0:T(8,128)(2,1)S(1)}, bf16[1,28,2048]{2,1,0:T(8,128)(2,1)}, u32[]{:S(2)}) copy-start(bf16[1,28,2048]{2,1,0:T(8,128)(2,1)} %param.11) | copy-start | bytes 344068
  9.7 5.2 %copy-start.5 = (bf16[1,28,2048]{2,1,0:T(8,128)(2,1)S(1)}, bf16[1,28,2048]{2,1,0:T(8,128)(2,1)}, u32[]{:S(2)}) copy-start(bf16[1,28,2048]{2,1,0:T(8,128)(2,1)} %param.10) | copy-start | bytes 344068
  9.7 22.8 %copy-start.9 = (s32[1,6,2]{1,2,0:T(2,128)S(1)}, s32[1,6,2]{1,2,0:T(2,128)}, u32[]{:S(2)}) copy-start(s32[1,6,2]{1,2,0:T(2,128)} %param.14) | copy-start | bytes 148
  9.7 23.0 %copy-start.7 = (s32[1,6,2]{1,2,0:T(2,128)S(1)}, s32[1,6,2]{1,2,0:T(2,128)}, u32[]{:S(2)}) copy-start(s32[1,6,2]{1,2,0:T(2,128)} %param.13) | copy-start | bytes 148
  9.7 23.0 %copy-start.8 = (s32[1,6,2]{1,2,0:T(2,128)S(1)}, s32[1,6,2]{1,2,0:T(2,128)}, u32[]{:S(2)}) copy-start(s32[1,6,2]{1,2,0:T(2,128)} %param.12) | copy-start | bytes 148
  9.7 25.1 %all-to-all-start = ((bf16[4,1344,128]{2,1,0:T(8,128)(2,1)}), bf16[4,1344,128]{2,1,0:T(8,128)(2,1)S(1)}, u32[]{:S(2)}, u32[]{:S(2)}) async-start(bf16[4,1344,128]{2,1,0:T(8,128)(2,1)} %tile.9), calls=%async_computation | async-start | bytes 2752512 | tf_op jit(solution)/shard_map/all_to_all | solution.py:262
  14.8 92.0 %all-gather.2.cloned.1.call-start = ((), (), s32[]{:S(2)}) async-start(), calls=%async_computation.1 | async-start | bytes 5242880 | tf_op jit(solution)/shard_map/all_gather | solution.py:296
  14.8 19.8 %copy-start.6 = (f32[1,2048]{1,0:T(1,128)S(1)}, f32[1,2048]{1,0:T(1,128)}, u32[]{:S(2)}) copy-start(f32[1,2048]{1,0:T(1,128)} %param.9) | copy-start | bytes 24580
  15.0 19.8 %collective-permute-start = (bf16[1024,128]{1,0:T(8,128)(2,1)S(1)}, bf16[1024,128]{1,0:T(8,128)(2,1)S(1)}, u32[]{:S(2)}, u32[]{:S(2)}) collective-permute-start(bf16[1024,128]{1,0:T(8,128)(2,1)S(1)} %bitcast.54), channel_id=1, source_target_pairs={{480,0},{482,2},{484,4},{486,6},{488,8},{490,10},{492,12},{494,14}... | collective-permute-start | bytes 786440 | tf_op jit(solution)/shard_map/ppermute | solution.py:64
  19.2 15.5 %collective-permute-start.12 = (bf16[1024,128]{1,0:T(8,128)(2,1)S(1)}, bf16[1024,128]{1,0:T(8,128)(2,1)S(1)}, u32[]{:S(2)}, u32[]{:S(2)}) collective-permute-start(bf16[1024,128]{1,0:T(8,128)(2,1)S(1)} %bitcast.55), channel_id=1, source_target_pairs={{480,8},{482,10},{484,12},{486,14},{488,16},{490,18},{492,20},{494... | collective-permute-start | bytes 786440 | tf_op jit(solution)/shard_map/ppermute | solution.py:64
  22.6 12.2 %collective-permute-start.11 = (bf16[1024,128]{1,0:T(8,128)(2,1)S(1)}, bf16[1024,128]{1,0:T(8,128)(2,1)S(1)}, u32[]{:S(2)}, u32[]{:S(2)}) collective-permute-start(bf16[1024,128]{1,0:T(8,128)(2,1)S(1)} %bitcast.56), channel_id=1, source_target_pairs={{480,16},{482,18},{484,20},{486,22},{488,24},{490,26},{492,28},{49... | collective-permute-start | bytes 786440 | tf_op jit(solution)/shard_map/ppermute | solution.py:64
  29.2 8.0 %collective-permute-start.10 = (bf16[1024,128]{1,0:T(8,128)(2,1)S(1)}, bf16[1024,128]{1,0:T(8,128)(2,1)S(1)}, u32[]{:S(2)}, u32[]{:S(2)}) collective-permute-start(bf16[1024,128]{1,0:T(8,128)(2,1)S(1)} %bitcast.57), channel_id=1, source_target_pairs={{480,24},{482,26},{484,28},{486,30},{488,0},{490,2},{492,4},{494,6... | collective-permute-start | bytes 786440 | tf_op jit(solution)/shard_map/ppermute | solution.py:64
  38.3 22.3 %collective-permute-start.1 = (f32[24,128]{1,0:T(8,128)S(1)}, f32[24,128]{1,0:T(8,128)S(1)}, u32[]{:S(2)}, u32[]{:S(2)}) collective-permute-start(f32[24,128]{1,0:T(8,128)S(1)} %pad_bitcast_fusion), channel_id=1, source_target_pairs={{0,32},{32,64},{64,96},{96,128},{128,160},{160,192},{192,224},{224... | collective-permute-start | bytes 36872 | tf_op jit(solution)/shard_map/ppermute | solution.py:69
  41.3 29.6 %collective-permute-start.2 = (bf16[5376,128]{1,0:T(8,128)(2,1)S(1)}, bf16[5376,128]{1,0:T(8,128)(2,1)S(1)}, u32[]{:S(2)}, u32[]{:S(2)}) collective-permute-start(bf16[5376,128]{1,0:T(8,128)(2,1)S(1)} %bitcast.45), channel_id=1, source_target_pairs={{0,2},{2,4},{4,6},{6,0},{8,10},{10,12},{12,14},{14,8},{16,18},{18,... | collective-permute-start | bytes 4128776 | tf_op jit(solution)/shard_map/ppermute | solution.py:56
  44.1 26.9 %collective-permute-start.3 = (bf16[5376,128]{1,0:T(8,128)(2,1)S(1)}, bf16[5376,128]{1,0:T(8,128)(2,1)}, u32[]{:S(2)}, u32[]{:S(2)}) collective-permute-start(bf16[5376,128]{1,0:T(8,128)(2,1)S(1)} %bitcast.46), channel_id=1, source_target_pairs={{0,6},{2,0},{4,2},{6,4},{8,14},{10,8},{12,10},{14,12},{16,22},{18,... | collective-permute-start | bytes 4128776 | tf_op jit(solution)/shard_map/ppermute | solution.py:56
  47.8 21.0 %collective-permute-start.5 = (f32[3,128]{1,0:T(4,128)S(1)}, f32[3,128]{1,0:T(4,128)S(1)}, u32[]{:S(2)}, u32[]{:S(2)}) collective-permute-start(f32[3,128]{1,0:T(4,128)S(1)} %bitcast.62), channel_id=1, source_target_pairs={{0,33},{1,32},{32,65},{33,64},{64,97},{65,96},{96,129},{97,128},{1... | collective-permute-start | bytes 4616 | tf_op jit(solution)/shard_map/ppermute | solution.py:75
  61.3 7.5 %collective-permute-start.4 = (s32[12]{0:T(128)S(1)}, s32[12]{0:T(128)S(1)}, u32[]{:S(2)}, u32[]{:S(2)}) collective-permute-start(s32[12]{0:T(128)S(1)} %get-tuple-element.42), channel_id=1, source_target_pairs={{0,32},{32,0},{64,96},{96,64},{128,160},{160,128},{192,224},{224,1... | collective-permute-start | bytes 152 | tf_op jit(solution)/shard_map/ppermute | solution.py:80
  68.8 26.0 %collective-permute-start.8 = (bf16[384,2048]{1,0:T(8,128)(2,1)}, bf16[384,2048]{1,0:T(8,128)(2,1)}, u32[]{:S(2)}, u32[]{:S(2)}) collective-permute-start(bf16[384,2048]{1,0:T(8,128)(2,1)} %bitcast.51), channel_id=1, source_target_pairs={{0,32},{32,64},{64,96},{96,128},{128,160},{160,192},{192,224},{224... | collective-permute-start | bytes 4718600 | tf_op jit(solution)/shard_map/ppermute | solution.py:69
  71.0 32.0 %copy-start.1 = (bf16[512,512]{1,0:T(8,128)(2,1)}, bf16[512,512]{1,0:T(8,128)(2,1)S(1)}, u32[]{:S(2)}) copy-start(bf16[512,512]{1,0:T(8,128)(2,1)S(1)} %fusion.spread) | copy-start | bytes 1572868
  71.0 20.7 %collective-permute-start.6 = (bf16[2688,128]{1,0:T(8,128)(2,1)S(1)}, bf16[2688,128]{1,0:T(8,128)(2,1)S(1)}, u32[]{:S(2)}, u32[]{:S(2)}) collective-permute-start(bf16[2688,128]{1,0:T(8,128)(2,1)S(1)} %slice.36), channel_id=1, source_target_pairs={{0,2},{2,4},{4,6},{6,0},{8,10},{10,12},{12,14},{14,8},{16,18},{18,... | collective-permute-start | bytes 2064392 | tf_op jit(solution)/shard_map/ppermute | solution.py:56
  75.3 17.0 %collective-permute-start.7 = (bf16[2688,128]{1,0:T(8,128)(2,1)S(1)}, bf16[2688,128]{1,0:T(8,128)(2,1)S(1)}, u32[]{:S(2)}, u32[]{:S(2)}) collective-permute-start(bf16[2688,128]{1,0:T(8,128)(2,1)S(1)} %slice.37), channel_id=1, source_target_pairs={{0,6},{2,0},{4,2},{6,4},{8,14},{10,8},{12,10},{14,12},{16,22},{18,... | collective-permute-start | bytes 2064392 | tf_op jit(solution)/shard_map/ppermute | solution.py:56
  78.9 24.0 %copy-start.3 = (s32[3,24]{1,0:T(4,128)}, s32[3,24]{1,0:T(4,128)S(1)}, u32[]{:S(2)}) copy-start(s32[3,24]{1,0:T(4,128)S(1)} %add_add_fusion.table) | copy-start | bytes 868
  94.8 12.1 %collective-permute-start.9 = (bf16[12,256,128]{2,1,0:T(8,128)(2,1)S(1)}, bf16[12,256,128]{2,1,0:T(8,128)(2,1)}, u32[]{:S(2)}, u32[]{:S(2)}) collective-permute-start(bf16[12,256,128]{2,1,0:T(8,128)(2,1)S(1)} %give_encodings.1), channel_id=1, source_target_pairs={{0,32},{32,0},{64,96},{96,64},{128,160},{160,128},{192,224},{224,1... | collective-permute-start | bytes 2359304 | tf_op jit(solution)/shard_map/ppermute | solution.py:80
  (1 other events, 0.9 us)
Sparse Core Ops, SparseCore 0:
  38.4 54.7 all-gather.1

commit v8 on v7

--- a/solution.py
+++ b/solution.py
@@ -301,14 +301,13 @@
         axis_index_groups=ring_groups(lax.axis_size("segment"), 1),
     ).reshape(RING, W_ROWS, HD)
     d_before, d_after = turned(line_d, 1, 1), turned(line_d, -1, 1)
-    info_here = to_next(info).reshape(-1)
+    info_here, rows = lax.optimization_barrier((to_next(info).reshape(-1), rows))
     squares_other = to_next_other_mp(squares.reshape(-1, HD)).reshape(-1)
     squares_here = info_here[:tokens]
     gain_here = info_here[tokens:tokens + local_width]
     ints = info_here[tokens + local_width:tokens + local_width + 2 * REQ].astype(jnp.int32)
     live, requests_here = ints[:REQ], ints[REQ:]
     requests_other = other_core(requests_here)
-    requests_other, squares_other, rows = lax.optimization_barrier((requests_other, squares_other, rows))
     x_here = to_next(rows)
     spread = spread_of(core, place)
     d_before, d_after, spread, requests_other = lax.optimization_barrier((d_before, d_after, spread, requests_other))
@@ -319,11 +318,13 @@
         [source_table(requests_here, core, place), source_table(requests_other, core, place)], axis=1
     )
 
-    given, x_here = lax.optimization_barrier((give(table, d_pieces), x_here))
+    inv_rms = lax.rsqrt((squares_here + squares_other) / full_width + eps_norm)
+    given, x_here, inv_column, gain_row = lax.optimization_barrier(
+        (give(table, d_pieces), x_here, inv_rms[:, None], gain_here[None, :])
+    )
     slabs = other_core(given)
     own = pick(table, d_pieces, spread)
-    inv_rms = lax.rsqrt((squares_here + squares_other) / full_width + eps_norm)
-    updated = attend(live, table, own, slabs, spread, all_w, x_here, inv_rms[:, None], gain_here[None, :])
+    updated = attend(live, table, own, slabs, spread, all_w, x_here, inv_column, gain_row)
     return updated[None]
 
 

time: 135 us -> 139 us (1.030)
  the two profiles are of different devices: /device:TPU:1 before, /device:TPU:255 now
where the time goes in v8:
time: 139 us; the launch traced here: 138 us
  starting transfers between devices  68.6 us (49%)
  Pallas kernels  25 us (18%)
  waiting for transfers between devices  15.6 us (11%)
  between operations  13.7 us (10%)
  local copies, waits for them, and re-layouts  10.3 us (7%)
  other arithmetic  4.79 us (3%)
    ppermute x2, starting transfers between devices, to_next(): lax.ppermute(value, 'segment', [(s, (s + 1) % count) for s in range(count)])  21.7 us
    pallas_call x1, Pallas kernels, attend(): pl.pallas_call(attend_kernel, grid_spec=pltpu.PrefetchScalarGridSpec(num_...  18.9 us
    ppermute x2, starting transfers between devices, other_core(): return lax.ppermute(value, 'segment', [(s, s ^ 1) for s in range(count)])  16.6 us
    ppermute x4, starting transfers between devices, turned(): return lax.ppermute(value, ('segment', 'db'), pairs)  10.8 us
    ppermute x4, waiting for transfers between devices, turned(): return lax.ppermute(value, ('segment', 'db'), pairs)  9.91 us
    ppermute x4, starting transfers between devices, to_next_turned(): return lax.ppermute(value, ('segment', 'db'), pairs)  9.72 us
    ppermute x1, starting transfers between devices, to_next_other_mp(): return lax.ppermute(value, ('segment', 'mp'), pairs)  5.52 us
    unnamed x29, local copies, waits for them, and re-layouts  5.28 us
  transfers between devices with their start and end apart: 15, of which 6 were waited for; matrix products, arithmetic and copies ran while one was open for 5% of the time, Pallas kernels for 4%

profile of v8, /device:TPU:255, one launch (start us, length us, event | category | flops | bytes accessed | tf_op | source)
XLA Modules:
  0.0 138.0 jit_solution(4491653801976531824)
XLA Ops:
  6.5 1.1 copy-done
  8.4 1.3 tile.9
  9.7 4.3 %all-to-all-start = ((bf16[4,1344,128]{2,1,0:T(8,128)(2,1)}), bf16[4,1344,128]{2,1,0:T(8,128)(2,1)S(1)}, u32[]{:S(2)}, u32[]{:S(2)}) async-start(bf16[4,1344,128]{2,1,0:T(8,128)(2,1)} %tile.9), calls=%async_computation | async-start | bytes 2752512 | tf_op jit(solution)/shard_map/all_to_all | solution.py:262
  14.1 1.9 %collective-permute-start = (bf16[1024,128]{1,0:T(8,128)(2,1)S(1)}, bf16[1024,128]{1,0:T(8,128)(2,1)S(1)}, u32[]{:S(2)}, u32[]{:S(2)}) collective-permute-start(bf16[1024,128]{1,0:T(8,128)(2,1)S(1)} %bitcast.51), channel_id=1, source_target_pairs={{480,0},{482,2},{484,4},{486,6},{488,8},{490,10},{492,12},{494,14}... | collective-permute-start | bytes 786440 | tf_op jit(solution)/shard_map/ppermute | solution.py:64
  16.1 1.9 %collective-permute-start.12 = (bf16[1024,128]{1,0:T(8,128)(2,1)S(1)}, bf16[1024,128]{1,0:T(8,128)(2,1)S(1)}, u32[]{:S(2)}, u32[]{:S(2)}) collective-permute-start(bf16[1024,128]{1,0:T(8,128)(2,1)S(1)} %bitcast.52), channel_id=1, source_target_pairs={{480,8},{482,10},{484,12},{486,14},{488,16},{490,18},{492,20},{494... | collective-permute-start | bytes 786440 | tf_op jit(solution)/shard_map/ppermute | solution.py:64
  18.0 2.9 %collective-permute-start.11 = (bf16[1024,128]{1,0:T(8,128)(2,1)S(1)}, bf16[1024,128]{1,0:T(8,128)(2,1)S(1)}, u32[]{:S(2)}, u32[]{:S(2)}) collective-permute-start(bf16[1024,128]{1,0:T(8,128)(2,1)S(1)} %bitcast.53), channel_id=1, source_target_pairs={{480,16},{482,18},{484,20},{486,22},{488,24},{490,26},{492,28},{49... | collective-permute-start | bytes 786440 | tf_op jit(solution)/shard_map/ppermute | solution.py:64
  20.9 2.9 %collective-permute-start.10 = (bf16[1024,128]{1,0:T(8,128)(2,1)S(1)}, bf16[1024,128]{1,0:T(8,128)(2,1)S(1)}, u32[]{:S(2)}, u32[]{:S(2)}) collective-permute-start(bf16[1024,128]{1,0:T(8,128)(2,1)S(1)} %bitcast.54), channel_id=1, source_target_pairs={{480,24},{482,26},{484,28},{486,30},{488,0},{490,2},{492,4},{494,6... | collective-permute-start | bytes 786440 | tf_op jit(solution)/shard_map/ppermute | solution.py:64
  24.3 1.8 %multiply_reduce_fusion = f32[384]{0:T(512)S(1)} fusion(bf16[1,384,2048]{2,1,0:T(8,128)(2,1)} %param.8), kind=kLoop, calls=%fused_computation | loop fusion | flops 2358912 | bytes 1574400 | tf_op jit(solution)/shard_map/reduce_sum | solution.py:285
  27.2 3.1 %collective-permute-done.10 = bf16[1024,128]{1,0:T(8,128)(2,1)S(1)} collective-permute-done((bf16[1024,128]{1,0:T(8,128)(2,1)S(1)}, bf16[1024,128]{1,0:T(8,128)(2,1)S(1)}, u32[]{:S(2)}, u32[]{:S(2)}) %collective-permute-start.10) | collective-permute-done | bytes 262176 | tf_op jit(solution)/shard_map/ppermute | solution.py:64
  31.3 3.5 %collective-permute-start.2 = (bf16[5376,128]{1,0:T(8,128)(2,1)S(1)}, bf16[5376,128]{1,0:T(8,128)(2,1)S(1)}, u32[]{:S(2)}, u32[]{:S(2)}) collective-permute-start(bf16[5376,128]{1,0:T(8,128)(2,1)S(1)} %bitcast.42), channel_id=1, source_target_pairs={{0,2},{2,4},{4,6},{6,0},{8,10},{10,12},{12,14},{14,8},{16,18},{18,... | collective-permute-start | bytes 4128776 | tf_op jit(solution)/shard_map/ppermute | solution.py:56
  34.9 1.9 %collective-permute-start.3 = (bf16[5376,128]{1,0:T(8,128)(2,1)S(1)}, bf16[5376,128]{1,0:T(8,128)(2,1)}, u32[]{:S(2)}, u32[]{:S(2)}) collective-permute-start(bf16[5376,128]{1,0:T(8,128)(2,1)S(1)} %bitcast.43), channel_id=1, source_target_pairs={{0,6},{2,0},{4,2},{6,4},{8,14},{10,8},{12,10},{14,12},{16,22},{18,... | collective-permute-start | bytes 4128776 | tf_op jit(solution)/shard_map/ppermute | solution.py:56
  36.9 10.9 %collective-permute-start.1 = (f32[24,128]{1,0:T(8,128)S(1)}, f32[24,128]{1,0:T(8,128)S(1)}, u32[]{:S(2)}, u32[]{:S(2)}) collective-permute-start(f32[24,128]{1,0:T(8,128)S(1)} %pad_bitcast_fusion), channel_id=1, source_target_pairs={{0,32},{32,64},{64,96},{96,128},{128,160},{160,192},{192,224},{224... | collective-permute-start | bytes 36872 | tf_op jit(solution)/shard_map/ppermute | solution.py:69
  48.6 10.8 %collective-permute-start.7 = (bf16[384,2048]{1,0:T(8,128)(2,1)}, bf16[384,2048]{1,0:T(8,128)(2,1)}, u32[]{:S(2)}, u32[]{:S(2)}) collective-permute-start(bf16[384,2048]{1,0:T(8,128)(2,1)} %bitcast.48), channel_id=1, source_target_pairs={{0,32},{32,64},{64,96},{96,128},{128,160},{160,192},{192,224},{224... | collective-permute-start | bytes 4718600 | tf_op jit(solution)/shard_map/ppermute | solution.py:69
  60.3 5.5 %collective-permute-start.8 = (f32[3,128]{1,0:T(4,128)S(1)}, f32[3,128]{1,0:T(4,128)S(1)}, u32[]{:S(2)}, u32[]{:S(2)}) collective-permute-start(f32[3,128]{1,0:T(4,128)S(1)} %bitcast.61), channel_id=1, source_target_pairs={{0,33},{1,32},{32,65},{33,64},{64,97},{65,96},{96,129},{97,128},{1... | collective-permute-start | bytes 4616 | tf_op jit(solution)/shard_map/ppermute | solution.py:75
  67.1 10.1 %collective-permute-start.4 = (s32[12]{0:T(128)S(1)}, s32[12]{0:T(128)S(1)}, u32[]{:S(2)}, u32[]{:S(2)}) collective-permute-start(s32[12]{0:T(128)S(1)} %get-tuple-element.44), channel_id=1, source_target_pairs={{0,32},{32,0},{64,96},{96,64},{128,160},{160,128},{192,224},{224,1... | collective-permute-start | bytes 152 | tf_op jit(solution)/shard_map/ppermute | solution.py:80
  78.0 2.2 %collective-permute-start.5 = (bf16[2688,128]{1,0:T(8,128)(2,1)S(1)}, bf16[2688,128]{1,0:T(8,128)(2,1)S(1)}, u32[]{:S(2)}, u32[]{:S(2)}) collective-permute-start(bf16[2688,128]{1,0:T(8,128)(2,1)S(1)} %slice.32), channel_id=1, source_target_pairs={{0,2},{2,4},{4,6},{6,0},{8,10},{10,12},{12,14},{14,8},{16,18},{18,... | collective-permute-start | bytes 2064392 | tf_op jit(solution)/shard_map/ppermute | solution.py:56
  80.2 1.1 slice.33
  81.4 3.1 %collective-permute-start.6 = (bf16[2688,128]{1,0:T(8,128)(2,1)S(1)}, bf16[2688,128]{1,0:T(8,128)(2,1)S(1)}, u32[]{:S(2)}, u32[]{:S(2)}) collective-permute-start(bf16[2688,128]{1,0:T(8,128)(2,1)S(1)} %slice.33), channel_id=1, source_target_pairs={{0,6},{2,0},{4,2},{6,4},{8,14},{10,8},{12,10},{14,12},{16,22},{18,... | collective-permute-start | bytes 2064392 | tf_op jit(solution)/shard_map/ppermute | solution.py:56
  84.7 5.4 %collective-permute-done.5.ol_ref = bf16[2688,128]{1,0:T(8,128)(2,1)S(1)} collective-permute-done((bf16[2688,128]{1,0:T(8,128)(2,1)S(1)}, bf16[2688,128]{1,0:T(8,128)(2,1)S(1)}, u32[]{:S(2)}, u32[]{:S(2)}) %collective-permute-start.5) | collective-permute-done | bytes 688160 | tf_op jit(solution)/shard_map/ppermute | solution.py:56
  90.0 4.5 %collective-permute-done.6.or_ref = bf16[2688,128]{1,0:T(8,128)(2,1)S(1)} collective-permute-done((bf16[2688,128]{1,0:T(8,128)(2,1)S(1)}, bf16[2688,128]{1,0:T(8,128)(2,1)S(1)}, u32[]{:S(2)}, u32[]{:S(2)}) %collective-permute-start.6) | collective-permute-done | bytes 688160 | tf_op jit(solution)/shard_map/ppermute | solution.py:56
  94.6 2.9 %give_encodings.1 = bf16[12,256,128]{2,1,0:T(8,128)(2,1)} custom-call(s32[3,24]{1,0:T(4,128)S(1)} %add_add_fusion.table, bf16[5376,128]{1,0:T(8,128)(2,1)S(1)} %bitcast.44, bf16[5376,128]{1,0:T(8,128)(2,1)} %collective-permute-done.3.r_ref, bf16[2688,128]{1,0:T(8,128)(2,1)S(1)} %collective-permute-done.5.ol_ref, ...), custom_call_target="tpu_custom_call" | custom-call | tf_op jit(solution)/shard_map/give_encodings/pallas_call | solution.py:128
  97.5 6.6 %collective-permute-start.9 = (bf16[12,256,128]{2,1,0:T(8,128)(2,1)}, bf16[12,256,128]{2,1,0:T(8,128)(2,1)}, u32[]{:S(2)}, u32[]{:S(2)}) collective-permute-start(bf16[12,256,128]{2,1,0:T(8,128)(2,1)} %give_encodings.1), channel_id=1, source_target_pairs={{0,32},{32,0},{64,96},{96,64},{128,160},{160,128},{192,224},{224,1... | collective-permute-start | bytes 2359304 | tf_op jit(solution)/shard_map/ppermute | solution.py:80
  108.2 3.2 %pick_encodings.1.own_ref = bf16[768,512]{1,0:T(8,128)(2,1)S(1)} custom-call(s32[3,24]{1,0:T(4,128)S(1)} %add_add_fusion.table, bf16[5376,128]{1,0:T(8,128)(2,1)S(1)} %bitcast.45, bf16[5376,128]{1,0:T(8,128)(2,1)} %collective-permute-done.3.r_ref, bf16[2688,128]{1,0:T(8,128)(2,1)S(1)} %copy-done.4, bf16[2688,128]{1,0:T(8,128)(2,1)S(1)} %copy-done.6, ...), custom_call_target="tpu_custom_call" | custom-call | tf_op jit(solution)/shard_map/pick_encodings/pallas_call | solution.py:140
  112.3 18.9 %attend_heads.1 = bf16[384,2048]{1,0:T(8,128)(2,1)} custom-call(s32[12]{0:T(128)} %get-tuple-element.45.live, s32[3,24]{1,0:T(4,128)} %copy-done.7, bf16[768,512]{1,0:T(8,128)(2,1)} %copy-done.2, bf16[12,256,128]{2,1,0:T(8,128)(2,1)} %collective-permute-done.9.slabs, bf16[512,512]{1,0:T(8,128)(2,1)} %fusion.spread, bf16[16,1024,128]{2,1,0:T(8,128)(2,1)} %bitcast.46, ...), custom_call_target="tpu_custom_call" | custom-call | tf_op jit(solution)/shard_map/attend_heads/pallas_call | solution.py:210
  (70 shorter events, 12.4 us)
Async XLA Ops:
  9.7 4.3 %copy-start.8 = (bf16[1,28,2048]{2,1,0:T(8,128)(2,1)S(1)}, bf16[1,28,2048]{2,1,0:T(8,128)(2,1)}, u32[]{:S(2)}) copy-start(bf16[1,28,2048]{2,1,0:T(8,128)(2,1)} %param.11) | copy-start | bytes 344068
  9.7 4.3 %copy-start.9 = (bf16[1,28,2048]{2,1,0:T(8,128)(2,1)S(1)}, bf16[1,28,2048]{2,1,0:T(8,128)(2,1)}, u32[]{:S(2)}) copy-start(bf16[1,28,2048]{2,1,0:T(8,128)(2,1)} %param.10) | copy-start | bytes 344068
  9.7 14.2 %copy-start.13 = (s32[1,6,2]{1,2,0:T(2,128)S(1)}, s32[1,6,2]{1,2,0:T(2,128)}, u32[]{:S(2)}) copy-start(s32[1,6,2]{1,2,0:T(2,128)} %param.14) | copy-start | bytes 148
  9.7 14.4 %copy-start.11 = (s32[1,6,2]{1,2,0:T(2,128)S(1)}, s32[1,6,2]{1,2,0:T(2,128)}, u32[]{:S(2)}) copy-start(s32[1,6,2]{1,2,0:T(2,128)} %param.13) | copy-start | bytes 148
  9.7 14.4 %copy-start.12 = (s32[1,6,2]{1,2,0:T(2,128)S(1)}, s32[1,6,2]{1,2,0:T(2,128)}, u32[]{:S(2)}) copy-start(s32[1,6,2]{1,2,0:T(2,128)} %param.12) | copy-start | bytes 148
  9.7 16.5 %all-to-all-start = ((bf16[4,1344,128]{2,1,0:T(8,128)(2,1)}), bf16[4,1344,128]{2,1,0:T(8,128)(2,1)S(1)}, u32[]{:S(2)}, u32[]{:S(2)}) async-start(bf16[4,1344,128]{2,1,0:T(8,128)(2,1)} %tile.9), calls=%async_computation | async-start | bytes 2752512 | tf_op jit(solution)/shard_map/all_to_all | solution.py:262
  13.9 98.3 %all-gather.2.cloned.1.call-start = ((), (), s32[]{:S(2)}) async-start(), calls=%async_computation.1 | async-start | bytes 5242880 | tf_op jit(solution)/shard_map/all_gather | solution.py:296
  14.0 12.1 %copy-start.10 = (f32[1,2048]{1,0:T(1,128)S(1)}, f32[1,2048]{1,0:T(1,128)}, u32[]{:S(2)}) copy-start(f32[1,2048]{1,0:T(1,128)} %param.9) | copy-start | bytes 24580
  14.1 12.0 %collective-permute-start = (bf16[1024,128]{1,0:T(8,128)(2,1)S(1)}, bf16[1024,128]{1,0:T(8,128)(2,1)S(1)}, u32[]{:S(2)}, u32[]{:S(2)}) collective-permute-start(bf16[1024,128]{1,0:T(8,128)(2,1)S(1)} %bitcast.51), channel_id=1, source_target_pairs={{480,0},{482,2},{484,4},{486,6},{488,8},{490,10},{492,12},{494,14}... | collective-permute-start | bytes 786440 | tf_op jit(solution)/shard_map/ppermute | solution.py:64
  16.1 10.1 %collective-permute-start.12 = (bf16[1024,128]{1,0:T(8,128)(2,1)S(1)}, bf16[1024,128]{1,0:T(8,128)(2,1)S(1)}, u32[]{:S(2)}, u32[]{:S(2)}) collective-permute-start(bf16[1024,128]{1,0:T(8,128)(2,1)S(1)} %bitcast.52), channel_id=1, source_target_pairs={{480,8},{482,10},{484,12},{486,14},{488,16},{490,18},{492,20},{494... | collective-permute-start | bytes 786440 | tf_op jit(solution)/shard_map/ppermute | solution.py:64
  18.0 9.2 %collective-permute-start.11 = (bf16[1024,128]{1,0:T(8,128)(2,1)S(1)}, bf16[1024,128]{1,0:T(8,128)(2,1)S(1)}, u32[]{:S(2)}, u32[]{:S(2)}) collective-permute-start(bf16[1024,128]{1,0:T(8,128)(2,1)S(1)} %bitcast.53), channel_id=1, source_target_pairs={{480,16},{482,18},{484,20},{486,22},{488,24},{490,26},{492,28},{49... | collective-permute-start | bytes 786440 | tf_op jit(solution)/shard_map/ppermute | solution.py:64
  20.9 9.3 %collective-permute-start.10 = (bf16[1024,128]{1,0:T(8,128)(2,1)S(1)}, bf16[1024,128]{1,0:T(8,128)(2,1)S(1)}, u32[]{:S(2)}, u32[]{:S(2)}) collective-permute-start(bf16[1024,128]{1,0:T(8,128)(2,1)S(1)} %bitcast.54), channel_id=1, source_target_pairs={{480,24},{482,26},{484,28},{486,30},{488,0},{490,2},{492,4},{494,6... | collective-permute-start | bytes 786440 | tf_op jit(solution)/shard_map/ppermute | solution.py:64
  31.3 46.6 %collective-permute-start.2 = (bf16[5376,128]{1,0:T(8,128)(2,1)S(1)}, bf16[5376,128]{1,0:T(8,128)(2,1)S(1)}, u32[]{:S(2)}, u32[]{:S(2)}) collective-permute-start(bf16[5376,128]{1,0:T(8,128)(2,1)S(1)} %bitcast.42), channel_id=1, source_target_pairs={{0,2},{2,4},{4,6},{6,0},{8,10},{10,12},{12,14},{14,8},{16,18},{18,... | collective-permute-start | bytes 4128776 | tf_op jit(solution)/shard_map/ppermute | solution.py:56
  34.9 43.1 %collective-permute-start.3 = (bf16[5376,128]{1,0:T(8,128)(2,1)S(1)}, bf16[5376,128]{1,0:T(8,128)(2,1)}, u32[]{:S(2)}, u32[]{:S(2)}) collective-permute-start(bf16[5376,128]{1,0:T(8,128)(2,1)S(1)} %bitcast.43), channel_id=1, source_target_pairs={{0,6},{2,0},{4,2},{6,4},{8,14},{10,8},{12,10},{14,12},{16,22},{18,... | collective-permute-start | bytes 4128776 | tf_op jit(solution)/shard_map/ppermute | solution.py:56
  36.9 11.7 %collective-permute-start.1 = (f32[24,128]{1,0:T(8,128)S(1)}, f32[24,128]{1,0:T(8,128)S(1)}, u32[]{:S(2)}, u32[]{:S(2)}) collective-permute-start(f32[24,128]{1,0:T(8,128)S(1)} %pad_bitcast_fusion), channel_id=1, source_target_pairs={{0,32},{32,64},{64,96},{96,128},{128,160},{160,192},{192,224},{224... | collective-permute-start | bytes 36872 | tf_op jit(solution)/shard_map/ppermute | solution.py:69
  48.6 49.0 %collective-permute-start.7 = (bf16[384,2048]{1,0:T(8,128)(2,1)}, bf16[384,2048]{1,0:T(8,128)(2,1)}, u32[]{:S(2)}, u32[]{:S(2)}) collective-permute-start(bf16[384,2048]{1,0:T(8,128)(2,1)} %bitcast.48), channel_id=1, source_target_pairs={{0,32},{32,64},{64,96},{96,128},{128,160},{160,192},{192,224},{224... | collective-permute-start | bytes 4718600 | tf_op jit(solution)/shard_map/ppermute | solution.py:69
  60.3 24.2 %collective-permute-start.8 = (f32[3,128]{1,0:T(4,128)S(1)}, f32[3,128]{1,0:T(4,128)S(1)}, u32[]{:S(2)}, u32[]{:S(2)}) collective-permute-start(f32[3,128]{1,0:T(4,128)S(1)} %bitcast.61), channel_id=1, source_target_pairs={{0,33},{1,32},{32,65},{33,64},{64,97},{65,96},{96,129},{97,128},{1... | collective-permute-start | bytes 4616 | tf_op jit(solution)/shard_map/ppermute | solution.py:75
  67.1 10.9 %collective-permute-start.4 = (s32[12]{0:T(128)S(1)}, s32[12]{0:T(128)S(1)}, u32[]{:S(2)}, u32[]{:S(2)}) collective-permute-start(s32[12]{0:T(128)S(1)} %get-tuple-element.44), channel_id=1, source_target_pairs={{0,32},{32,0},{64,96},{96,64},{128,160},{160,128},{192,224},{224,1... | collective-permute-start | bytes 152 | tf_op jit(solution)/shard_map/ppermute | solution.py:80
  78.0 12.0 %collective-permute-start.5 = (bf16[2688,128]{1,0:T(8,128)(2,1)S(1)}, bf16[2688,128]{1,0:T(8,128)(2,1)S(1)}, u32[]{:S(2)}, u32[]{:S(2)}) collective-permute-start(bf16[2688,128]{1,0:T(8,128)(2,1)S(1)} %slice.32), channel_id=1, source_target_pairs={{0,2},{2,4},{4,6},{6,0},{8,10},{10,12},{12,14},{14,8},{16,18},{18,... | collective-permute-start | bytes 2064392 | tf_op jit(solution)/shard_map/ppermute | solution.py:56
  81.4 13.2 %collective-permute-start.6 = (bf16[2688,128]{1,0:T(8,128)(2,1)S(1)}, bf16[2688,128]{1,0:T(8,128)(2,1)S(1)}, u32[]{:S(2)}, u32[]{:S(2)}) collective-permute-start(bf16[2688,128]{1,0:T(8,128)(2,1)S(1)} %slice.33), channel_id=1, source_target_pairs={{0,6},{2,0},{4,2},{6,4},{8,14},{10,8},{12,10},{14,12},{16,22},{18,... | collective-permute-start | bytes 2064392 | tf_op jit(solution)/shard_map/ppermute | solution.py:56
  84.7 20.3 %copy-start.7 = (s32[3,24]{1,0:T(4,128)}, s32[3,24]{1,0:T(4,128)S(1)}, u32[]{:S(2)}) copy-start(s32[3,24]{1,0:T(4,128)S(1)} %add_add_fusion.table) | copy-start | bytes 868
  90.0 7.5 %copy-start.3 = (bf16[2688,128]{1,0:T(8,128)(2,1)}, bf16[2688,128]{1,0:T(8,128)(2,1)S(1)}, u32[]{:S(2)}) copy-start(bf16[2688,128]{1,0:T(8,128)(2,1)S(1)} %collective-permute-done.5.ol_ref) | copy-start | bytes 2064388
  94.6 3.0 %copy-start.5 = (bf16[2688,128]{1,0:T(8,128)(2,1)}, bf16[2688,128]{1,0:T(8,128)(2,1)S(1)}, u32[]{:S(2)}) copy-start(bf16[2688,128]{1,0:T(8,128)(2,1)S(1)} %collective-permute-done.6.or_ref) | copy-start | bytes 2064388
  97.5 14.7 %collective-permute-start.9 = (bf16[12,256,128]{2,1,0:T(8,128)(2,1)}, bf16[12,256,128]{2,1,0:T(8,128)(2,1)}, u32[]{:S(2)}, u32[]{:S(2)}) collective-permute-start(bf16[12,256,128]{2,1,0:T(8,128)(2,1)} %give_encodings.1), channel_id=1, source_target_pairs={{0,32},{32,0},{64,96},{96,64},{128,160},{160,128},{192,224},{224,1... | collective-permute-start | bytes 2359304 | tf_op jit(solution)/shard_map/ppermute | solution.py:80
  (5 other events, 5.2 us)
Sparse Core Ops, SparseCore 0:
  31.5 49.0 all-gather.1

commit v9 on v8

--- a/solution.py
+++ b/solution.py
@@ -301,16 +301,18 @@
         axis_index_groups=ring_groups(lax.axis_size("segment"), 1),
     ).reshape(RING, W_ROWS, HD)
     d_before, d_after = turned(line_d, 1, 1), turned(line_d, -1, 1)
-    info_here, rows = lax.optimization_barrier((to_next(info).reshape(-1), rows))
-    squares_other = to_next_other_mp(squares.reshape(-1, HD)).reshape(-1)
+    info_here = to_next(info).reshape(-1)
     squares_here = info_here[:tokens]
     gain_here = info_here[tokens:tokens + local_width]
     ints = info_here[tokens + local_width:tokens + local_width + 2 * REQ].astype(jnp.int32)
     live, requests_here = ints[:REQ], ints[REQ:]
     requests_other = other_core(requests_here)
+    spread = spread_of(core, place)
+    d_before, d_after, spread, requests_other, rows, squares = lax.optimization_barrier(
+        (d_before, d_after, spread, requests_other, rows, squares)
+    )
     x_here = to_next(rows)
-    spread = spread_of(core, place)
-    d_before, d_after, spread, requests_other = lax.optimization_barrier((d_before, d_after, spread, requests_other))
+    squares_other = to_next_other_mp(squares.reshape(-1, HD)).reshape(-1)
     mid_d = line_d.shape[0] // 2
     d_pieces = (line_d, d_after, turned(d_before[:mid_d], 1, 1), turned(d_after[mid_d:], -1, 1), d_before)
 

time: 139 us -> 135 us (0.971)
  the two profiles are of different devices: /device:TPU:255 before, /device:TPU:1 now
where the time goes in v9:
time: 135 us; the launch traced here: 133 us
  starting transfers between devices  61.8 us (46%)
  Pallas kernels  24.6 us (18%)
  waiting for transfers between devices  19.3 us (14%)
  between operations  13.7 us (10%)
  local copies, waits for them, and re-layouts  8.22 us (6%)
  other arithmetic  4.8 us (4%)
    pallas_call x1, Pallas kernels, attend(): pl.pallas_call(attend_kernel, grid_spec=pltpu.PrefetchScalarGridSpec(num_...  18.9 us
    ppermute x4, starting transfers between devices, to_next_turned(): return lax.ppermute(value, ('segment', 'db'), pairs)  17.5 us
    ppermute x4, starting transfers between devices, turned(): return lax.ppermute(value, ('segment', 'db'), pairs)  13 us
    ppermute x2, starting transfers between devices, other_core(): return lax.ppermute(value, 'segment', [(s, s ^ 1) for s in range(count)])  12.8 us
    ppermute x1, waiting for transfers between devices, to_next_other_mp(): return lax.ppermute(value, ('segment', 'mp'), pairs)  10.1 us
    ppermute x1, starting transfers between devices, to_next_other_mp(): return lax.ppermute(value, ('segment', 'mp'), pairs)  7.92 us
    ppermute x2, waiting for transfers between devices, to_next(): lax.ppermute(value, 'segment', [(s, (s + 1) % count) for s in range(count)])  5.96 us
    ppermute x2, starting transfers between devices, to_next(): lax.ppermute(value, 'segment', [(s, (s + 1) % count) for s in range(count)])  5.48 us
  transfers between devices with their start and end apart: 15, of which 4 were waited for; matrix products, arithmetic and copies ran while one was open for 5% of the time, Pallas kernels for 4%

profile of v9, /device:TPU:1, one launch (start us, length us, event | category | flops | bytes accessed | tf_op | source)
XLA Modules:
  0.0 132.5 jit_solution(6681008127484048688)
XLA Ops:
  8.4 1.3 tile.9
  9.7 5.2 %all-to-all-start = ((bf16[4,1344,128]{2,1,0:T(8,128)(2,1)}), bf16[4,1344,128]{2,1,0:T(8,128)(2,1)S(1)}, u32[]{:S(2)}, u32[]{:S(2)}) async-start(bf16[4,1344,128]{2,1,0:T(8,128)(2,1)} %tile.9), calls=%async_computation | async-start | bytes 2752512 | tf_op jit(solution)/shard_map/all_to_all | solution.py:262
  15.0 4.2 %collective-permute-start = (bf16[1024,128]{1,0:T(8,128)(2,1)S(1)}, bf16[1024,128]{1,0:T(8,128)(2,1)S(1)}, u32[]{:S(2)}, u32[]{:S(2)}) collective-permute-start(bf16[1024,128]{1,0:T(8,128)(2,1)S(1)} %bitcast.50), channel_id=1, source_target_pairs={{480,0},{482,2},{484,4},{486,6},{488,8},{490,10},{492,12},{494,14}... | collective-permute-start | bytes 786440 | tf_op jit(solution)/shard_map/ppermute | solution.py:64
  19.2 3.4 %collective-permute-start.12 = (bf16[1024,128]{1,0:T(8,128)(2,1)S(1)}, bf16[1024,128]{1,0:T(8,128)(2,1)S(1)}, u32[]{:S(2)}, u32[]{:S(2)}) collective-permute-start(bf16[1024,128]{1,0:T(8,128)(2,1)S(1)} %bitcast.51), channel_id=1, source_target_pairs={{480,8},{482,10},{484,12},{486,14},{488,16},{490,18},{492,20},{494... | collective-permute-start | bytes 786440 | tf_op jit(solution)/shard_map/ppermute | solution.py:64
  22.6 6.6 %collective-permute-start.11 = (bf16[1024,128]{1,0:T(8,128)(2,1)S(1)}, bf16[1024,128]{1,0:T(8,128)(2,1)S(1)}, u32[]{:S(2)}, u32[]{:S(2)}) collective-permute-start(bf16[1024,128]{1,0:T(8,128)(2,1)S(1)} %bitcast.52), channel_id=1, source_target_pairs={{480,16},{482,18},{484,20},{486,22},{488,24},{490,26},{492,28},{49... | collective-permute-start | bytes 786440 | tf_op jit(solution)/shard_map/ppermute | solution.py:64
  29.2 3.2 %collective-permute-start.10 = (bf16[1024,128]{1,0:T(8,128)(2,1)S(1)}, bf16[1024,128]{1,0:T(8,128)(2,1)S(1)}, u32[]{:S(2)}, u32[]{:S(2)}) collective-permute-start(bf16[1024,128]{1,0:T(8,128)(2,1)S(1)} %bitcast.53), channel_id=1, source_target_pairs={{480,24},{482,26},{484,28},{486,30},{488,0},{490,2},{492,4},{494,6... | collective-permute-start | bytes 786440 | tf_op jit(solution)/shard_map/ppermute | solution.py:64
  32.9 1.8 %multiply_reduce_fusion = f32[384]{0:T(512)S(1)} fusion(bf16[1,384,2048]{2,1,0:T(8,128)(2,1)} %param.8), kind=kLoop, calls=%fused_computation | loop fusion | flops 2358912 | bytes 1574400 | tf_op jit(solution)/shard_map/reduce_sum | solution.py:285
  34.8 2.4 %collective-permute-done.10 = bf16[1024,128]{1,0:T(8,128)(2,1)S(1)} collective-permute-done((bf16[1024,128]{1,0:T(8,128)(2,1)S(1)}, bf16[1024,128]{1,0:T(8,128)(2,1)S(1)}, u32[]{:S(2)}, u32[]{:S(2)}) %collective-permute-start.10) | collective-permute-done | bytes 262176 | tf_op jit(solution)/shard_map/ppermute | solution.py:64
  38.3 2.2 %collective-permute-start.2 = (bf16[5376,128]{1,0:T(8,128)(2,1)S(1)}, bf16[5376,128]{1,0:T(8,128)(2,1)S(1)}, u32[]{:S(2)}, u32[]{:S(2)}) collective-permute-start(bf16[5376,128]{1,0:T(8,128)(2,1)S(1)} %bitcast.41), channel_id=1, source_target_pairs={{0,2},{2,4},{4,6},{6,0},{8,10},{10,12},{12,14},{14,8},{16,18},{18,... | collective-permute-start | bytes 4128776 | tf_op jit(solution)/shard_map/ppermute | solution.py:56
  40.5 4.3 %collective-permute-start.3 = (bf16[5376,128]{1,0:T(8,128)(2,1)S(1)}, bf16[5376,128]{1,0:T(8,128)(2,1)}, u32[]{:S(2)}, u32[]{:S(2)}) collective-permute-start(bf16[5376,128]{1,0:T(8,128)(2,1)S(1)} %bitcast.42), channel_id=1, source_target_pairs={{0,6},{2,0},{4,2},{6,4},{8,14},{10,8},{12,10},{14,12},{16,22},{18,... | collective-permute-start | bytes 4128776 | tf_op jit(solution)/shard_map/ppermute | solution.py:56
  44.9 3.6 %collective-permute-start.1 = (f32[24,128]{1,0:T(8,128)S(1)}, f32[24,128]{1,0:T(8,128)S(1)}, u32[]{:S(2)}, u32[]{:S(2)}) collective-permute-start(f32[24,128]{1,0:T(8,128)S(1)} %pad_bitcast_fusion), channel_id=1, source_target_pairs={{0,32},{32,64},{64,96},{96,128},{128,160},{160,192},{192,224},{224... | collective-permute-start | bytes 36872 | tf_op jit(solution)/shard_map/ppermute | solution.py:69
  49.4 6.0 %collective-permute-done.1 = f32[24,128]{1,0:T(8,128)S(1)} collective-permute-done((f32[24,128]{1,0:T(8,128)S(1)}, f32[24,128]{1,0:T(8,128)S(1)}, u32[]{:S(2)}, u32[]{:S(2)}) %collective-permute-start.1) | collective-permute-done | bytes 12320 | tf_op jit(solution)/shard_map/ppermute | solution.py:69
  56.0 10.9 %collective-permute-start.4 = (s32[12]{0:T(128)S(1)}, s32[12]{0:T(128)S(1)}, u32[]{:S(2)}, u32[]{:S(2)}) collective-permute-start(s32[12]{0:T(128)S(1)} %get-tuple-element.44), channel_id=1, source_target_pairs={{0,32},{32,0},{64,96},{96,64},{128,160},{160,128},{192,224},{224,1... | collective-permute-start | bytes 152 | tf_op jit(solution)/shard_map/ppermute | solution.py:80
  67.8 1.9 %collective-permute-start.7 = (bf16[384,2048]{1,0:T(8,128)(2,1)}, bf16[384,2048]{1,0:T(8,128)(2,1)S(1)}, u32[]{:S(2)}, u32[]{:S(2)}) collective-permute-start(bf16[384,2048]{1,0:T(8,128)(2,1)} %bitcast.47), channel_id=1, source_target_pairs={{0,32},{32,64},{64,96},{96,128},{128,160},{160,192},{192,224},{224... | collective-permute-start | bytes 4718600 | tf_op jit(solution)/shard_map/ppermute | solution.py:69
  70.4 3.8 %collective-permute-start.5 = (bf16[2688,128]{1,0:T(8,128)(2,1)S(1)}, bf16[2688,128]{1,0:T(8,128)(2,1)S(1)}, u32[]{:S(2)}, u32[]{:S(2)}) collective-permute-start(bf16[2688,128]{1,0:T(8,128)(2,1)S(1)} %slice.34), channel_id=1, source_target_pairs={{0,2},{2,4},{4,6},{6,0},{8,10},{10,12},{12,14},{14,8},{16,18},{18,... | collective-permute-start | bytes 2064392 | tf_op jit(solution)/shard_map/ppermute | solution.py:56
  74.1 1.2 slice.35
  75.3 2.7 %collective-permute-start.6 = (bf16[2688,128]{1,0:T(8,128)(2,1)S(1)}, bf16[2688,128]{1,0:T(8,128)(2,1)S(1)}, u32[]{:S(2)}, u32[]{:S(2)}) collective-permute-start(bf16[2688,128]{1,0:T(8,128)(2,1)S(1)} %slice.35), channel_id=1, source_target_pairs={{0,6},{2,0},{4,2},{6,4},{8,14},{10,8},{12,10},{14,12},{16,22},{18,... | collective-permute-start | bytes 2064392 | tf_op jit(solution)/shard_map/ppermute | solution.py:56
  78.0 7.9 %collective-permute-start.8 = (f32[3,128]{1,0:T(4,128)S(1)}, f32[3,128]{1,0:T(4,128)S(1)}, u32[]{:S(2)}, u32[]{:S(2)}) collective-permute-start(f32[3,128]{1,0:T(4,128)S(1)} %bitcast.58), channel_id=1, source_target_pairs={{0,33},{1,32},{32,65},{33,64},{64,97},{65,96},{96,129},{97,128},{1... | collective-permute-start | bytes 4616 | tf_op jit(solution)/shard_map/ppermute | solution.py:75
  86.1 10.1 %collective-permute-done.8 = f32[3,128]{1,0:T(4,128)S(1)} collective-permute-done((f32[3,128]{1,0:T(4,128)S(1)}, f32[3,128]{1,0:T(4,128)S(1)}, u32[]{:S(2)}, u32[]{:S(2)}) %collective-permute-start.8) | collective-permute-done | bytes 1568 | tf_op jit(solution)/shard_map/ppermute | solution.py:75
  96.2 3.1 %give_encodings.1 = bf16[12,256,128]{2,1,0:T(8,128)(2,1)} custom-call(s32[3,24]{1,0:T(4,128)S(1)} %add_add_fusion.table, bf16[5376,128]{1,0:T(8,128)(2,1)S(1)} %bitcast.43, bf16[5376,128]{1,0:T(8,128)(2,1)} %collective-permute-done.3.r_ref, bf16[2688,128]{1,0:T(8,128)(2,1)S(1)} %collective-permute-done.5.ol_ref, ...), custom_call_target="tpu_custom_call" | custom-call | tf_op jit(solution)/shard_map/give_encodings/pallas_call | solution.py:128
  99.3 1.2 copy-done.4
  100.5 1.9 %collective-permute-start.9 = (bf16[12,256,128]{2,1,0:T(8,128)(2,1)}, bf16[12,256,128]{2,1,0:T(8,128)(2,1)}, u32[]{:S(2)}, u32[]{:S(2)}) collective-permute-start(bf16[12,256,128]{2,1,0:T(8,128)(2,1)} %give_encodings.1), channel_id=1, source_target_pairs={{0,32},{32,0},{64,96},{96,64},{128,160},{160,128},{192,224},{224,1... | collective-permute-start | bytes 2359304 | tf_op jit(solution)/shard_map/ppermute | solution.py:80
  102.4 2.6 %pick_encodings.1.own_ref = bf16[768,512]{1,0:T(8,128)(2,1)S(1)} custom-call(s32[3,24]{1,0:T(4,128)S(1)} %add_add_fusion.table, bf16[5376,128]{1,0:T(8,128)(2,1)S(1)} %bitcast.44, bf16[5376,128]{1,0:T(8,128)(2,1)} %collective-permute-done.3.r_ref, bf16[2688,128]{1,0:T(8,128)(2,1)S(1)} %collective-permute-done.5.ol_ref, ...), custom_call_target="tpu_custom_call" | custom-call | tf_op jit(solution)/shard_map/pick_encodings/pallas_call | solution.py:140
  106.7 18.9 %attend_heads.1 = bf16[384,2048]{1,0:T(8,128)(2,1)} custom-call(s32[12]{0:T(128)} %get-tuple-element.45.live, s32[3,24]{1,0:T(4,128)} %copy-done.3, bf16[768,512]{1,0:T(8,128)(2,1)} %copy-done.2, bf16[12,256,128]{2,1,0:T(8,128)(2,1)} %collective-permute-done.9.slabs, bf16[512,512]{1,0:T(8,128)(2,1)} %fusion.spread, bf16[16,1024,128]{2,1,0:T(8,128)(2,1)} %bitcast.45, ...), custom_call_target="tpu_custom_call" | custom-call | tf_op jit(solution)/shard_map/attend_heads/pallas_call | solution.py:210
  (64 shorter events, 8.5 us)
Async XLA Ops:
  9.7 5.2 %copy-start.5 = (bf16[1,28,2048]{2,1,0:T(8,128)(2,1)S(1)}, bf16[1,28,2048]{2,1,0:T(8,128)(2,1)}, u32[]{:S(2)}) copy-start(bf16[1,28,2048]{2,1,0:T(8,128)(2,1)} %param.11) | copy-start | bytes 344068
  9.7 5.2 %copy-start.6 = (bf16[1,28,2048]{2,1,0:T(8,128)(2,1)S(1)}, bf16[1,28,2048]{2,1,0:T(8,128)(2,1)}, u32[]{:S(2)}) copy-start(bf16[1,28,2048]{2,1,0:T(8,128)(2,1)} %param.10) | copy-start | bytes 344068
  9.7 22.8 %copy-start.10 = (s32[1,6,2]{1,2,0:T(2,128)S(1)}, s32[1,6,2]{1,2,0:T(2,128)}, u32[]{:S(2)}) copy-start(s32[1,6,2]{1,2,0:T(2,128)} %param.14) | copy-start | bytes 148
  9.7 23.0 %copy-start.8 = (s32[1,6,2]{1,2,0:T(2,128)S(1)}, s32[1,6,2]{1,2,0:T(2,128)}, u32[]{:S(2)}) copy-start(s32[1,6,2]{1,2,0:T(2,128)} %param.13) | copy-start | bytes 148
  9.7 23.0 %copy-start.9 = (s32[1,6,2]{1,2,0:T(2,128)S(1)}, s32[1,6,2]{1,2,0:T(2,128)}, u32[]{:S(2)}) copy-start(s32[1,6,2]{1,2,0:T(2,128)} %param.12) | copy-start | bytes 148
  9.7 25.1 %all-to-all-start = ((bf16[4,1344,128]{2,1,0:T(8,128)(2,1)}), bf16[4,1344,128]{2,1,0:T(8,128)(2,1)S(1)}, u32[]{:S(2)}, u32[]{:S(2)}) async-start(bf16[4,1344,128]{2,1,0:T(8,128)(2,1)} %tile.9), calls=%async_computation | async-start | bytes 2752512 | tf_op jit(solution)/shard_map/all_to_all | solution.py:262
  14.8 91.9 %all-gather.2.cloned.1.call-start = ((), (), s32[]{:S(2)}) async-start(), calls=%async_computation.1 | async-start | bytes 5242880 | tf_op jit(solution)/shard_map/all_gather | solution.py:296
  14.8 19.8 %copy-start.7 = (f32[1,2048]{1,0:T(1,128)S(1)}, f32[1,2048]{1,0:T(1,128)}, u32[]{:S(2)}) copy-start(f32[1,2048]{1,0:T(1,128)} %param.9) | copy-start | bytes 24580
  15.0 19.8 %collective-permute-start = (bf16[1024,128]{1,0:T(8,128)(2,1)S(1)}, bf16[1024,128]{1,0:T(8,128)(2,1)S(1)}, u32[]{:S(2)}, u32[]{:S(2)}) collective-permute-start(bf16[1024,128]{1,0:T(8,128)(2,1)S(1)} %bitcast.50), channel_id=1, source_target_pairs={{480,0},{482,2},{484,4},{486,6},{488,8},{490,10},{492,12},{494,14}... | collective-permute-start | bytes 786440 | tf_op jit(solution)/shard_map/ppermute | solution.py:64
  19.2 15.5 %collective-permute-start.12 = (bf16[1024,128]{1,0:T(8,128)(2,1)S(1)}, bf16[1024,128]{1,0:T(8,128)(2,1)S(1)}, u32[]{:S(2)}, u32[]{:S(2)}) collective-permute-start(bf16[1024,128]{1,0:T(8,128)(2,1)S(1)} %bitcast.51), channel_id=1, source_target_pairs={{480,8},{482,10},{484,12},{486,14},{488,16},{490,18},{492,20},{494... | collective-permute-start | bytes 786440 | tf_op jit(solution)/shard_map/ppermute | solution.py:64
  22.6 12.2 %collective-permute-start.11 = (bf16[1024,128]{1,0:T(8,128)(2,1)S(1)}, bf16[1024,128]{1,0:T(8,128)(2,1)S(1)}, u32[]{:S(2)}, u32[]{:S(2)}) collective-permute-start(bf16[1024,128]{1,0:T(8,128)(2,1)S(1)} %bitcast.52), channel_id=1, source_target_pairs={{480,16},{482,18},{484,20},{486,22},{488,24},{490,26},{492,28},{49... | collective-permute-start | bytes 786440 | tf_op jit(solution)/shard_map/ppermute | solution.py:64
  29.2 8.0 %collective-permute-start.10 = (bf16[1024,128]{1,0:T(8,128)(2,1)S(1)}, bf16[1024,128]{1,0:T(8,128)(2,1)S(1)}, u32[]{:S(2)}, u32[]{:S(2)}) collective-permute-start(bf16[1024,128]{1,0:T(8,128)(2,1)S(1)} %bitcast.53), channel_id=1, source_target_pairs={{480,24},{482,26},{484,28},{486,30},{488,0},{490,2},{492,4},{494,6... | collective-permute-start | bytes 786440 | tf_op jit(solution)/shard_map/ppermute | solution.py:64
  38.3 29.5 %collective-permute-start.2 = (bf16[5376,128]{1,0:T(8,128)(2,1)S(1)}, bf16[5376,128]{1,0:T(8,128)(2,1)S(1)}, u32[]{:S(2)}, u32[]{:S(2)}) collective-permute-start(bf16[5376,128]{1,0:T(8,128)(2,1)S(1)} %bitcast.41), channel_id=1, source_target_pairs={{0,2},{2,4},{4,6},{6,0},{8,10},{10,12},{12,14},{14,8},{16,18},{18,... | collective-permute-start | bytes 4128776 | tf_op jit(solution)/shard_map/ppermute | solution.py:56
  40.5 27.3 %collective-permute-start.3 = (bf16[5376,128]{1,0:T(8,128)(2,1)S(1)}, bf16[5376,128]{1,0:T(8,128)(2,1)}, u32[]{:S(2)}, u32[]{:S(2)}) collective-permute-start(bf16[5376,128]{1,0:T(8,128)(2,1)S(1)} %bitcast.42), channel_id=1, source_target_pairs={{0,6},{2,0},{4,2},{6,4},{8,14},{10,8},{12,10},{14,12},{16,22},{18,... | collective-permute-start | bytes 4128776 | tf_op jit(solution)/shard_map/ppermute | solution.py:56
  44.9 10.5 %collective-permute-start.1 = (f32[24,128]{1,0:T(8,128)S(1)}, f32[24,128]{1,0:T(8,128)S(1)}, u32[]{:S(2)}, u32[]{:S(2)}) collective-permute-start(f32[24,128]{1,0:T(8,128)S(1)} %pad_bitcast_fusion), channel_id=1, source_target_pairs={{0,32},{32,64},{64,96},{96,128},{128,160},{160,192},{192,224},{224... | collective-permute-start | bytes 36872 | tf_op jit(solution)/shard_map/ppermute | solution.py:69
  56.0 11.7 %collective-permute-start.4 = (s32[12]{0:T(128)S(1)}, s32[12]{0:T(128)S(1)}, u32[]{:S(2)}, u32[]{:S(2)}) collective-permute-start(s32[12]{0:T(128)S(1)} %get-tuple-element.44), channel_id=1, source_target_pairs={{0,32},{32,0},{64,96},{96,64},{128,160},{160,128},{192,224},{224,1... | collective-permute-start | bytes 152 | tf_op jit(solution)/shard_map/ppermute | solution.py:80
  67.8 31.5 %collective-permute-start.7 = (bf16[384,2048]{1,0:T(8,128)(2,1)}, bf16[384,2048]{1,0:T(8,128)(2,1)S(1)}, u32[]{:S(2)}, u32[]{:S(2)}) collective-permute-start(bf16[384,2048]{1,0:T(8,128)(2,1)} %bitcast.47), channel_id=1, source_target_pairs={{0,32},{32,64},{64,96},{96,128},{128,160},{160,192},{192,224},{224... | collective-permute-start | bytes 4718600 | tf_op jit(solution)/shard_map/ppermute | solution.py:69
  70.4 25.8 %collective-permute-start.5 = (bf16[2688,128]{1,0:T(8,128)(2,1)S(1)}, bf16[2688,128]{1,0:T(8,128)(2,1)S(1)}, u32[]{:S(2)}, u32[]{:S(2)}) collective-permute-start(bf16[2688,128]{1,0:T(8,128)(2,1)S(1)} %slice.34), channel_id=1, source_target_pairs={{0,2},{2,4},{4,6},{6,0},{8,10},{10,12},{12,14},{14,8},{16,18},{18,... | collective-permute-start | bytes 2064392 | tf_op jit(solution)/shard_map/ppermute | solution.py:56
  75.3 20.9 %collective-permute-start.6 = (bf16[2688,128]{1,0:T(8,128)(2,1)S(1)}, bf16[2688,128]{1,0:T(8,128)(2,1)S(1)}, u32[]{:S(2)}, u32[]{:S(2)}) collective-permute-start(bf16[2688,128]{1,0:T(8,128)(2,1)S(1)} %slice.35), channel_id=1, source_target_pairs={{0,6},{2,0},{4,2},{6,4},{8,14},{10,8},{12,10},{14,12},{16,22},{18,... | collective-permute-start | bytes 2064392 | tf_op jit(solution)/shard_map/ppermute | solution.py:56
  78.0 18.2 %collective-permute-start.8 = (f32[3,128]{1,0:T(4,128)S(1)}, f32[3,128]{1,0:T(4,128)S(1)}, u32[]{:S(2)}, u32[]{:S(2)}) collective-permute-start(f32[3,128]{1,0:T(4,128)S(1)} %bitcast.58), channel_id=1, source_target_pairs={{0,33},{1,32},{32,65},{33,64},{64,97},{65,96},{96,129},{97,128},{1... | collective-permute-start | bytes 4616 | tf_op jit(solution)/shard_map/ppermute | solution.py:75
  86.1 16.3 %copy-start.3 = (s32[3,24]{1,0:T(4,128)}, s32[3,24]{1,0:T(4,128)S(1)}, u32[]{:S(2)}) copy-start(s32[3,24]{1,0:T(4,128)S(1)} %add_add_fusion.table) | copy-start | bytes 868
  96.2 6.2 %copy-start.1 = (bf16[512,512]{1,0:T(8,128)(2,1)S(1)}, bf16[512,512]{1,0:T(8,128)(2,1)}, u32[]{:S(2)}) copy-start(bf16[512,512]{1,0:T(8,128)(2,1)} %fusion.spread) | copy-start | bytes 1572868
  99.3 1.2 copy-start.4
  100.5 6.3 %collective-permute-start.9 = (bf16[12,256,128]{2,1,0:T(8,128)(2,1)}, bf16[12,256,128]{2,1,0:T(8,128)(2,1)}, u32[]{:S(2)}, u32[]{:S(2)}) collective-permute-start(bf16[12,256,128]{2,1,0:T(8,128)(2,1)} %give_encodings.1), channel_id=1, source_target_pairs={{0,32},{32,0},{64,96},{96,64},{128,160},{160,128},{192,224},{224,1... | collective-permute-start | bytes 2359304 | tf_op jit(solution)/shard_map/ppermute | solution.py:80
  (2 other events, 2.0 us)
Sparse Core Ops, SparseCore 0:
  38.4 54.7 all-gather.1

commit v10 on v9

--- a/solution.py
+++ b/solution.py
@@ -308,11 +308,11 @@
     live, requests_here = ints[:REQ], ints[REQ:]
     requests_other = other_core(requests_here)
     spread = spread_of(core, place)
-    d_before, d_after, spread, requests_other, rows, squares = lax.optimization_barrier(
-        (d_before, d_after, spread, requests_other, rows, squares)
+    squares_other = to_next_other_mp(squares.reshape(-1, HD)).reshape(-1)
+    d_before, d_after, spread, requests_other, squares_other, rows = lax.optimization_barrier(
+        (d_before, d_after, spread, requests_other, squares_other, rows)
     )
     x_here = to_next(rows)
-    squares_other = to_next_other_mp(squares.reshape(-1, HD)).reshape(-1)
     mid_d = line_d.shape[0] // 2
     d_pieces = (line_d, d_after, turned(d_before[:mid_d], 1, 1), turned(d_after[mid_d:], -1, 1), d_before)
 
@@ -321,11 +321,11 @@
     )
 
     inv_rms = lax.rsqrt((squares_here + squares_other) / full_width + eps_norm)
-    given, x_here, inv_column, gain_row = lax.optimization_barrier(
-        (give(table, d_pieces), x_here, inv_rms[:, None], gain_here[None, :])
-    )
-    slabs = other_core(given)
-    own = pick(table, d_pieces, spread)
+    slabs = other_core(give(table, d_pieces))
+    own_table, x_here, inv_column, gain_row = lax.optimization_barrier(
+        (table, x_here, inv_rms[:, None], gain_here[None, :])
+    )
+    own = pick(own_table, d_pieces, spread)
     updated = attend(live, table, own, slabs, spread, all_w, x_here, inv_column, gain_row)
     return updated[None]
 

time: 135 us -> 134 us (level); the launches traced: 133 us -> 133 us
  local copies, waits for them, and re-layouts: 8.22 us -> 10.3 us
    ppermute x4, waiting for transfers between devices: 0.01 us -> 12.8 us  [turned(): return lax.ppermute(value, ('segment', 'db'), pairs)]
    ppermute x1, waiting for transfers between devices: 10.1 us -> 2.82 us  [to_next_other_mp(): return lax.ppermute(value, ('segment', 'mp'), pairs)]
    ppermute x2, waiting for transfers between devices: 5.96 us -> 0.01 us  [to_next(): lax.ppermute(value, 'segment', [(s, (s + 1) % count) for s in range(count)])]
    ppermute x2, starting transfers between devices: 12.8 us -> 8.3 us  [other_core(): return lax.ppermute(value, 'segment', [(s, s ^ 1) for s in range(count)])]
    ppermute x1, starting transfers between devices: 7.92 us -> 12.1 us  [to_next_other_mp(): return lax.ppermute(value, ('segment', 'mp'), pairs)]
    unnamed x24 -> x29, local copies, waits for them, and re-layouts: 3.23 us -> 5.28 us
  transfers between devices with their start and end apart: 15 -> 15, of which waited for: 4 -> 3; matrix products, arithmetic and copies ran while one was open for 5% -> 5% of each run, Pallas kernels for 4% -> 4%
where the time goes in v10:
time: 134 us; the launch traced here: 133 us
  starting transfers between devices  61.5 us (46%)
  Pallas kernels  24.9 us (19%)
  waiting for transfers between devices  18.1 us (14%)
  between operations  13.7 us (10%)
  local copies, waits for them, and re-layouts  10.3 us (8%)
  other arithmetic  4.79 us (4%)
    pallas_call x1, Pallas kernels, attend(): pl.pallas_call(attend_kernel, grid_spec=pltpu.PrefetchScalarGridSpec(num_...  18.9 us
    ppermute x4, starting transfers between devices, to_next_turned(): return lax.ppermute(value, ('segment', 'db'), pairs)  17.5 us
    ppermute x4, starting transfers between devices, turned(): return lax.ppermute(value, ('segment', 'db'), pairs)  13 us
    ppermute x4, waiting for transfers between devices, turned(): return lax.ppermute(value, ('segment', 'db'), pairs)  12.8 us
    ppermute x1, starting transfers between devices, to_next_other_mp(): return lax.ppermute(value, ('segment', 'mp'), pairs)  12.1 us
    ppermute x2, starting transfers between devices, other_core(): return lax.ppermute(value, 'segment', [(s, s ^ 1) for s in range(count)])  8.3 us
    ppermute x2, starting transfers between devices, to_next(): lax.ppermute(value, 'segment', [(s, (s + 1) % count) for s in range(count)])  5.49 us
    unnamed x29, local copies, waits for them, and re-layouts  5.28 us
  transfers between devices with their start and end apart: 15, of which 3 were waited for; matrix products, arithmetic and copies ran while one was open for 5% of the time, Pallas kernels for 4%

profile of v10, /device:TPU:1, one launch (start us, length us, event | category | flops | bytes accessed | tf_op | source)
XLA Modules:
  0.0 133.4 jit_solution(2960934112831013248)
XLA Ops:
  6.5 1.1 copy-done
  8.4 1.3 tile.9
  9.7 5.2 %all-to-all-start = ((bf16[4,1344,128]{2,1,0:T(8,128)(2,1)}), bf16[4,1344,128]{2,1,0:T(8,128)(2,1)S(1)}, u32[]{:S(2)}, u32[]{:S(2)}) async-start(bf16[4,1344,128]{2,1,0:T(8,128)(2,1)} %tile.9), calls=%async_computation | async-start | bytes 2752512 | tf_op jit(solution)/shard_map/all_to_all | solution.py:262
  15.0 4.2 %collective-permute-start = (bf16[1024,128]{1,0:T(8,128)(2,1)S(1)}, bf16[1024,128]{1,0:T(8,128)(2,1)S(1)}, u32[]{:S(2)}, u32[]{:S(2)}) collective-permute-start(bf16[1024,128]{1,0:T(8,128)(2,1)S(1)} %bitcast.54), channel_id=1, source_target_pairs={{480,0},{482,2},{484,4},{486,6},{488,8},{490,10},{492,12},{494,14}... | collective-permute-start | bytes 786440 | tf_op jit(solution)/shard_map/ppermute | solution.py:64
  19.2 3.4 %collective-permute-start.12 = (bf16[1024,128]{1,0:T(8,128)(2,1)S(1)}, bf16[1024,128]{1,0:T(8,128)(2,1)S(1)}, u32[]{:S(2)}, u32[]{:S(2)}) collective-permute-start(bf16[1024,128]{1,0:T(8,128)(2,1)S(1)} %bitcast.55), channel_id=1, source_target_pairs={{480,8},{482,10},{484,12},{486,14},{488,16},{490,18},{492,20},{494... | collective-permute-start | bytes 786440 | tf_op jit(solution)/shard_map/ppermute | solution.py:64
  22.6 6.6 %collective-permute-start.11 = (bf16[1024,128]{1,0:T(8,128)(2,1)S(1)}, bf16[1024,128]{1,0:T(8,128)(2,1)S(1)}, u32[]{:S(2)}, u32[]{:S(2)}) collective-permute-start(bf16[1024,128]{1,0:T(8,128)(2,1)S(1)} %bitcast.56), channel_id=1, source_target_pairs={{480,16},{482,18},{484,20},{486,22},{488,24},{490,26},{492,28},{49... | collective-permute-start | bytes 786440 | tf_op jit(solution)/shard_map/ppermute | solution.py:64
  29.2 3.2 %collective-permute-start.10 = (bf16[1024,128]{1,0:T(8,128)(2,1)S(1)}, bf16[1024,128]{1,0:T(8,128)(2,1)S(1)}, u32[]{:S(2)}, u32[]{:S(2)}) collective-permute-start(bf16[1024,128]{1,0:T(8,128)(2,1)S(1)} %bitcast.57), channel_id=1, source_target_pairs={{480,24},{482,26},{484,28},{486,30},{488,0},{490,2},{492,4},{494,6... | collective-permute-start | bytes 786440 | tf_op jit(solution)/shard_map/ppermute | solution.py:64
  32.9 1.8 %multiply_reduce_fusion = f32[384]{0:T(512)S(1)} fusion(bf16[1,384,2048]{2,1,0:T(8,128)(2,1)} %param.8), kind=kLoop, calls=%fused_computation | loop fusion | flops 2358912 | bytes 1574400 | tf_op jit(solution)/shard_map/reduce_sum | solution.py:285
  34.8 2.4 %collective-permute-done.10 = bf16[1024,128]{1,0:T(8,128)(2,1)S(1)} collective-permute-done((bf16[1024,128]{1,0:T(8,128)(2,1)S(1)}, bf16[1024,128]{1,0:T(8,128)(2,1)S(1)}, u32[]{:S(2)}, u32[]{:S(2)}) %collective-permute-start.10) | collective-permute-done | bytes 262176 | tf_op jit(solution)/shard_map/ppermute | solution.py:64
  38.3 2.2 %collective-permute-start.2 = (bf16[5376,128]{1,0:T(8,128)(2,1)S(1)}, bf16[5376,128]{1,0:T(8,128)(2,1)S(1)}, u32[]{:S(2)}, u32[]{:S(2)}) collective-permute-start(bf16[5376,128]{1,0:T(8,128)(2,1)S(1)} %bitcast.45), channel_id=1, source_target_pairs={{0,2},{2,4},{4,6},{6,0},{8,10},{10,12},{12,14},{14,8},{16,18},{18,... | collective-permute-start | bytes 4128776 | tf_op jit(solution)/shard_map/ppermute | solution.py:56
  40.5 4.3 %collective-permute-start.3 = (bf16[5376,128]{1,0:T(8,128)(2,1)S(1)}, bf16[5376,128]{1,0:T(8,128)(2,1)}, u32[]{:S(2)}, u32[]{:S(2)}) collective-permute-start(bf16[5376,128]{1,0:T(8,128)(2,1)S(1)} %bitcast.46), channel_id=1, source_target_pairs={{0,6},{2,0},{4,2},{6,4},{8,14},{10,8},{12,10},{14,12},{16,22},{18,... | collective-permute-start | bytes 4128776 | tf_op jit(solution)/shard_map/ppermute | solution.py:56
  44.9 3.6 %collective-permute-start.1 = (f32[24,128]{1,0:T(8,128)S(1)}, f32[24,128]{1,0:T(8,128)S(1)}, u32[]{:S(2)}, u32[]{:S(2)}) collective-permute-start(f32[24,128]{1,0:T(8,128)S(1)} %pad_bitcast_fusion), channel_id=1, source_target_pairs={{0,32},{32,64},{64,96},{96,128},{128,160},{160,192},{192,224},{224... | collective-permute-start | bytes 36872 | tf_op jit(solution)/shard_map/ppermute | solution.py:69
  49.4 12.1 %collective-permute-start.5 = (f32[3,128]{1,0:T(4,128)S(1)}, f32[3,128]{1,0:T(4,128)S(1)}, u32[]{:S(2)}, u32[]{:S(2)}) collective-permute-start(f32[3,128]{1,0:T(4,128)S(1)} %bitcast.62), channel_id=1, source_target_pairs={{0,33},{1,32},{32,65},{33,64},{64,97},{65,96},{96,129},{97,128},{1... | collective-permute-start | bytes 4616 | tf_op jit(solution)/shard_map/ppermute | solution.py:75
  62.2 4.8 %collective-permute-start.4 = (s32[12]{0:T(128)S(1)}, s32[12]{0:T(128)S(1)}, u32[]{:S(2)}, u32[]{:S(2)}) collective-permute-start(s32[12]{0:T(128)S(1)} %get-tuple-element.44), channel_id=1, source_target_pairs={{0,32},{32,0},{64,96},{96,64},{128,160},{160,128},{192,224},{224,1... | collective-permute-start | bytes 152 | tf_op jit(solution)/shard_map/ppermute | solution.py:80
  67.0 2.8 %collective-permute-done.5 = f32[3,128]{1,0:T(4,128)S(1)} collective-permute-done((f32[3,128]{1,0:T(4,128)S(1)}, f32[3,128]{1,0:T(4,128)S(1)}, u32[]{:S(2)}, u32[]{:S(2)}) %collective-permute-start.5) | collective-permute-done | bytes 1568 | tf_op jit(solution)/shard_map/ppermute | solution.py:75
  69.8 1.9 %collective-permute-start.6 = (bf16[384,2048]{1,0:T(8,128)(2,1)}, bf16[384,2048]{1,0:T(8,128)(2,1)}, u32[]{:S(2)}, u32[]{:S(2)}) collective-permute-start(bf16[384,2048]{1,0:T(8,128)(2,1)} %bitcast.51), channel_id=1, source_target_pairs={{0,32},{32,64},{64,96},{96,128},{128,160},{160,192},{192,224},{224... | collective-permute-start | bytes 4718600 | tf_op jit(solution)/shard_map/ppermute | solution.py:69
  71.8 3.1 %collective-permute-start.7 = (bf16[2688,128]{1,0:T(8,128)(2,1)S(1)}, bf16[2688,128]{1,0:T(8,128)(2,1)S(1)}, u32[]{:S(2)}, u32[]{:S(2)}) collective-permute-start(bf16[2688,128]{1,0:T(8,128)(2,1)S(1)} %slice.39), channel_id=1, source_target_pairs={{0,2},{2,4},{4,6},{6,0},{8,10},{10,12},{12,14},{14,8},{16,18},{18,... | collective-permute-start | bytes 2064392 | tf_op jit(solution)/shard_map/ppermute | solution.py:56
  74.9 1.2 slice.40
  76.1 3.4 %collective-permute-start.8 = (bf16[2688,128]{1,0:T(8,128)(2,1)S(1)}, bf16[2688,128]{1,0:T(8,128)(2,1)S(1)}, u32[]{:S(2)}, u32[]{:S(2)}) collective-permute-start(bf16[2688,128]{1,0:T(8,128)(2,1)S(1)} %slice.40), channel_id=1, source_target_pairs={{0,6},{2,0},{4,2},{6,4},{8,14},{10,8},{12,10},{14,12},{16,22},{18,... | collective-permute-start | bytes 2064392 | tf_op jit(solution)/shard_map/ppermute | solution.py:56
  79.7 12.8 %collective-permute-done.7.ol_ref = bf16[2688,128]{1,0:T(8,128)(2,1)S(1)} collective-permute-done((bf16[2688,128]{1,0:T(8,128)(2,1)S(1)}, bf16[2688,128]{1,0:T(8,128)(2,1)S(1)}, u32[]{:S(2)}, u32[]{:S(2)}) %collective-permute-start.7) | collective-permute-done | bytes 688160 | tf_op jit(solution)/shard_map/ppermute | solution.py:56
  92.5 3.1 %give_encodings.1 = bf16[12,256,128]{2,1,0:T(8,128)(2,1)} custom-call(s32[3,24]{1,0:T(4,128)S(1)} %add_add_fusion.table, bf16[5376,128]{1,0:T(8,128)(2,1)S(1)} %bitcast.47, bf16[5376,128]{1,0:T(8,128)(2,1)} %collective-permute-done.3.r_ref, bf16[2688,128]{1,0:T(8,128)(2,1)S(1)} %collective-permute-done.7.ol_ref, ...), custom_call_target="tpu_custom_call" | custom-call | tf_op jit(solution)/shard_map/give_encodings/pallas_call | solution.py:128
  95.6 3.5 %collective-permute-start.9 = (bf16[12,256,128]{2,1,0:T(8,128)(2,1)}, bf16[12,256,128]{2,1,0:T(8,128)(2,1)}, u32[]{:S(2)}, u32[]{:S(2)}) collective-permute-start(bf16[12,256,128]{2,1,0:T(8,128)(2,1)} %give_encodings.1), channel_id=1, source_target_pairs={{0,32},{32,0},{64,96},{96,64},{128,160},{160,128},{192,224},{224,1... | collective-permute-start | bytes 2359304 | tf_op jit(solution)/shard_map/ppermute | solution.py:80
  103.8 2.9 %pick_encodings.1.own_ref = bf16[768,512]{1,0:T(8,128)(2,1)S(1)} custom-call(s32[3,24]{1,0:T(4,128)S(1)} %add_add_fusion.table, bf16[5376,128]{1,0:T(8,128)(2,1)S(1)} %bitcast.48, bf16[5376,128]{1,0:T(8,128)(2,1)} %collective-permute-done.3.r_ref, bf16[2688,128]{1,0:T(8,128)(2,1)S(1)} %copy-done.4, bf16[2688,128]{1,0:T(8,128)(2,1)S(1)} %copy-done.6, ...), custom_call_target="tpu_custom_call" | custom-call | tf_op jit(solution)/shard_map/pick_encodings/pallas_call | solution.py:140
  107.6 18.9 %attend_heads.1 = bf16[384,2048]{1,0:T(8,128)(2,1)} custom-call(s32[12]{0:T(128)} %get-tuple-element.45.live, s32[3,24]{1,0:T(4,128)} %copy-done.7, bf16[768,512]{1,0:T(8,128)(2,1)} %copy-done.2, bf16[12,256,128]{2,1,0:T(8,128)(2,1)} %collective-permute-done.9.slabs, bf16[512,512]{1,0:T(8,128)(2,1)} %fusion.spread, bf16[16,1024,128]{2,1,0:T(8,128)(2,1)} %bitcast.49, ...), custom_call_target="tpu_custom_call" | custom-call | tf_op jit(solution)/shard_map/attend_heads/pallas_call | solution.py:210
  (70 shorter events, 9.8 us)
Async XLA Ops:
  9.7 5.2 %copy-start.8 = (bf16[1,28,2048]{2,1,0:T(8,128)(2,1)S(1)}, bf16[1,28,2048]{2,1,0:T(8,128)(2,1)}, u32[]{:S(2)}) copy-start(bf16[1,28,2048]{2,1,0:T(8,128)(2,1)} %param.11) | copy-start | bytes 344068
  9.7 5.2 %copy-start.9 = (bf16[1,28,2048]{2,1,0:T(8,128)(2,1)S(1)}, bf16[1,28,2048]{2,1,0:T(8,128)(2,1)}, u32[]{:S(2)}) copy-start(bf16[1,28,2048]{2,1,0:T(8,128)(2,1)} %param.10) | copy-start | bytes 344068
  9.7 22.8 %copy-start.13 = (s32[1,6,2]{1,2,0:T(2,128)S(1)}, s32[1,6,2]{1,2,0:T(2,128)}, u32[]{:S(2)}) copy-start(s32[1,6,2]{1,2,0:T(2,128)} %param.14) | copy-start | bytes 148
  9.7 23.0 %copy-start.11 = (s32[1,6,2]{1,2,0:T(2,128)S(1)}, s32[1,6,2]{1,2,0:T(2,128)}, u32[]{:S(2)}) copy-start(s32[1,6,2]{1,2,0:T(2,128)} %param.13) | copy-start | bytes 148
  9.7 23.0 %copy-start.12 = (s32[1,6,2]{1,2,0:T(2,128)S(1)}, s32[1,6,2]{1,2,0:T(2,128)}, u32[]{:S(2)}) copy-start(s32[1,6,2]{1,2,0:T(2,128)} %param.12) | copy-start | bytes 148
  9.7 25.1 %all-to-all-start = ((bf16[4,1344,128]{2,1,0:T(8,128)(2,1)}), bf16[4,1344,128]{2,1,0:T(8,128)(2,1)S(1)}, u32[]{:S(2)}, u32[]{:S(2)}) async-start(bf16[4,1344,128]{2,1,0:T(8,128)(2,1)} %tile.9), calls=%async_computation | async-start | bytes 2752512 | tf_op jit(solution)/shard_map/all_to_all | solution.py:262
  14.8 92.8 %all-gather.2.cloned.1.call-start = ((), (), s32[]{:S(2)}) async-start(), calls=%async_computation.1 | async-start | bytes 5242880 | tf_op jit(solution)/shard_map/all_gather | solution.py:296
  14.8 19.8 %copy-start.10 = (f32[1,2048]{1,0:T(1,128)S(1)}, f32[1,2048]{1,0:T(1,128)}, u32[]{:S(2)}) copy-start(f32[1,2048]{1,0:T(1,128)} %param.9) | copy-start | bytes 24580
  15.0 19.8 %collective-permute-start = (bf16[1024,128]{1,0:T(8,128)(2,1)S(1)}, bf16[1024,128]{1,0:T(8,128)(2,1)S(1)}, u32[]{:S(2)}, u32[]{:S(2)}) collective-permute-start(bf16[1024,128]{1,0:T(8,128)(2,1)S(1)} %bitcast.54), channel_id=1, source_target_pairs={{480,0},{482,2},{484,4},{486,6},{488,8},{490,10},{492,12},{494,14}... | collective-permute-start | bytes 786440 | tf_op jit(solution)/shard_map/ppermute | solution.py:64
  19.2 15.5 %collective-permute-start.12 = (bf16[1024,128]{1,0:T(8,128)(2,1)S(1)}, bf16[1024,128]{1,0:T(8,128)(2,1)S(1)}, u32[]{:S(2)}, u32[]{:S(2)}) collective-permute-start(bf16[1024,128]{1,0:T(8,128)(2,1)S(1)} %bitcast.55), channel_id=1, source_target_pairs={{480,8},{482,10},{484,12},{486,14},{488,16},{490,18},{492,20},{494... | collective-permute-start | bytes 786440 | tf_op jit(solution)/shard_map/ppermute | solution.py:64
  22.6 12.2 %collective-permute-start.11 = (bf16[1024,128]{1,0:T(8,128)(2,1)S(1)}, bf16[1024,128]{1,0:T(8,128)(2,1)S(1)}, u32[]{:S(2)}, u32[]{:S(2)}) collective-permute-start(bf16[1024,128]{1,0:T(8,128)(2,1)S(1)} %bitcast.56), channel_id=1, source_target_pairs={{480,16},{482,18},{484,20},{486,22},{488,24},{490,26},{492,28},{49... | collective-permute-start | bytes 786440 | tf_op jit(solution)/shard_map/ppermute | solution.py:64
  29.2 8.0 %collective-permute-start.10 = (bf16[1024,128]{1,0:T(8,128)(2,1)S(1)}, bf16[1024,128]{1,0:T(8,128)(2,1)S(1)}, u32[]{:S(2)}, u32[]{:S(2)}) collective-permute-start(bf16[1024,128]{1,0:T(8,128)(2,1)S(1)} %bitcast.57), channel_id=1, source_target_pairs={{480,24},{482,26},{484,28},{486,30},{488,0},{490,2},{492,4},{494,6... | collective-permute-start | bytes 786440 | tf_op jit(solution)/shard_map/ppermute | solution.py:64
  38.3 31.5 %collective-permute-start.2 = (bf16[5376,128]{1,0:T(8,128)(2,1)S(1)}, bf16[5376,128]{1,0:T(8,128)(2,1)S(1)}, u32[]{:S(2)}, u32[]{:S(2)}) collective-permute-start(bf16[5376,128]{1,0:T(8,128)(2,1)S(1)} %bitcast.45), channel_id=1, source_target_pairs={{0,2},{2,4},{4,6},{6,0},{8,10},{10,12},{12,14},{14,8},{16,18},{18,... | collective-permute-start | bytes 4128776 | tf_op jit(solution)/shard_map/ppermute | solution.py:56
  40.5 29.3 %collective-permute-start.3 = (bf16[5376,128]{1,0:T(8,128)(2,1)S(1)}, bf16[5376,128]{1,0:T(8,128)(2,1)}, u32[]{:S(2)}, u32[]{:S(2)}) collective-permute-start(bf16[5376,128]{1,0:T(8,128)(2,1)S(1)} %bitcast.46), channel_id=1, source_target_pairs={{0,6},{2,0},{4,2},{6,4},{8,14},{10,8},{12,10},{14,12},{16,22},{18,... | collective-permute-start | bytes 4128776 | tf_op jit(solution)/shard_map/ppermute | solution.py:56
  44.9 16.6 %collective-permute-start.1 = (f32[24,128]{1,0:T(8,128)S(1)}, f32[24,128]{1,0:T(8,128)S(1)}, u32[]{:S(2)}, u32[]{:S(2)}) collective-permute-start(f32[24,128]{1,0:T(8,128)S(1)} %pad_bitcast_fusion), channel_id=1, source_target_pairs={{0,32},{32,64},{64,96},{96,128},{128,160},{160,192},{192,224},{224... | collective-permute-start | bytes 36872 | tf_op jit(solution)/shard_map/ppermute | solution.py:69
  49.4 20.4 %collective-permute-start.5 = (f32[3,128]{1,0:T(4,128)S(1)}, f32[3,128]{1,0:T(4,128)S(1)}, u32[]{:S(2)}, u32[]{:S(2)}) collective-permute-start(f32[3,128]{1,0:T(4,128)S(1)} %bitcast.62), channel_id=1, source_target_pairs={{0,33},{1,32},{32,65},{33,64},{64,97},{65,96},{96,129},{97,128},{1... | collective-permute-start | bytes 4616 | tf_op jit(solution)/shard_map/ppermute | solution.py:75
  62.2 7.6 %collective-permute-start.4 = (s32[12]{0:T(128)S(1)}, s32[12]{0:T(128)S(1)}, u32[]{:S(2)}, u32[]{:S(2)}) collective-permute-start(s32[12]{0:T(128)S(1)} %get-tuple-element.44), channel_id=1, source_target_pairs={{0,32},{32,0},{64,96},{96,64},{128,160},{160,128},{192,224},{224,1... | collective-permute-start | bytes 152 | tf_op jit(solution)/shard_map/ppermute | solution.py:80
  69.8 29.9 %collective-permute-start.6 = (bf16[384,2048]{1,0:T(8,128)(2,1)}, bf16[384,2048]{1,0:T(8,128)(2,1)}, u32[]{:S(2)}, u32[]{:S(2)}) collective-permute-start(bf16[384,2048]{1,0:T(8,128)(2,1)} %bitcast.51), channel_id=1, source_target_pairs={{0,32},{32,64},{64,96},{96,128},{128,160},{160,192},{192,224},{224... | collective-permute-start | bytes 4718600 | tf_op jit(solution)/shard_map/ppermute | solution.py:69
  71.8 20.7 %collective-permute-start.7 = (bf16[2688,128]{1,0:T(8,128)(2,1)S(1)}, bf16[2688,128]{1,0:T(8,128)(2,1)S(1)}, u32[]{:S(2)}, u32[]{:S(2)}) collective-permute-start(bf16[2688,128]{1,0:T(8,128)(2,1)S(1)} %slice.39), channel_id=1, source_target_pairs={{0,2},{2,4},{4,6},{6,0},{8,10},{10,12},{12,14},{14,8},{16,18},{18,... | collective-permute-start | bytes 2064392 | tf_op jit(solution)/shard_map/ppermute | solution.py:56
  76.1 16.4 %collective-permute-start.8 = (bf16[2688,128]{1,0:T(8,128)(2,1)S(1)}, bf16[2688,128]{1,0:T(8,128)(2,1)S(1)}, u32[]{:S(2)}, u32[]{:S(2)}) collective-permute-start(bf16[2688,128]{1,0:T(8,128)(2,1)S(1)} %slice.40), channel_id=1, source_target_pairs={{0,6},{2,0},{4,2},{6,4},{8,14},{10,8},{12,10},{14,12},{16,22},{18,... | collective-permute-start | bytes 2064392 | tf_op jit(solution)/shard_map/ppermute | solution.py:56
  79.7 20.9 %copy-start.7 = (s32[3,24]{1,0:T(4,128)}, s32[3,24]{1,0:T(4,128)S(1)}, u32[]{:S(2)}) copy-start(s32[3,24]{1,0:T(4,128)S(1)} %add_add_fusion.table) | copy-start | bytes 868
  92.5 3.1 %copy-start.3 = (bf16[2688,128]{1,0:T(8,128)(2,1)}, bf16[2688,128]{1,0:T(8,128)(2,1)S(1)}, u32[]{:S(2)}) copy-start(bf16[2688,128]{1,0:T(8,128)(2,1)S(1)} %collective-permute-done.7.ol_ref) | copy-start | bytes 2064388
  92.5 3.1 %copy-start.5 = (bf16[2688,128]{1,0:T(8,128)(2,1)}, bf16[2688,128]{1,0:T(8,128)(2,1)S(1)}, u32[]{:S(2)}) copy-start(bf16[2688,128]{1,0:T(8,128)(2,1)S(1)} %collective-permute-done.8.or_ref) | copy-start | bytes 2064388
  95.6 12.0 %collective-permute-start.9 = (bf16[12,256,128]{2,1,0:T(8,128)(2,1)}, bf16[12,256,128]{2,1,0:T(8,128)(2,1)}, u32[]{:S(2)}, u32[]{:S(2)}) collective-permute-start(bf16[12,256,128]{2,1,0:T(8,128)(2,1)} %give_encodings.1), channel_id=1, source_target_pairs={{0,32},{32,0},{64,96},{96,64},{128,160},{160,128},{192,224},{224,1... | collective-permute-start | bytes 2359304 | tf_op jit(solution)/shard_map/ppermute | solution.py:80
  (5 other events, 5.2 us)
Sparse Core Ops, SparseCore 0:
  38.4 54.7 all-gather.1
